TPU v7x, 128 devices: a whole 4x4x4 slice. The times are simulated.
128 devices in a mesh: seq: 8 (over z_hi, y), fsdp: 16 (over x, z_lo, core).
Axes of the slice: x: 4, y: 4, z: 4 (z_hi: 2, z_lo: 2; z = z_hi * 2 + z_lo), core: 2. Of those that a mesh axis runs over, the one named last changes fastest.
Arguments:
- hidden_in: bfloat16 [16, 1024, 2048], P('fsdp', 'seq'), may hold values from -6 to 6
- cotangent: bfloat16 [16, 1024, 2048], P('fsdp', 'seq'), may hold values from -6 to 6
- seq_lengths: int32 [16, 2], P('fsdp'), may hold values from 65 to 896, as said below
- slot_block: int32 [16, 8], P('fsdp'), may hold values from 0 to 7, as said below
- ln1_gain: bfloat16 [2048], P(('seq', 'fsdp')), may hold values from 0.25 to 1.75
- ln1_bias: bfloat16 [2048], P(('seq', 'fsdp')), may hold values from -1.1953125 to 1.1953125
- w_qkv: bfloat16 [2048, 6144], P(('seq', 'fsdp')), may hold values from -0.125 to 0.125
- qkv_bias: bfloat16 [6144], P(('seq', 'fsdp')), may hold values from -1.1953125 to 1.1953125
- w_out: bfloat16 [2048, 2048], P(('seq', 'fsdp')), may hold values from -0.5 to 0.5
- ln2_gain: bfloat16 [2048], P(('seq', 'fsdp')), may hold values from 0.25 to 1.75
- ln2_bias: bfloat16 [2048], P(('seq', 'fsdp')), may hold values from -1.1953125 to 1.1953125
- w_gate: bfloat16 [2048, 5632], P(('seq', 'fsdp')), may hold values from -0.125 to 0.125
- w_up: bfloat16 [2048, 5632], P(('seq', 'fsdp')), may hold values from -0.125 to 0.125
- w_down: bfloat16 [2048, 5632], P(('seq', 'fsdp')), may hold values from -0.078125 to 0.078125
Outputs:
- hidden_out: bfloat16 [16, 1024, 2048], P('fsdp', 'seq')
- input_grad: float32 [16, 1024, 2048], P('fsdp', 'seq')
- ln1_gain_grad: float32 [2048], P(('seq', 'fsdp'))
- ln1_bias_grad: float32 [2048], P(('seq', 'fsdp'))
- w_qkv_grad: float32 [2048, 6144], P(('seq', 'fsdp'))
- qkv_bias_grad: float32 [6144], P(('seq', 'fsdp'))
- w_out_grad: float32 [2048, 2048], P(('seq', 'fsdp'))
- ln2_gain_grad: float32 [2048], P(('seq', 'fsdp'))
- ln2_bias_grad: float32 [2048], P(('seq', 'fsdp'))
- w_gate_grad: float32 [2048, 5632], P(('seq', 'fsdp'))
- w_up_grad: float32 [2048, 5632], P(('seq', 'fsdp'))
- w_down_grad: float32 [2048, 5632], P(('seq', 'fsdp'))
Inputs may be any that keep to these rules, and one draw needn't show every extreme that they name: `seq_lengths`: each group holds two sequences, in this order, each padded to whole 128-token blocks; together their blocks fill the group's 8 blocks, and each has less than half a block of padding. `slot_block`: each row is an order of the group's block numbers; slot s lies on seq device s.
All inputs are finite; a program needn't handle non-finite values.
Results may differ from a plain program's by a relative error of at most 0.018.
Values may be sent and summed in bfloat16 or wider, within the bound.
A program may use at most 704 MiB of HBM per device.

v0:
```python
import functools

import jax
import jax.numpy as jnp
from jax import lax
from jax.experimental import pallas as pl
from jax.experimental.pallas import tpu as pltpu
from jax.sharding import Mesh
from jax.sharding import PartitionSpec as P

D = 2048
HEADS = 32
HEAD_DIM = 64
ROT = 16
FF = 5632
BLOCK = 128
TP = 8
HD = D // TP
FC = FF // TP

EPS = 1e-05
NEG = -1e30
SCALE = HEAD_DIM ** (-0.5)
TPA = ("y", "core")
XZ = ("x", "zh", "zl")
ROWS = ("zh", "y", "x", "zl", "core")
GRP = ("x", "zl", "core")
SLOT = ("zh", "y")


def permute_features(v):
    lead = v.shape[:-1]
    n = len(lead)
    v = v.reshape(lead + (2, 4, 4, 2, 32))
    v = v.transpose(tuple(range(n)) + (n + 2, n, n + 3, n + 1, n + 4))
    return v.reshape(lead + (D,))


def restore_features(v):
    lead = v.shape[:-1]
    n = len(lead)
    v = v.reshape(lead + (4, 2, 2, 4, 32))
    v = v.transpose(tuple(range(n)) + (n + 1, n + 3, n, n + 2, n + 4))
    return v.reshape(lead + (D,))


def block_places(lengths, blocks):
    first_pad = (lengths[0] + BLOCK - 1) // BLOCK * BLOCK
    offsets = jnp.arange(BLOCK, dtype=jnp.int32)
    placed = (blocks[:, None] * BLOCK + offsets[None, :]).reshape(-1)
    second = (placed >= first_pad).astype(jnp.int32)
    position = placed - second * first_pad
    limit = jnp.where(second == 1, lengths[1], lengths[0])
    return second, position, position < limit


def layer_norm(values):
    average = jnp.mean(values, axis=-1, keepdims=True)
    centred = values - average
    inv_scale = lax.rsqrt(jnp.mean(centred * centred, axis=-1, keepdims=True) + EPS)
    return centred * inv_scale, inv_scale


def norm_back(grad_in, normed, inv_scale, gain):
    scaled = grad_in * gain
    return inv_scale * (
        scaled
        - jnp.mean(scaled, axis=-1, keepdims=True)
        - normed * jnp.mean(scaled * normed, axis=-1, keepdims=True)
    )


FP = 768
HALF = BLOCK // 2
ANY = pl.BlockSpec(memory_space=pl.ANY)
VM = pl.BlockSpec(memory_space=pltpu.VMEM)
BF = jnp.bfloat16
F32 = jnp.float32


def params(cid):
    return pltpu.CompilerParams(
        collective_id=cid, has_side_effects=True, vmem_limit_bytes=56 * 1024 * 1024
    )


def meet(peers):
    barrier = pltpu.get_barrier_semaphore()
    for peer in peers:
        pl.semaphore_signal(
            barrier, inc=1, device_id=peer, device_id_type=pl.DeviceIdType.MESH
        )
    pl.semaphore_wait(barrier, len(peers))


def remote(sems, i, src, dst, peer):
    return pltpu.make_async_remote_copy(
        src_ref=src,
        dst_ref=dst,
        send_sem=sems[0].at[i],
        recv_sem=sems[1].at[i],
        device_id=peer,
        device_id_type=pl.DeviceIdType.MESH,
    )


def ring():
    y = lax.axis_index("y")
    c = lax.axis_index("core")
    up = lax.rem(y + 1, 4)
    opp = lax.rem(y + 2, 4)
    dn = lax.rem(y + 3, 4)
    return y, c, up, opp, dn


def ring_peers(up, dn, c):
    return {"y": up}, {"y": dn}, {"core": 1 - c}


N_AG = 11
N_RS = 10


class RingGather:
    def __init__(self, own, full, local_sem, sems):
        y, c, up, opp, dn = ring()
        to_up, to_dn, to_sib = ring_peers(up, dn, c)
        first, last = pl.ds(0, HALF), pl.ds(HALF, HALF)
        cp = functools.partial(remote, sems)

        def pass_on(i, block, peer, *rows):
            ref = full.at[(block, c) + rows]
            return cp(i, ref, ref, peer)

        self.up1 = cp(0, own.at[first], full.at[y, c, first], to_up)
        self.dn1 = cp(1, own.at[last], full.at[y, c, last], to_dn)
        self.up2 = cp(2, own.at[last], full.at[y, c, last], to_up)
        self.dn2 = cp(3, own.at[first], full.at[y, c, first], to_dn)
        self.here = pltpu.make_async_copy(own, full.at[y, c], local_sem)
        self.far1 = pass_on(5, dn, to_up, first)
        self.far2 = pass_on(6, up, to_dn, last)
        self.sib = [
            cp(4, own, full.at[y, c], to_sib),
            pass_on(7, dn, to_sib),
            pass_on(8, up, to_sib),
            pass_on(9, opp, to_sib, first),
            pass_on(10, opp, to_sib, last),
        ]

    def start(self):
        for one in (self.up1, self.dn1, self.up2, self.dn2, self.sib[0], self.here):
            one.start()

    def forward(self):
        self.up1.wait_recv()
        self.far1.start()
        self.dn1.wait_recv()
        self.far2.start()

    def share(self):
        self.up2.wait_recv()
        self.sib[1].start()
        self.dn2.wait_recv()
        self.sib[2].start()

    def share_far(self):
        self.far1.wait_recv()
        self.sib[3].start()
        self.far2.wait_recv()
        self.sib[4].start()

    def finish(self):
        for one in self.sib:
            one.wait_recv()
        self.here.wait()
        for one in [self.up1, self.dn1, self.up2, self.dn2, self.far1, self.far2] + self.sib:
            one.wait_send()

    def run(self, work=None):
        for step in (self.start, self.forward, self.share, self.share_far):
            step()
            if work is not None:
                work()
        self.finish()


def rows_loop(count, step, body):
    @pl.loop(0, count // step)
    def _(i):
        body(pl.ds(pl.multiple_of(i * step, step), step))


RS_SCRATCH = [
    pltpu.VMEM((4, BLOCK, D), F32),
    pltpu.VMEM((4, BLOCK, D), BF),
    pltpu.VMEM((4, BLOCK, D), BF),
    pltpu.VMEM((2, HALF, D), BF),
    pltpu.VMEM((2, HALF, D), BF),
    pltpu.VMEM((2, BLOCK, D), BF),
    pltpu.VMEM((2, BLOCK, D), BF),
    pltpu.SemaphoreType.DMA((N_RS,)),
    pltpu.SemaphoreType.DMA((N_RS,)),
]


class RingScatter:
    def __init__(self, mine, sib_out, sib_in, far_out, far_in, near_out, near_in, *sems):
        y, c, up, opp, dn = ring()
        to_up, to_dn, to_sib = ring_peers(up, dn, c)
        first, last = pl.ds(0, HALF), pl.ds(HALF, HALF)
        cp = functools.partial(remote, sems)
        self.order = (opp, up, dn, y)
        self.mine, self.sib_in = mine, sib_in
        self.far_out, self.far_in = far_out, far_in
        self.near_out, self.near_in = near_out, near_in
        self.sib = [cp(j, sib_out(j), sib_in.at[j], to_sib) for j in range(4)]
        self.far = [
            cp(4, far_out.at[0], far_in.at[0], to_up),
            cp(5, far_out.at[1], far_in.at[1], to_dn),
        ]
        self.early = [
            cp(6, near_out.at[0, last], near_in.at[0, last], to_up),
            cp(7, near_out.at[1, first], near_in.at[1, first], to_dn),
        ]
        self.late = [
            cp(8, near_out.at[0, first], near_in.at[0, first], to_up),
            cp(9, near_out.at[1, last], near_in.at[1, last], to_dn),
        ]

    def both(self, j, rows):
        return self.mine(j, rows) + self.sib_in[j, rows, :].astype(F32)

    def send_far(self):
        self.sib[0].wait_recv()
        for k in range(2):

            def add(r, k=k):
                q = pl.ds(k * HALF + r.start, r.size)
                self.far_out[k, r, :] = self.both(0, q).astype(BF)

            rows_loop(HALF, 32, add)
            self.far[k].start()

    def send_early(self, k):
        self.sib[1 + k].wait_recv()

        def add(r):
            q = pl.ds((1 - k) * HALF + r.start, r.size)
            self.near_out[k, q, :] = self.both(1 + k, q).astype(BF)

        rows_loop(HALF, 32, add)
        self.early[k].start()

    def send_late(self):
        for k in range(2):
            self.far[k].wait_recv()

            def add(r, k=k):
                q = pl.ds(k * HALF + r.start, r.size)
                self.near_out[k, q, :] = (
                    self.both(1 + k, q) + self.far_in[k, r, :].astype(F32)
                ).astype(BF)

            rows_loop(HALF, 32, add)
            self.late[k].start()

    def wait(self):
        self.sib[3].wait_recv()
        for one in self.early + self.late:
            one.wait_recv()

    def total(self, rows):
        return (
            self.both(3, rows)
            + self.near_in[0, rows, :].astype(F32)
            + self.near_in[1, rows, :].astype(F32)
        )

    def finish(self):
        for one in self.sib + self.far + self.early + self.late:
            one.wait_send()


def ring_scatter(partial, scratch, between=None):
    part, sib_out = scratch[:2]
    c = lax.axis_index("core")
    scatter = RingScatter(
        lambda j, rows: part[j, rows, :], lambda j: sib_out.at[j], *scratch[2:]
    )

    def produce(j):
        def put(columns, value):
            part[j, :, columns] = jnp.where(c == 0, value[0], value[1])
            sib_out[j, :, columns] = jnp.where(c == 0, value[1], value[0]).astype(BF)

        partial(scatter.order[j], put)
        scatter.sib[j].start()

    produce(0)
    produce(1)
    scatter.send_far()
    scatter.send_early(0)
    produce(2)
    scatter.send_early(1)
    scatter.send_late()
    produce(3)
    if between is not None:
        between()
    scatter.wait()
    return scatter


AG_SCRATCH = [
    pltpu.VMEM((BLOCK, D), BF),
    pltpu.SemaphoreType.DMA,
    pltpu.SemaphoreType.DMA((N_AG,)),
    pltpu.SemaphoreType.DMA((N_AG,)),
]
FULL = jax.ShapeDtypeStruct((4, 2, BLOCK, D), BF)


def order_out(gathered, weight):
    for x in range(4):
        for zl in range(2):
            for a in range(2):
                row = x * 64 + zl * 32 + a * 16
                weight[row : row + 16, :] = gathered[x, a * 2 + zl]


OUT_ROWS = pltpu.VMEM((HD, D), BF)


def kernel_out_proj(attended, gathered, hidden, gains, middle, full, weight, *scratch):
    own, local_sem, *sems = scratch[:4]
    y, c, up, opp, dn = ring()
    meet(ring_peers(up, dn, c))
    order_out(gathered, weight)

    def partial(block, put):
        a = attended[block].reshape(2 * BLOCK, HD)

        @pl.loop(0, 4)
        def _(i):
            q = pl.ds(pl.multiple_of(i * 512, 512), 512)
            put(q, jnp.dot(a, weight[:, q], preferred_element_type=F32).reshape(2, BLOCK, 512))

    scatter = ring_scatter(partial, scratch[4:])

    def norm(r):
        row = hidden[r, :].astype(F32) + scatter.total(r)
        middle[r, :] = row
        normed, _ = layer_norm(row)
        own[r, :] = (normed * gains[2:3, :] + gains[3:4, :]).astype(BF)

    rows_loop(BLOCK, 16, norm)
    RingGather(own, full, local_sem, sems).run()
    scatter.finish()


def out_proj(attended, weight, hidden, gains, cid):
    return pl.pallas_call(
        kernel_out_proj,
        out_shape=(jax.ShapeDtypeStruct((BLOCK, D), F32), FULL),
        in_specs=[VM] * 4,
        out_specs=(VM, ANY),
        scratch_shapes=[OUT_ROWS] + AG_SCRATCH + RS_SCRATCH,
        compiler_params=params(cid),
        name="out_proj",
    )(attended, weight, hidden, gains)


NN = (((1,), (0,)), ((), ()))
NT = (((1,), (1,)), ((), ()))
TN = (((0,), (0,)), ((), ()))
TOKENS = 4 * BLOCK
KEYS = 2 * TOKENS
TILE = 2 * BLOCK


def dot(a, b, dims):
    return lax.dot_general(a, b, dims, preferred_element_type=F32)


def lane(n):
    return lax.broadcasted_iota(jnp.int32, (1, n), 1)


def turn_tables(base):
    entry = lax.rem(lane(BLOCK), HEAD_DIM)
    freq = jnp.exp(
        lax.rem(entry, ROT // 2).astype(F32) * (-2.0 / ROT * 9.210340371976184)
    )
    freq = jnp.where(entry < ROT, freq, 0.0)
    place = (base + lax.broadcasted_iota(jnp.int32, (BLOCK, 1), 0)).astype(F32)
    phase = place * freq
    return jnp.cos(phase), jnp.sin(phase)


def turn(v, cosine, sines, direction):
    entry = lax.rem(lane(BLOCK), HEAD_DIM)
    s = sines * direction
    ahead = pltpu.roll(v, BLOCK - ROT // 2, 1)
    behind = pltpu.roll(v, ROT // 2, 1)
    return v * cosine + jnp.where(entry < ROT // 2, -ahead, behind) * s


def key_bias(table, g, tile):
    token = lane(BLOCK)
    q_code, q_low = [], []
    for j in range(2):
        low = table[g, 1, 2 * tile + j] * 4096
        q_code.append(low + table[g, 0, 2 * tile + j] + token)
        q_low.append(low + jnp.zeros_like(token))
    q_code = jnp.concatenate(q_code, axis=1)
    q_low = jnp.concatenate(q_low, axis=1)
    column = lax.broadcasted_iota(jnp.int32, (BLOCK, 1), 0)
    rows = []
    for k in range(8):
        place = table[g, 0, k] + column
        code = jnp.where(place < table[g, 2, k], table[g, 1, k] * 4096 + place, 1 << 20)
        kept = jnp.logical_and(code <= q_code, code >= q_low)
        rows.append(jnp.where(kept, 0.0, NEG))
    return jnp.concatenate(rows, axis=0)


def head_mask(h):
    first = lane(BLOCK) < HEAD_DIM
    return jnp.where(first if h == 0 else jnp.logical_not(first), 1.0, 0.0).astype(BF)


def kernel_attend(
    table,
    tokens,
    weight,
    shift,
    grad_out,
    out_rows,
    queries,
    kv,
    lse,
    attended,
    grad_all,
    out_full,
    cosines,
    sines,
    send,
    recv,
    *more_sems,
):
    partner = {"zh": 1 - lax.axis_index("zh")}
    y0, c, up, opp, dn = ring()
    meet(list(ring_peers(up, dn, c)) + plane_peers())
    sems = (send, recv)
    gather = RingGather(grad_out, grad_all, more_sems[0], more_sems[1:3])
    gather.start()
    plane = PlaneGather(out_rows, out_full, *more_sems[3:])
    plane.start()

    @pl.loop(0, 4)
    def _(y):
        at = pl.ds(pl.multiple_of(y * BLOCK, BLOCK), BLOCK)
        for g in range(2):
            cosine, sine = turn_tables(table[g, 0, y])
            cosines[g, at, :] = cosine
            sines[g, at, :] = sine
        a = tokens[y].reshape(TILE, D)
        new = dot(a, weight[:, HD:], NN) + shift[:, HD:]
        for g in range(2):
            rows = slice(g * BLOCK, (g + 1) * BLOCK)
            for pair in range(2):
                q = slice(pair * BLOCK, (pair + 1) * BLOCK)
                turned = turn(new[rows, q], cosines[g, at, :], sines[g, at, :], 1.0)
                kv[0, g, at, q] = turned.astype(BF)
            kv[1, g, at, :] = new[rows, HD:].astype(BF)

    own, other = pl.ds(0, TOKENS), pl.ds(TOKENS, TOKENS)
    trade = [
        remote(sems, g, kv.at[:, g, own, :], kv.at[:, g, other, :], partner) for g in range(2)
    ]
    for one in trade:
        one.start()
    gather.forward()
    plane.middle()

    @pl.loop(0, 4)
    def _(y):
        at = pl.ds(pl.multiple_of(y * BLOCK, BLOCK), BLOCK)
        new = dot(tokens[y].reshape(TILE, D), weight[:, :HD], NN) + shift[:, :HD]
        for g in range(2):
            rows = slice(g * BLOCK, (g + 1) * BLOCK)
            for pair in range(2):
                q = slice(pair * BLOCK, (pair + 1) * BLOCK)
                turned = turn(new[rows, q], cosines[g, at, :], sines[g, at, :], 1.0)
                queries[g, at, q] = turned.astype(BF) * jnp.asarray(SCALE, BF)

    gather.share()
    for g in range(2):
        trade[g].wait_recv()
        if g == 1:
            gather.share_far()

        @pl.loop(0, 2)
        def _(tile, g=g):
            at = pl.ds(pl.multiple_of(tile * TILE, TILE), TILE)
            bias = key_bias(table, g, tile)
            for pair in range(2):
                q = slice(pair * BLOCK, (pair + 1) * BLOCK)
                k_all = kv[0, g, :, q]
                v_all = kv[1, g, :, q]
                out = jnp.zeros((TILE, BLOCK), F32)
                for h in range(2):
                    s = dot(k_all, queries[g, at, q] * head_mask(h), NT) + bias
                    top = jnp.max(s, axis=0, keepdims=True)
                    p = jnp.exp(s - top)
                    total = jnp.sum(p, axis=0, keepdims=True)
                    w = (p * (1.0 / total)).astype(BF)
                    lse[g, 2 * pair + h : 2 * pair + h + 1, at] = top + jnp.log(total)
                    out = out + dot(w, v_all * head_mask(h), TN)
                for j in range(2):
                    attended[2 * tile + j, g, :, q] = out[j * BLOCK : (j + 1) * BLOCK].astype(BF)

    for one in trade:
        one.wait_send()
    gather.finish()
    plane.finish()


SM = pl.BlockSpec(memory_space=pltpu.SMEM)


def attend(table, tokens, weight, shift, grad_out, out_rows, cid):
    return pl.pallas_call(
        kernel_attend,
        out_shape=(
            jax.ShapeDtypeStruct((2, TOKENS, HD), BF),
            jax.ShapeDtypeStruct((2, 2, KEYS, HD), BF),
            jax.ShapeDtypeStruct((2, 8, TOKENS), F32),
            jax.ShapeDtypeStruct((4, 2, BLOCK, HD), BF),
            FULL,
            jax.ShapeDtypeStruct((4, 4, 16, D), BF),
        ),
        in_specs=[SM] + [VM] * 5,
        out_specs=(VM, VM, VM, VM, ANY, ANY),
        scratch_shapes=[
            pltpu.VMEM((2, TOKENS, BLOCK), F32),
            pltpu.VMEM((2, TOKENS, BLOCK), F32),
            pltpu.SemaphoreType.DMA((2,)),
            pltpu.SemaphoreType.DMA((2,)),
        ]
        + AG_SCRATCH[1:]
        + PG_SEMS,
        compiler_params=params(cid),
        name="attend",
    )(table, tokens, weight, shift, grad_out, out_rows)


def kernel_attend_back(
    table,
    branch,
    gathered,
    attended,
    queries,
    kv,
    lse,
    mlp_out,
    middle,
    joined_grad,
    out_part,
    hidden_out,
    weight,
    grads,
    dq,
    dkv,
    kv_out,
    kv_in,
    send,
    recv,
    *scratch,
):
    partner = {"zh": 1 - lax.axis_index("zh")}
    y0, c, up, opp, dn = ring()
    meet(list(ring_peers(up, dn, c)) + [partner])
    sems = (send, recv)
    order = (opp, up, dn, y0)
    scatter = RingScatter(
        lambda j, rows: mlp_out[order[j], c, rows, :].astype(F32),
        lambda j: mlp_out.at[order[j], 1 - c],
        *scratch,
    )
    for one in scatter.sib:
        one.start()
    order_out(gathered, weight)

    @pl.loop(0, 4)
    def _(y):
        at = pl.ds(pl.multiple_of(y * BLOCK, BLOCK), BLOCK)
        new = dot(branch[y].reshape(TILE, D), weight[...], NT)
        for g in range(2):
            grads[g, at, :] = new[g * BLOCK : (g + 1) * BLOCK].astype(BF)

    scatter.send_far()
    scatter.send_early(0)
    scatter.send_early(1)
    trade = [remote(sems, g, kv_out.at[g], kv_in.at[g], partner) for g in range(2)]
    own, other = pl.ds(0, TOKENS), pl.ds(TOKENS, TOKENS)
    for g in range(2):

        @pl.loop(0, 2)
        def _(tile, g=g):
            at = pl.ds(pl.multiple_of(tile * TILE, TILE), TILE)
            bias = key_bias(table, g, tile)
            for pair in range(2):
                q = slice(pair * BLOCK, (pair + 1) * BLOCK)
                k_all = kv[0, g, :, q]
                v_all = kv[1, g, :, q]
                new_q = jnp.zeros((TILE, BLOCK), F32)
                new_k = jnp.zeros((KEYS, BLOCK), F32)
                new_v = jnp.zeros((KEYS, BLOCK), F32)
                for h in range(2):
                    q_head = queries[g, at, q] * head_mask(h)
                    g_head = grads[g, at, q] * head_mask(h)
                    s = dot(k_all, q_head, NT) + bias
                    p = jnp.exp(s - lse[g, 2 * pair + h : 2 * pair + h + 1, at])
                    p_grad = dot(v_all, g_head, NT)
                    mean = jnp.sum(p * p_grad, axis=0, keepdims=True)
                    s_grad = (p * (p_grad - mean)).astype(BF)
                    new_v = new_v + dot(p.astype(BF), g_head, NN)
                    new_k = new_k + dot(s_grad, q_head, NN)
                    new_q = new_q + dot(s_grad, k_all * head_mask(h), TN)
                dq[g, at, q] = new_q * SCALE

                @pl.when(tile == 0)
                def _():
                    dkv[0, g, :, q] = new_k
                    dkv[1, g, :, q] = new_v

                @pl.when(tile != 0)
                def _():
                    dkv[0, g, :, q] += new_k
                    dkv[1, g, :, q] += new_v

        for i in range(2):
            kv_out[g, i] = dkv[i, g, other, :].astype(BF)
        trade[g].start()
        if g == 0:
            scatter.send_late()

    @pl.loop(0, 8)
    def _(i):
        q = pl.ds(pl.multiple_of(i * TILE, TILE), TILE)
        new = dot(attended[...].reshape(8 * BLOCK, HD), branch[:, :, :, q].reshape(8 * BLOCK, TILE), TN)
        for x in range(4):
            for zl in range(2):
                for a in range(2):
                    row = x * 64 + zl * 32 + a * 16
                    out_part[x * 4 + a * 2 + zl, :, q] = new[row : row + 16].astype(BF)

    scatter.wait()

    def add(r):
        hidden_out[r, :] = (middle[r, :] + scatter.total(r)).astype(BF)

    rows_loop(BLOCK, 32, add)
    for g in range(2):
        trade[g].wait_recv()

        @pl.loop(0, 4)
        def _(y, g=g):
            at = pl.ds(pl.multiple_of(y * BLOCK, BLOCK), BLOCK)
            cosine, sine = turn_tables(table[g, 0, y])
            for pair in range(2):
                q = slice(pair * BLOCK, (pair + 1) * BLOCK)
                joined_grad[y, g, :, q] = turn(dq[g, at, q], cosine, sine, -1.0).astype(BF)
                new = dkv[0, g, at, q] + kv_in[g, 0, at, q].astype(F32)
                joined_grad[y, g, :, HD + pair * BLOCK : HD + (pair + 1) * BLOCK] = turn(
                    new, cosine, sine, -1.0
                ).astype(BF)
            joined_grad[y, g, :, 2 * HD :] = (
                dkv[1, g, at, :] + kv_in[g, 1, at, :].astype(F32)
            ).astype(BF)

    for one in trade:
        one.wait_send()
    scatter.finish()


def attend_back(table, branch, weight, attended, queries, kv, lse, mlp_out, middle, cid):
    return pl.pallas_call(
        kernel_attend_back,
        out_shape=(
            jax.ShapeDtypeStruct((4, 2, BLOCK, 3 * HD), BF),
            jax.ShapeDtypeStruct((16, 16, D), BF),
            jax.ShapeDtypeStruct((BLOCK, D), BF),
        ),
        in_specs=[SM] + [VM] * 8,
        out_specs=(VM, VM, VM),
        scratch_shapes=[
            OUT_ROWS,
            pltpu.VMEM((2, TOKENS, HD), BF),
            pltpu.VMEM((2, TOKENS, HD), F32),
            pltpu.VMEM((2, 2, KEYS, HD), F32),
            pltpu.VMEM((2, 2, TOKENS, HD), BF),
            pltpu.VMEM((2, 2, TOKENS, HD), BF),
            pltpu.SemaphoreType.DMA((2,)),
            pltpu.SemaphoreType.DMA((2,)),
        ]
        + RS_SCRATCH[2:],
        compiler_params=params(cid),
        name="attend_back",
    )(table, branch, weight, attended, queries, kv, lse, mlp_out, middle)


def kernel_mlp(
    two,
    grad_all,
    w,
    middle,
    grad_out,
    gains,
    middle_grad,
    sums,
    out_part,
    mlp_part,
    full,
    inner,
    gate_grad,
    up_grad,
    *scratch,
):
    own, local_sem, *sems = scratch[:4]
    y, c, up, opp, dn = ring()
    meet(ring_peers(up, dn, c))

    held = jnp.logical_or(lane(FP) >= BLOCK, y < 2)

    def partial(block, put):
        a = two[block].reshape(TILE, D)
        gate = dot(a, w[:, 0].reshape(D, FP), NN)
        up_proj = dot(a, w[:, 1].reshape(D, FP), NN)
        grad = dot(grad_all[block].reshape(TILE, D), w[:, 2].reshape(D, FP), NN)
        sig = 1.0 / (1.0 + jnp.exp(-gate))
        active = gate * sig
        low = (active * up_proj).astype(BF)
        low_gate = (grad * up_proj * sig * (1.0 + gate * (1.0 - sig))).astype(BF)
        low_up = (grad * active).astype(BF)
        for ref, value in ((inner, low), (gate_grad, low_gate), (up_grad, low_up)):
            ref[block] = jnp.where(held, value, jnp.zeros((), BF)).reshape(2, BLOCK, FP)

        @pl.loop(0, 4)
        def _(i):
            q = pl.ds(pl.multiple_of(i * 512, 512), 512)
            wide = pl.ds(i * 4, 4)
            new = dot(gate_grad[block].reshape(TILE, FP), w[wide, 0].reshape(512, FP), NT)
            new = new + dot(up_grad[block].reshape(TILE, FP), w[wide, 1].reshape(512, FP), NT)
            put(q, new.reshape(2, BLOCK, 512))

        @pl.loop(0, 4)
        def _(i):
            q = pl.ds(pl.multiple_of(i * 512, 512), 512)
            wide = pl.ds(i * 4, 4)
            new = dot(inner[block].reshape(TILE, FP), w[wide, 2].reshape(512, FP), NT)
            out_part[block, :, :, q] = new.astype(BF).reshape(2, BLOCK, 512)

    scatter = ring_scatter(partial, scratch[4:])
    sums[...] = jnp.zeros_like(sums)

    def back(r):
        row = scatter.total(r)
        normed, inv = layer_norm(middle[r, :])
        grad = grad_out[r, :].astype(F32) + norm_back(row, normed, inv, gains[2:3, :])
        middle_grad[r, :] = grad
        own[r, :] = grad.astype(BF)
        sums[0:1, :] += jnp.sum(row * normed, axis=0, keepdims=True)
        sums[1:2, :] += jnp.sum(row, axis=0, keepdims=True)

    rows_loop(BLOCK, 16, back)
    done = []

    def weight_grads():
        begin = 2 * len(done)
        done.append(begin)

        @pl.loop(begin, begin + 2)
        def _(i):
            q = pl.ds(pl.multiple_of(i * TILE, TILE), TILE)
            a = two[:, :, :, q].reshape(TP * BLOCK, TILE)
            b = grad_all[:, :, :, q].reshape(TP * BLOCK, TILE)
            for k, (left, right) in enumerate(((a, gate_grad), (a, up_grad), (b, inner))):
                new = dot(left, right[...].reshape(TP * BLOCK, FP), TN).astype(BF)
                mlp_part[pl.ds(2 * i, 2), k] = new.reshape(2, BLOCK, FP)

    RingGather(own, full, local_sem, sems).run(weight_grads)
    scatter.finish()


def mlp(two, grad_all, w, middle, grad_out, gains, cid):
    return pl.pallas_call(
        kernel_mlp,
        out_shape=(
            jax.ShapeDtypeStruct((BLOCK, D), F32),
            jax.ShapeDtypeStruct((8, D), F32),
            FULL,
            jax.ShapeDtypeStruct((16, 3, BLOCK, FP), BF),
            FULL,
        ),
        in_specs=[VM] * 6,
        out_specs=(VM, VM, VM, VM, ANY),
        scratch_shapes=[pltpu.VMEM((4, 2, BLOCK, FP), BF)] * 3 + AG_SCRATCH + RS_SCRATCH,
        compiler_params=params(cid),
        name="mlp",
    )(two, grad_all, w, middle, grad_out, gains)


class PlaneScatter:
    COPIES = 12

    def __init__(self, part, a_in, b_in, a_mid, b_mid, a_last, b_last, send, recv):
        self.refs = part, a_in, b_in, a_mid, b_mid, a_last, b_last
        sems = send, recv
        half = part.shape[-1] // 2
        self.lanes = pl.ds(0, half), pl.ds(half, half)
        self.x = lax.axis_index("x")
        self.z = lax.axis_index("zh") * 2 + lax.axis_index("zl")
        self.one, self.two = [], []
        for d in range(1, 4):
            x = lax.rem(self.x + d, 4)
            z = lax.rem(self.z + d, 4)
            to_x = {"x": x}
            to_z = {"zh": z // 2, "zl": lax.rem(z, 2)}
            a, b = self.lanes
            k = d - 1
            self.one.append(remote(sems, k, part.at[:, z, :, a], a_in.at[k], to_z))
            self.one.append(remote(sems, 3 + k, part.at[x, :, :, b], b_in.at[k], to_x))
            self.two.append(remote(sems, 6 + k, a_mid.at[x], a_last.at[k], to_x))
            self.two.append(remote(sems, 9 + k, b_mid.at[z], b_last.at[k], to_z))

    def start(self):
        for copy in self.one:
            copy.start()

    def middle(self):
        part, a_in, b_in, a_mid, b_mid, _, _ = self.refs
        for copy in self.one:
            copy.wait_recv()
        a, b = self.lanes

        @pl.loop(0, 4)
        def _(i):
            a_mid[i] = (
                part[i, self.z, :, a].astype(F32) + jnp.sum(a_in[:, i].astype(F32), axis=0)
            ).astype(BF)
            b_mid[i] = (
                part[self.x, i, :, b].astype(F32) + jnp.sum(b_in[:, i].astype(F32), axis=0)
            ).astype(BF)

        for copy in self.two:
            copy.start()

    def finish(self, out):
        _, _, _, a_mid, b_mid, a_last, b_last = self.refs
        for copy in self.two:
            copy.wait_recv()
        a, b = self.lanes
        out[:, a] = (
            a_mid[self.x].astype(F32) + jnp.sum(a_last[...].astype(F32), axis=0)
        ).astype(BF)
        out[:, b] = (
            b_mid[self.z].astype(F32) + jnp.sum(b_last[...].astype(F32), axis=0)
        ).astype(BF)
        for copy in self.one + self.two:
            copy.wait_send()


def plane_scratch(rows, lanes):
    half = lanes // 2
    return [
        pltpu.VMEM((3, 4, rows, half), BF),
        pltpu.VMEM((3, 4, rows, half), BF),
        pltpu.VMEM((4, rows, half), BF),
        pltpu.VMEM((4, rows, half), BF),
        pltpu.VMEM((3, rows, half), BF),
        pltpu.VMEM((3, rows, half), BF),
        pltpu.SemaphoreType.DMA((PlaneScatter.COPIES,)),
        pltpu.SemaphoreType.DMA((PlaneScatter.COPIES,)),
    ]


def plane_peers():
    peers = []
    for d in range(1, 4):
        z = lax.rem(lax.axis_index("zh") * 2 + lax.axis_index("zl") + d, 4)
        peers.append({"x": lax.rem(lax.axis_index("x") + d, 4)})
        peers.append({"zh": z // 2, "zl": lax.rem(z, 2)})
    return peers


def kernel_qkv_back(
    joined_grad,
    weight,
    hidden,
    middle_grad,
    gains,
    tokens,
    out_part,
    input_grad,
    sums,
    shift_sum,
    qkv_sum,
    out_sum,
    part,
    *scratch,
):
    y, c, up, opp, dn = ring()
    meet(list(ring_peers(up, dn, c)) + plane_peers())
    out_scatter = PlaneScatter(out_part, *scratch[:8])
    qkv_scatter = PlaneScatter(part, *scratch[8:16])
    out_scatter.start()
    flat = joined_grad[...].reshape(TP * BLOCK, 3 * HD)

    @pl.loop(0, 8)
    def _(i):
        q = pl.ds(pl.multiple_of(i * TILE, TILE), TILE)
        new = dot(tokens[:, :, :, q].reshape(TP * BLOCK, TILE), flat, TN).astype(BF)
        part[i // 2, 2 * lax.rem(i, 2)] = new[:BLOCK]
        part[i // 2, 2 * lax.rem(i, 2) + 1] = new[BLOCK:]

    qkv_scatter.start()

    def partial(block, put):
        a = joined_grad[block].reshape(2 * BLOCK, 3 * HD)

        @pl.loop(0, 4)
        def _(i):
            q = pl.ds(pl.multiple_of(i * 512, 512), 512)
            put(q, dot(a, weight[q, :], NT).reshape(2, BLOCK, 512))

    def between():
        out_scatter.middle()
        shift_sum[...] = jnp.broadcast_to(
            jnp.sum(flat.astype(F32), axis=0, keepdims=True), shift_sum.shape
        )
        qkv_scatter.middle()

    scatter = ring_scatter(partial, scratch[16:], between)
    sums[...] = jnp.zeros_like(sums)

    def back(r):
        row = scatter.total(r)
        normed, inv = layer_norm(hidden[r, :].astype(F32))
        input_grad[r, :] = middle_grad[r, :] + norm_back(row, normed, inv, gains[0:1, :])
        sums[0:1, :] += jnp.sum(row * normed, axis=0, keepdims=True)
        sums[1:2, :] += jnp.sum(row, axis=0, keepdims=True)

    rows_loop(BLOCK, 16, back)
    scatter.finish()
    out_scatter.finish(out_sum)
    qkv_scatter.finish(qkv_sum)


def qkv_back(joined_grad, weight, hidden, middle_grad, gains, tokens, out_part, cid):
    return pl.pallas_call(
        kernel_qkv_back,
        out_shape=(
            jax.ShapeDtypeStruct((BLOCK, D), F32),
            jax.ShapeDtypeStruct((8, D), F32),
            jax.ShapeDtypeStruct((8, 3 * HD), F32),
            jax.ShapeDtypeStruct((BLOCK, 3 * HD), BF),
            jax.ShapeDtypeStruct((16, D), BF),
        ),
        in_specs=[VM] * 7,
        out_specs=(VM,) * 5,
        scratch_shapes=[pltpu.VMEM((4, 4, BLOCK, 3 * HD), BF)]
        + plane_scratch(16, D)
        + plane_scratch(BLOCK, 3 * HD)
        + RS_SCRATCH,
        compiler_params=params(cid),
        name="qkv_back",
    )(joined_grad, weight, hidden, middle_grad, gains, tokens, out_part.reshape(4, 4, 16, D))


TP_STEPS = [(dy, dc) for dy in range(4) for dc in range(2) if (dy, dc) != (0, 0)]
XZ_STEPS = [(dx, dz) for dx in range(4) for dz in range(4) if (dx, dz) != (0, 0)]


def tp_peer(step):
    y = lax.rem(lax.axis_index("y") + step[0], 4)
    c = lax.rem(lax.axis_index("core") + step[1], 2)
    return {"y": y, "core": c}, y * 2 + c


def xz_peer(step):
    x = lax.rem(lax.axis_index("x") + step[0], 4)
    z = lax.rem(lax.axis_index("zh") * 2 + lax.axis_index("zl") + step[1], 4)
    return {"x": x, "zh": z // 2, "zl": lax.rem(z, 2)}, x * 4 + z


def meet_all(split):
    peers = [tp_peer(s)[0] for s in TP_STEPS] + [xz_peer(s)[0] for s in XZ_STEPS]
    barrier = pltpu.get_barrier_semaphore()
    for peer in peers:
        pl.semaphore_signal(
            barrier, inc=1, device_id=peer, device_id_type=pl.DeviceIdType.MESH
        )

    @pl.when(split)
    def _():
        pl.semaphore_signal(
            barrier, inc=1, device_id=swap_peer(), device_id_type=pl.DeviceIdType.MESH
        )

    pl.semaphore_wait(barrier, len(peers) + split.astype(jnp.int32))


def swap_peer():
    return {"zh": lax.axis_index("core"), "core": lax.axis_index("zh")}


def swap_start(split, src, dst, local_sem, sems, i):
    @pl.when(split)
    def _():
        remote(sems, i, src, dst, swap_peer()).start()

    @pl.when(jnp.logical_not(split))
    def _():
        pltpu.make_async_copy(src, dst, local_sem).start()


def swap_wait(split, src, dst, local_sem, sems, i):
    @pl.when(split)
    def _():
        remote(sems, i, src, dst, swap_peer()).wait()

    @pl.when(jnp.logical_not(split))
    def _():
        pltpu.make_async_copy(src, dst, local_sem).wait()


N_TP = len(TP_STEPS)
N_XZ = len(XZ_STEPS)


class PlaneGather:
    COPIES = 12

    def __init__(self, src, full, local_sem, send, recv):
        sems = send, recv
        half = src.shape[-1] // 2
        a, b = pl.ds(0, half), pl.ds(half, half)
        rest = (slice(None),) * (len(src.shape) - 1)
        x = lax.axis_index("x")
        z = lax.axis_index("zh") * 2 + lax.axis_index("zl")
        self.one, self.two = [], []
        every = slice(None)
        for d in range(1, 4):
            k = d - 1
            z_to = lax.rem(z + d, 4)
            to_x = {"x": lax.rem(x + d, 4)}
            to_z = {"zh": z_to // 2, "zl": lax.rem(z_to, 2)}
            self.one.append(remote(sems, k, src.at[rest + (a,)], full.at[(x, z) + rest + (a,)], to_x))
            self.one.append(remote(sems, 3 + k, src.at[rest + (b,)], full.at[(x, z) + rest + (b,)], to_z))
            row = full.at[(every, z) + rest + (a,)]
            self.two.append(remote(sems, 6 + k, row, row, to_z))
            row = full.at[(x, every) + rest + (b,)]
            self.two.append(remote(sems, 9 + k, row, row, to_x))
        self.here = pltpu.make_async_copy(src, full.at[x, z], local_sem)

    def start(self):
        for copy in self.one:
            copy.start()
        self.here.start()

    def middle(self):
        self.here.wait()
        for copy in self.one:
            copy.wait_recv()
        for copy in self.two:
            copy.start()

    def finish(self):
        for copy in self.two:
            copy.wait_recv()
        for copy in self.one + self.two:
            copy.wait_send()


PG_SEMS = [
    pltpu.SemaphoreType.DMA,
    pltpu.SemaphoreType.DMA((PlaneGather.COPIES,)),
    pltpu.SemaphoreType.DMA((PlaneGather.COPIES,)),
]


def first_lane(rank):
    return jnp.where(rank < 4, 6 * rank, 5 * rank + 3) * BLOCK


def head_lane(part, rank):
    return part * D + (lax.rem(rank, 2) * 4 + rank // 2) * HD


def lanes_at(start, n):
    return pl.ds(pl.multiple_of(start, BLOCK), n)


def spread_gains(small_all, gains, shift, rank):
    rows = small_all[...].reshape(BLOCK, BLOCK)
    source = lax.broadcasted_iota(jnp.int32, (BLOCK, 1), 0)
    f = lane(D)
    mine = (f // 16) == source
    for i in range(4):
        pick = (source == 16 * i + lax.rem(f, 16)).astype(F32)
        value = jnp.dot(rows, pick, preferred_element_type=F32)
        gains[i : i + 1, :] = jnp.sum(jnp.where(mine, value, 0.0), axis=0, keepdims=True)
    core = lax.rem(source, 2)
    y = lax.rem(source // 2, 4)
    zl = lax.rem(source // 8, 2)
    zh = lax.rem(source // 16, 2)
    x = source // 32
    owner = (zh * 4 + y) * 16 + x * 4 + zl * 2 + core
    for i in range(3):
        j = head_lane(i, rank) + lane(HD)
        pick = (source == 64 + lax.rem(j, 48)).astype(F32)
        value = jnp.dot(rows, pick, preferred_element_type=F32)
        value = jnp.sum(jnp.where(j // 48 == owner, value, 0.0), axis=0, keepdims=True)
        shift[:, i * HD : (i + 1) * HD] = value


def kernel_front(
    small,
    hidden,
    w_qkv,
    w_gate,
    w_up,
    w_down,
    w_out,
    small_all,
    gains,
    shift,
    qkv_full,
    mlp_rows,
    out_rows,
    full,
    own,
    qkv_rows,
    local,
    send,
    recv,
    *sems,
):
    me = lax.axis_index("y") * 2 + lax.axis_index("core")
    xz = lax.axis_index("x") * 4 + lax.axis_index("zh") * 2 + lax.axis_index("zl")
    split = lax.axis_index("zh") != lax.axis_index("core")
    meet_all(split)
    cp = functools.partial(remote, (send, recv))
    tiny, qkv, mlp = [], [], []
    for k, step in enumerate(TP_STEPS):
        peer, there = tp_peer(step)
        tiny.append(cp(k, small, small_all.at[xz, me], peer))
        for i in range(3):
            src = w_qkv.at[:, lanes_at(head_lane(i, there), HD)]
            dst = qkv_rows.at[me, :, pl.ds(i * HD, HD)]
            qkv.append(cp((1 + i) * N_TP + k, src, dst, peer))
        for i, w in enumerate((w_gate, w_up, w_down)):
            src = w.at[:, lanes_at(first_lane(there), FP)]
            mlp.append(cp((4 + i) * N_TP + k, src, mlp_rows.at[i, me], peer))
    keep = [pltpu.make_async_copy(small, small_all.at[xz, me], local.at[0])]
    for i, w in enumerate((w_gate, w_up, w_down)):
        src = w_qkv.at[:, lanes_at(head_lane(i, me), HD)]
        dst = qkv_rows.at[me, :, pl.ds(i * HD, HD)]
        keep.append(pltpu.make_async_copy(src, dst, local.at[1 + i]))
        src = w.at[:, lanes_at(first_lane(me), FP)]
        keep.append(pltpu.make_async_copy(src, mlp_rows.at[i, me], local.at[4 + i]))
    for one in tiny + qkv + keep:
        one.start()
    last = 7 * N_TP + N_XZ
    for one in tiny:
        one.wait()
    keep[0].wait()
    wide = []
    for k, step in enumerate(XZ_STEPS):
        peer, _ = xz_peer(step)
        wide.append(cp(7 * N_TP + k, small_all.at[xz], small_all.at[xz], peer))
    for one in wide:
        one.start()
    for one in qkv + keep[1:]:
        one.wait()
    plane = PlaneGather(qkv_rows, qkv_full, *sems[:3])
    plane.start()
    for one in mlp:
        one.start()
    swap_start(split, w_out, out_rows, local.at[7], (send, recv), last)
    for one in wide:
        one.wait()
    gains[...] = jnp.zeros_like(gains)
    spread_gains(small_all, gains, shift, me)

    def norm(r):
        normed, _ = layer_norm(hidden[r, :].astype(F32))
        own[r, :] = (normed * gains[0:1, :] + gains[1:2, :]).astype(BF)

    rows_loop(BLOCK, 16, norm)
    gather = RingGather(own, full, sems[3], sems[4:])
    gather.start()
    plane.middle()
    gather.forward()
    gather.share()
    gather.share_far()
    for one in mlp:
        one.wait()
    swap_wait(split, w_out, out_rows, local.at[7], (send, recv), last)
    gather.finish()
    plane.finish()


def front(small, hidden, w_qkv, w_gate, w_up, w_down, w_out, cid):
    n = 7 * N_TP + N_XZ + 1
    return pl.pallas_call(
        kernel_front,
        out_shape=(
            jax.ShapeDtypeStruct((16, TP, 1, BLOCK), F32),
            jax.ShapeDtypeStruct((8, D), F32),
            jax.ShapeDtypeStruct((1, 3 * HD), F32),
            jax.ShapeDtypeStruct((4, 4, TP, 16, 3 * HD), BF),
            jax.ShapeDtypeStruct((3, TP, 16, FP), BF),
            jax.ShapeDtypeStruct((16, D), BF),
            FULL,
        ),
        in_specs=[ANY, VM] + [ANY] * 5,
        out_specs=(VM, VM, VM, ANY, ANY, ANY, ANY),
        scratch_shapes=[
            pltpu.VMEM((BLOCK, D), BF),
            pltpu.VMEM((TP, 16, 3 * HD), BF),
            pltpu.SemaphoreType.DMA((8,)),
            pltpu.SemaphoreType.DMA((n,)),
            pltpu.SemaphoreType.DMA((n,)),
        ]
        + PG_SEMS
        + AG_SCRATCH[1:],
        compiler_params=params(cid),
        name="front",
    )(small, hidden, w_qkv, w_gate, w_up, w_down, w_out)


def kernel_collect(
    one_sums,
    two_sums,
    shift,
    qkv,
    mlp,
    out,
    small,
    qkv_grad,
    gate_grad,
    up_grad,
    down_grad,
    out_grad,
    terms,
    terms_in,
    shift_own,
    shift_in,
    own,
    small_all,
    qkv_all,
    mlp_all,
    out_all,
    local,
    *sems,
):
    me = lax.axis_index("y") * 2 + lax.axis_index("core")
    xz = lax.axis_index("x") * 4 + lax.axis_index("zh") * 2 + lax.axis_index("zl")
    split = lax.axis_index("zh") != lax.axis_index("core")
    meet_all(split)
    cp = functools.partial(remote, sems)
    big, extra = [], []
    near, tile = pl.ds(BLOCK, FP - BLOCK), pl.ds(0, BLOCK)
    base = 2 * N_XZ + N_TP
    for k, step in enumerate(TP_STEPS):
        peer, there = tp_peer(step)
        dst = mlp_all.at[:, :, lanes_at(first_lane(me) + BLOCK, FP - BLOCK)]
        big.append(cp(base + k, mlp.at[:, there, :, near], dst, peer))
        dst = mlp_all.at[:, :, lanes_at(first_lane(me), BLOCK)]
        extra.append(cp(base + N_TP + k, mlp.at[:, there, :, tile], dst, peer))
        for i in range(3):
            dst = qkv_all.at[:, lanes_at(head_lane(i, me), HD)]
            big.append(cp(base + (2 + i) * N_TP + k, qkv.at[there, :, pl.ds(i * HD, HD)], dst, peer))
    keep = []
    dst = mlp_all.at[:, :, lanes_at(first_lane(me) + BLOCK, FP - BLOCK)]
    keep.append(pltpu.make_async_copy(mlp.at[:, me, :, near], dst, local.at[0]))
    for i in range(3):
        dst = qkv_all.at[:, lanes_at(head_lane(i, me), HD)]
        keep.append(pltpu.make_async_copy(qkv.at[me, :, pl.ds(i * HD, HD)], dst, local.at[1 + i]))
    dst = mlp_all.at[:, :, lanes_at(first_lane(me), BLOCK)]
    keep_tile = pltpu.make_async_copy(mlp.at[:, me, :, tile], dst, local.at[4])
    first_four = me < 4

    terms[...] = jnp.zeros_like(terms)
    shift_own[...] = jnp.zeros_like(shift_own)
    for p in range(16):
        q = slice(p * BLOCK, (p + 1) * BLOCK)
        terms[p, 0:2, :] = one_sums[0:2, q]
        terms[p, 2:4, :] = two_sums[0:2, q]
    for i in range(6):
        shift_own[i : i + 1, :] = shift[0:1, i * BLOCK : (i + 1) * BLOCK]
    wide = []
    for k, step in enumerate(XZ_STEPS):
        peer, there = xz_peer(step)
        wide.append(cp(k, terms.at[there], terms_in.at[xz], peer))
        wide.append(cp(N_XZ + k, shift_own, shift_in.at[xz], peer))
    for one in wide + big + keep:
        one.start()

    @pl.when(first_four)
    def _():
        keep_tile.start()
        for one in extra:
            one.start()

    last = base + 5 * N_TP
    swap_start(split, out, out_all, local.at[5], sems, last)
    for one in wide:
        one.wait()
    terms_in[xz] = terms[xz]
    shift_in[xz] = shift_own[...]
    own[0:8, :] = jnp.sum(terms_in[...], axis=0)
    own[8:16, :] = jnp.sum(shift_in[...], axis=0)
    tiny = []
    for k, step in enumerate(TP_STEPS):
        peer, _ = tp_peer(step)
        tiny.append(cp(2 * N_XZ + k, own, small_all.at[me], peer))
    for one in tiny:
        one.start()
    for one in big:
        one.wait()
    for one in keep:
        one.wait()
    for k, step in enumerate(TP_STEPS):
        source = lax.rem(lax.axis_index("y") + 4 - step[0], 4) * 2 + lax.rem(
            lax.axis_index("core") + 2 - step[1], 2
        )

        @pl.when(source < 4)
        def _(k=k):
            extra[k].wait_recv()

    @pl.when(first_four)
    def _():
        keep_tile.wait()
        for one in extra:
            one.wait_send()

    qkv_grad[...] = qkv_all[...].astype(F32)
    gate_grad[...] = mlp_all[0].astype(F32)
    up_grad[...] = mlp_all[1].astype(F32)
    down_grad[...] = mlp_all[2].astype(F32)
    swap_wait(split, out, out_all, local.at[5], sems, last)
    out_grad[...] = out_all[...].astype(F32)
    for one in tiny:
        one.wait()
    small_all[me] = own[...]
    small[...] = small_all[...]


def collect(one_sums, two_sums, shift, qkv, mlp, out, cid):
    n = 2 * N_XZ + 6 * N_TP + 1
    wide = jax.ShapeDtypeStruct((16, FF), F32)
    return pl.pallas_call(
        kernel_collect,
        out_shape=(
            jax.ShapeDtypeStruct((TP, 16, BLOCK), F32),
            jax.ShapeDtypeStruct((16, 3 * D), F32),
            wide,
            wide,
            wide,
            jax.ShapeDtypeStruct((16, D), F32),
        ),
        in_specs=[VM] * 3 + [ANY] * 3,
        out_specs=(VM,) * 6,
        scratch_shapes=[
            pltpu.VMEM((16, 8, BLOCK), F32),
            pltpu.VMEM((16, 8, BLOCK), F32),
            pltpu.VMEM((8, BLOCK), F32),
            pltpu.VMEM((16, 8, BLOCK), F32),
            pltpu.VMEM((16, BLOCK), F32),
            pltpu.VMEM((TP, 16, BLOCK), F32),
            pltpu.VMEM((16, 3 * D), BF),
            pltpu.VMEM((3, 16, FF), BF),
            pltpu.VMEM((16, D), BF),
            pltpu.SemaphoreType.DMA((6,)),
            pltpu.SemaphoreType.DMA((n,)),
            pltpu.SemaphoreType.DMA((n,)),
        ],
        compiler_params=params(cid),
        name="collect",
    )(one_sums, two_sums, shift, qkv, mlp, out)


def body(
    hidden_in,
    cotangent,
    seq_lengths,
    slot_block,
    ln1_gain,
    ln1_bias,
    w_qkv,
    qkv_bias,
    w_out,
    ln2_gain,
    ln2_bias,
    w_gate,
    w_up,
    w_down,
):
    bf, f32 = BF, F32
    zh = lax.axis_index("zh")
    y = lax.axis_index("y")
    core = lax.axis_index("core")
    xz = lax.axis_index("x") * 4 + zh * 2 + lax.axis_index("zl")

    lengths = seq_lengths[0]
    small = jnp.concatenate(
        [
            ln1_gain.astype(f32),
            ln1_bias.astype(f32),
            ln2_gain.astype(f32),
            ln2_bias.astype(f32),
            qkv_bias.astype(f32),
            lengths.astype(f32),
            slot_block[0].astype(f32),
            jnp.zeros(6, f32),
        ]
    ).reshape(1, BLOCK)
    hidden = permute_features(hidden_in[0])
    small_all, gains, shift, qkv_full, mlp_rows, out_rows, one_all = front(
        small, hidden, w_qkv, w_gate, w_up, w_down, w_out, 0
    )
    qkv_full = qkv_full.reshape(D, 3 * HD)
    mlp_full = lax.all_gather(mlp_rows.reshape(3, BLOCK, FP), XZ, axis=0, tiled=False)
    out_rows = permute_features(out_rows)
    small_all = small_all.reshape(BLOCK, BLOCK)

    plan = lax.dynamic_slice_in_dim(small_all, xz * TP + y * 2, 2, 0)[:, 112:122].astype(jnp.int32)
    blocks = plan[:, 2:].reshape(2, 2, 4)
    own_blocks = lax.dynamic_index_in_dim(blocks, zh, axis=1, keepdims=False)
    other_blocks = lax.dynamic_index_in_dim(blocks, 1 - zh, axis=1, keepdims=False)
    start = jnp.concatenate([own_blocks, other_blocks], axis=1) * BLOCK
    first_pad = (plan[:, 0:1] + BLOCK - 1) // BLOCK * BLOCK
    second = (start >= first_pad).astype(jnp.int32)
    limit = jnp.where(second == 1, plan[:, 1:2], plan[:, 0:1])
    table = jnp.stack([start - second * first_pad, second, limit], axis=1)
    place = (zh * 4 + y) * BLOCK
    _, _, slot_valid = block_places(lengths, slot_block[0])
    own_valid = lax.dynamic_slice_in_dim(slot_valid, place, BLOCK, 0)

    grad_out = permute_features(cotangent[0]) * own_valid[:, None].astype(bf)

    queries, kv, lse, attended, grad_all, out_full = attend(
        table, one_all, qkv_full, shift, grad_out, out_rows, 6
    )
    middle, two_all = out_proj(attended, out_full, hidden, gains, 2)
    middle_grad, two_sums, mlp_out, mlp_part, branch_all = mlp(
        two_all, grad_all, mlp_full, middle, grad_out, gains, 3
    )
    mlp_sum = lax.psum_scatter(
        mlp_part.reshape(16 * 3 * BLOCK, FP), XZ, scatter_dimension=0, tiled=True
    )
    joined_grad, out_part, hidden_out = attend_back(
        table, branch_all, out_full, attended, queries, kv, lse, mlp_out, middle, 7
    )
    input_grad, one_sums, shift_sum, qkv_sum, out_sum = qkv_back(
        joined_grad, qkv_full, hidden, middle_grad, gains, one_all, out_part, 4
    )

    small_sum, qkv_grad, gate_sum, up_sum, down_sum, out_grad = collect(
        one_sums,
        two_sums,
        shift_sum,
        qkv_sum.reshape(TP, 16, FP),
        mlp_sum.reshape(3, TP, 16, FP),
        out_sum,
        5,
    )
    vectors = jnp.sum(small_sum[:, :4], axis=0)
    vectors = lax.dynamic_slice_in_dim(vectors, (y * 2 + core) * 16, 16, 1)
    shift_grad = small_sum[:, 8:14].reshape(4, 2, 3, HD).transpose(2, 1, 0, 3).reshape(128, 48)
    row = (zh * 4 + y) * 16 + lax.axis_index("x") * 4 + lax.axis_index("zl") * 2 + core
    shift_grad = lax.dynamic_index_in_dim(shift_grad, row, 0, False)
    return (
        restore_features(hidden_out)[None],
        restore_features(input_grad)[None],
        vectors[0],
        vectors[1],
        qkv_grad,
        shift_grad,
        restore_features(out_grad),
        vectors[2],
        vectors[3],
        gate_sum,
        up_sum,
        down_sum,
    )


def solution(mesh):
    inner = Mesh(mesh.devices.reshape(2, 4, 4, 2, 2), ROWS)
    rows = P(ROWS)
    tokens = P(GRP, SLOT, None)
    placed = (
        tokens,
        tokens,
        P(GRP, None),
        P(GRP, None),
        rows,
        rows,
        P(ROWS, None),
        rows,
        P(ROWS, None),
        rows,
        rows,
        P(ROWS, None),
        P(ROWS, None),
        P(ROWS, None),
    )
    return jax.shard_map(
        body,
        mesh=inner,
        in_specs=placed,
        out_specs=(
            tokens,
            tokens,
            rows,
            rows,
            P(ROWS, None),
            rows,
            P(ROWS, None),
            rows,
            rows,
            P(ROWS, None),
            P(ROWS, None),
            P(ROWS, None),
        ),
        check_vma=False,
    )
```

profile of v0, /device:TPU:1, one launch (start us, length us, event | category | flops | bytes accessed | tf_op | source)
XLA Modules:
  0.0 398.1 jit_solution(11515265579961802753)
XLA Ops:
  7.2 0.7 convert_bitcast_fusion.1
  8.0 0.7 multiply_bitcast_fusion
  8.7 1.3 copy.54
  10.1 1.0 copy.56.hidden
  11.1 3.9 concatenate.21
  15.0 44.9 %front.1 = (f32[16,8,1,128]{3,2,1,0:T(1,128)}, f32[8,2048]{1,0:T(8,128)}, f32[1,768]{1,0:T(1,128)}, bf16[4,4,8,16,768]{4,3,2,1,0:T(8,128)(2,1)}, bf16[3,8,16,768...) custom-call(f32[1,128]{1,0:T(1,128)} %bitcast.84, bf16[128,2048]{1,0:T(8,128)(2,1)} %copy.56.hidden, ...), custom_call_target="tpu_custom_call" | custom-call | tf_op jit(solution)/shard_map/front/pallas_call | solution.py:1217
  60.0 0.6 fusion.3
  61.8 0.7 constant_dynamic-slice_fusion.4
  62.9 1.1 reshape.324
  64.1 0.9 reshape.325.out_rows
  65.0 1.4 fusion
  66.6 0.6 pad_add_fusion.table
  67.2 0.9 broadcast_multiply_fusion.grad_out
  68.1 45.2 %attend.1 = (bf16[2,512,256]{2,1,0:T(8,128)(2,1)}, bf16[2,2,1024,256]{3,2,1,0:T(8,128)(2,1)}, f32[2,8,512]{2,1,0:T(8,128)}, bf16[4,2,128,256]{3,2,1,0:T(8,128)(2...) custom-call(s32[2,3,8]{2,1,0:T(4,128)} %pad_add_fusion.table, ...), custom_call_target="tpu_custom_call" | custom-call | tf_op jit(solution)/shard_map/attend/pallas_call | solution.py:532
  113.3 51.6 %out_proj.1 = (f32[128,2048]{1,0:T(8,128)}, bf16[4,2,128,2048]{3,2,1,0:T(8,128)(2,1)}) custom-call(bf16[4,2,128,256]{3,2,1,0:T(8,128)(2,1)} %get-tuple-element.51.attended, bf16[4,4,16,2048]{3,2,1,0:T(8,128)(2,1)} %get-tuple-element.52.gathered, bf16[128,2048]{1,0:T(8,128)(2,1)} %copy.56.hidden, f32[8,2048]{1,0:T(8,128)} %get-tuple-element.53.gains), custom_call_target="tpu_custom_call" | custom-call | tf_op jit(solution)/shard_map/out_proj/pallas_call | solution.py:361
  165.0 74.1 %mlp.1 = (f32[128,2048]{1,0:T(8,128)}, f32[8,2048]{1,0:T(8,128)}, bf16[4,2,128,2048]{3,2,1,0:T(8,128)(2,1)}, bf16[16,3,128,768]{3,2,1,0:T(8,128)(2,1)}, bf16[4,2,128,2048]{3,2,1,0:T(8,128)(2,1)}) custom-call(bf16[4,2,128,2048]{3,2,1,0:T(8,128)(2,1)} %get-tuple-element.54.two, bf16[4,2,128,2048]{3,2,1,0:T(8,128)(2,1)} %get-tuple-element.55.grad_all, ...), custom_call_target="tpu_custom_call" | custom-call | tf_op jit(solution)/shard_map/mlp/pallas_call | solution.py:797
  239.1 69.1 %attend_back.1 = (bf16[4,2,128,768]{3,2,1,0:T(8,128)(2,1)}, bf16[16,16,2048]{2,1,0:T(8,128)(2,1)}, bf16[128,2048]{1,0:T(8,128)(2,1)}) custom-call(s32[2,3,8]{2,1,0:T(4,128)} %pad_add_fusion.table, bf16[4,2,128,2048]{3,2,1,0:T(8,128)(2,1)} %get-tuple-element.58.branch, bf16[4,4,16,2048]{3,2,1,0:T(8,128)(2,1)} %get-tuple-element.52.gathered, ...), custom_call_target="tpu_custom_call" | custom-call | tf_op jit(solution)/shard_map/attend_back/pallas_call | solution.py:688
  308.2 1.3 copy.64
  309.6 1.0 copy.71
  310.6 48.0 %qkv_back.1 = (f32[128,2048]{1,0:T(8,128)}, f32[8,2048]{1,0:T(8,128)}, f32[8,768]{1,0:T(8,128)}, bf16[128,768]{1,0:T(8,128)(2,1)}, bf16[16,2048]{1,0:T(8,128)(2,1)}) custom-call(bf16[4,2,128,768]{3,2,1,0:T(8,128)(2,1)} %get-tuple-element.64.joined_grad, bf16[2048,768]{1,0:T(8,128)(2,1)} %bitcast.66, bf16[128,2048]{1,0:T(8,128)(2,1)} %copy.56.hidden, ...), custom_call_target="tpu_custom_call" | custom-call | tf_op jit(solution)/shard_map/qkv_back/pallas_call | solution.py:961
  358.6 1.5 copy.67
  360.3 1.3 copy.72
  361.6 18.8 %collect.1 = (f32[8,16,128]{2,1,0:T(8,128)}, f32[16,6144]{1,0:T(8,128)}, f32[16,5632]{1,0:T(8,128)}, f32[16,5632]{1,0:T(8,128)}, f32[16,5632]{1,0:T(8,128)}, /*index=5*/f32[16,2048]{1,0:T(8,128)}) custom-call(f32[8,2048]{1,0:T(8,128)} %get-tuple-element.68.one_sums, f32[8,2048]{1,0:T(8,128)} %get-tuple-element.69.two_sums, ...), custom_call_target="tpu_custom_call" | custom-call | tf_op jit(solution)/shard_map/collect/pallas_call | solution.py:1366
  380.4 0.8 slice_reduce_fusion
  381.3 0.8 slice.55
  382.2 0.5 slice_bitcast_fusion.1
  382.8 1.2 reshape.334
  384.2 1.3 reshape.335
  386.1 1.8 copy.84
  387.9 1.7 copy.85
  389.6 0.7 copy.86
  390.3 0.7 copy.87
  (39 shorter events, 2.6 us)
Async XLA Ops:
  7.2 52.8 %copy-start.3 = (s32[1,2]{1,0:T(1,128)S(1)}, s32[1,2]{1,0:T(1,128)}, u32[]{:S(2)}) copy-start(s32[1,2]{1,0:T(1,128)} %param.16) | copy-start | bytes 28
  7.2 54.1 %copy-start = (bf16[1,128,2048]{2,1,0:T(8,128)(2,1)S(1)}, bf16[1,128,2048]{2,1,0:T(8,128)(2,1)}, u32[]{:S(2)}) copy-start(bf16[1,128,2048]{2,1,0:T(8,128)(2,1)} %param.15) | copy-start | bytes 1572868
  7.2 157.7 %all-gather.2.cloned.1.call-start = ((), (), s32[]{:S(2)}) async-start(), calls=%async_computation.1 | async-start | bytes 10027008 | tf_op jit(solution)/shard_map/all_gather | solution.py:1437
  59.9 301.7 %reduce-scatter.2.cloned.1.call-start = ((), (), s32[]{:S(2)}) async-start(), calls=%async_computation.2 | async-start | bytes 10027008 | tf_op jit(solution)/shard_map/reduce_scatter | solution.py:1463
  380.4 9.2 %copy-start.2 = (f32[16,5632]{1,0:T(8,128)S(1)}, f32[16,5632]{1,0:T(8,128)}, u32[]{:S(2)}) copy-start(f32[16,5632]{1,0:T(8,128)} %get-tuple-element.143) | copy-start | bytes 1081348
  380.4 9.9 %copy-start.1 = (f32[16,5632]{1,0:T(8,128)S(1)}, f32[16,5632]{1,0:T(8,128)}, u32[]{:S(2)}) copy-start(f32[16,5632]{1,0:T(8,128)} %get-tuple-element.144) | copy-start | bytes 1081348
Sparse Core Ops, SparseCore 0:
  60.0 99.6 all-gather.1
  239.2 116.0 reduce-scatter.1
where the time goes:
time: 403 us; the launch traced here: 398 us
  Pallas kernels  352 us (87%)
  local copies, waits for them, and re-layouts  25.7 us (6%)
  between operations  15.2 us (4%)
  other arithmetic  5.41 us (1%)
    pallas_call x1, Pallas kernels, mlp(): pl.pallas_call(kernel_mlp, out_shape=(jax.ShapeDtypeStruct((BLOCK, D), F3...  74.1 us
    pallas_call x1, Pallas kernels, attend_back(): pl.pallas_call(kernel_attend_back, out_shape=(jax.ShapeDtypeStruct((4, 2,...  69.1 us
    pallas_call x1, Pallas kernels, out_proj(): pl.pallas_call(kernel_out_proj, out_shape=(jax.ShapeDtypeStruct((BLOCK, D...  51.6 us
    pallas_call x1, Pallas kernels, qkv_back(): pl.pallas_call(kernel_qkv_back, out_shape=(jax.ShapeDtypeStruct((BLOCK, D...  48 us
    pallas_call x1, Pallas kernels, attend(): pl.pallas_call(kernel_attend, out_shape=(jax.ShapeDtypeStruct((2, TOKENS,...  45.2 us
    pallas_call x1, Pallas kernels, front(): pl.pallas_call(kernel_front, out_shape=(jax.ShapeDtypeStruct((16, TP, 1,...  44.9 us
    pallas_call x1, Pallas kernels, collect(): pl.pallas_call(kernel_collect, out_shape=(jax.ShapeDtypeStruct((TP, 16, B...  18.8 us
    unnamed x19, local copies, waits for them, and re-layouts  9.18 us
  transfers between devices with their start and end apart: 2, of which 0 were waited for; matrix products, arithmetic and copies ran while one was open for 3% of the time, Pallas kernels for 54%

commit v1 on v0

--- a/solution.py
+++ b/solution.py
@@ -28,30 +28,39 @@
 SLOT = ("zh", "y")
 
 
-def permute_features(v):
-    lead = v.shape[:-1]
-    n = len(lead)
-    v = v.reshape(lead + (2, 4, 4, 2, 32))
-    v = v.transpose(tuple(range(n)) + (n + 2, n, n + 3, n + 1, n + 4))
-    return v.reshape(lead + (D,))
-
-
-def restore_features(v):
-    lead = v.shape[:-1]
-    n = len(lead)
-    v = v.reshape(lead + (4, 2, 2, 4, 32))
-    v = v.transpose(tuple(range(n)) + (n + 1, n + 3, n, n + 2, n + 4))
-    return v.reshape(lead + (D,))
-
-
-def block_places(lengths, blocks):
-    first_pad = (lengths[0] + BLOCK - 1) // BLOCK * BLOCK
-    offsets = jnp.arange(BLOCK, dtype=jnp.int32)
-    placed = (blocks[:, None] * BLOCK + offsets[None, :]).reshape(-1)
-    second = (placed >= first_pad).astype(jnp.int32)
-    position = placed - second * first_pad
-    limit = jnp.where(second == 1, lengths[1], lengths[0])
-    return second, position, position < limit
+def permute_rows(row):
+    group = lane(BLOCK) // 32
+    tiles = []
+    for x in range(4):
+        for zh in range(2):
+            for zl in range(2):
+                out = None
+                for y in range(4):
+                    first = zh * 1024 + y * 256 + x * 64 + zl * 32
+                    tile = first // BLOCK * BLOCK
+                    shift = (32 * y - first % BLOCK) % BLOCK
+                    value = row[:, tile : tile + BLOCK]
+                    value = pltpu.roll(value, shift, 1) if shift else value
+                    out = value if out is None else jnp.where(group == y, value, out)
+                tiles.append(out)
+    return jnp.concatenate(tiles, axis=1)
+
+
+def restore_rows(row):
+    group = lane(BLOCK) // 32
+    tiles = []
+    for t in range(D // BLOCK):
+        out = None
+        for j in range(4):
+            first = t * BLOCK + 32 * j
+            zh, y, x, zl = first // 1024, first // 256 % 4, first // 64 % 4, first // 32 % 2
+            tile = (x * 4 + zh * 2 + zl) * BLOCK
+            shift = (32 * j - 32 * y) % BLOCK
+            value = row[:, tile : tile + BLOCK]
+            value = pltpu.roll(value, shift, 1) if shift else value
+            out = value if out is None else jnp.where(group == j, value, out)
+        tiles.append(out)
+    return jnp.concatenate(tiles, axis=1)
 
 
 def layer_norm(values):
@@ -338,11 +347,9 @@
 
     def partial(block, put):
         a = attended[block].reshape(2 * BLOCK, HD)
-
-        @pl.loop(0, 4)
-        def _(i):
-            q = pl.ds(pl.multiple_of(i * 512, 512), 512)
-            put(q, jnp.dot(a, weight[:, q], preferred_element_type=F32).reshape(2, BLOCK, 512))
+        for i in range(4):
+            q = slice(i * 512, (i + 1) * 512)
+            put(q, dot(a, weight[:, q], NN).reshape(2, BLOCK, 512))
 
     scatter = ring_scatter(partial, scratch[4:])
 
@@ -404,7 +411,7 @@
     return v * cosine + jnp.where(entry < ROT // 2, -ahead, behind) * s
 
 
-def key_bias(table, g, tile):
+def key_bias(table, g, tile, blocks):
     token = lane(BLOCK)
     q_code, q_low = [], []
     for j in range(2):
@@ -415,7 +422,7 @@
     q_low = jnp.concatenate(q_low, axis=1)
     column = lax.broadcasted_iota(jnp.int32, (BLOCK, 1), 0)
     rows = []
-    for k in range(8):
+    for k in blocks:
         place = table[g, 0, k] + column
         code = jnp.where(place < table[g, 2, k], table[g, 1, k] * 4096 + place, 1 << 20)
         kept = jnp.logical_and(code <= q_code, code >= q_low)
@@ -428,43 +435,72 @@
     return jnp.where(first if h == 0 else jnp.logical_not(first), 1.0, 0.0).astype(BF)
 
 
+def load(pairs, sems, first=0):
+    copies = []
+    for i, (src, dst) in enumerate(pairs):
+        copies.append(pltpu.make_async_copy(src, dst, sems.at[first + i]))
+        copies[-1].start()
+    return copies
+
+
 def kernel_attend(
     table,
-    tokens,
-    weight,
+    tokens_hbm,
+    weight_hbm,
     shift,
-    grad_out,
-    out_rows,
+    cotangent,
+    out_in,
     queries,
     kv,
     lse,
     attended,
+    grad_out,
     grad_all,
     out_full,
+    out_rows,
+    tokens,
+    weight,
     cosines,
     sines,
+    tops,
+    totals,
+    mixed,
+    local,
     send,
     recv,
-    *more_sems,
+    *sems,
 ):
     partner = {"zh": 1 - lax.axis_index("zh")}
+    weight_in, *token_in = load(
+        [(weight_hbm, weight)] + [(tokens_hbm.at[y], tokens.at[y]) for y in range(4)], local
+    )
     y0, c, up, opp, dn = ring()
+    base, limit = table[c, 0, y0], table[c, 2, y0]
+
+    def mask(r):
+        place = base + r.start + lax.broadcasted_iota(jnp.int32, (16, 1), 0)
+        row = jnp.where(place < limit, cotangent[r, :].astype(F32), 0.0)
+        grad_out[r, :] = permute_rows(row).astype(BF)
+
+    rows_loop(BLOCK, 16, mask)
+    out_rows[...] = permute_rows(out_in[...].astype(F32)).astype(BF)
     meet(list(ring_peers(up, dn, c)) + plane_peers())
-    sems = (send, recv)
-    gather = RingGather(grad_out, grad_all, more_sems[0], more_sems[1:3])
+    gather = RingGather(grad_out, grad_all, sems[0], sems[1:3])
     gather.start()
-    plane = PlaneGather(out_rows, out_full, *more_sems[3:])
+    plane = PlaneGather(out_rows, out_full, *sems[3:])
     plane.start()
 
-    @pl.loop(0, 4)
-    def _(y):
-        at = pl.ds(pl.multiple_of(y * BLOCK, BLOCK), BLOCK)
+    for y in range(4):
         for g in range(2):
+            at = slice(y * BLOCK, (y + 1) * BLOCK)
             cosine, sine = turn_tables(table[g, 0, y])
             cosines[g, at, :] = cosine
             sines[g, at, :] = sine
-        a = tokens[y].reshape(TILE, D)
-        new = dot(a, weight[:, HD:], NN) + shift[:, HD:]
+    weight_in.wait()
+    for y in range(4):
+        token_in[y].wait()
+        at = slice(y * BLOCK, (y + 1) * BLOCK)
+        new = dot(tokens[y].reshape(TILE, D), weight[:, HD:], NN) + shift[:, HD:]
         for g in range(2):
             rows = slice(g * BLOCK, (g + 1) * BLOCK)
             for pair in range(2):
@@ -475,16 +511,14 @@
 
     own, other = pl.ds(0, TOKENS), pl.ds(TOKENS, TOKENS)
     trade = [
-        remote(sems, g, kv.at[:, g, own, :], kv.at[:, g, other, :], partner) for g in range(2)
+        remote((send, recv), g, kv.at[:, g, own, :], kv.at[:, g, other, :], partner)
+        for g in range(2)
     ]
     for one in trade:
         one.start()
     gather.forward()
-    plane.middle()
-
-    @pl.loop(0, 4)
-    def _(y):
-        at = pl.ds(pl.multiple_of(y * BLOCK, BLOCK), BLOCK)
+    for y in range(4):
+        at = slice(y * BLOCK, (y + 1) * BLOCK)
         new = dot(tokens[y].reshape(TILE, D), weight[:, :HD], NN) + shift[:, :HD]
         for g in range(2):
             rows = slice(g * BLOCK, (g + 1) * BLOCK)
@@ -493,32 +527,55 @@
                 turned = turn(new[rows, q], cosines[g, at, :], sines[g, at, :], 1.0)
                 queries[g, at, q] = turned.astype(BF) * jnp.asarray(SCALE, BF)
 
+    plane.middle()
+    first_head = lax.broadcasted_iota(jnp.int32, (BLOCK, 1), 0) < HEAD_DIM
+
+    def work(part, g):
+        rows = slice(part * TOKENS, (part + 1) * TOKENS)
+
+        @pl.loop(0, 2)
+        def _(tile):
+            at = pl.ds(pl.multiple_of(tile * TILE, TILE), TILE)
+            bias = key_bias(table, g, tile, range(4 * part, 4 * part + 4))
+            for pair in range(2):
+                q = slice(pair * BLOCK, (pair + 1) * BLOCK)
+                k_all = kv[0, g, rows, q]
+                v_all = kv[1, g, rows, q]
+                out = jnp.zeros((BLOCK, TILE), F32)
+                keep, share = [], []
+                for h in range(2):
+                    row = slice(2 * pair + h, 2 * pair + h + 1)
+                    s = dot(k_all, queries[g, at, q] * head_mask(h), NT) + bias
+                    top = jnp.max(s, axis=0, keepdims=True)
+                    if part == 1:
+                        top = jnp.maximum(top, tops[g, row, at])
+                    p = jnp.exp(s - top)
+                    total = jnp.sum(p, axis=0, keepdims=True)
+                    out = out + dot(v_all * head_mask(h), p.astype(BF), TN)
+                    if part == 0:
+                        tops[g, row, at] = top
+                        totals[g, row, at] = total
+                    else:
+                        keep.append(jnp.exp(tops[g, row, at] - top))
+                        total = total + totals[g, row, at] * keep[h]
+                        lse[g, row, at] = top + jnp.log(total)
+                        share.append(1.0 / total)
+                if part == 0:
+                    mixed[g, q, at] = out
+                else:
+                    out = out + mixed[g, q, at] * jnp.where(first_head, keep[0], keep[1])
+                    out = (out * jnp.where(first_head, share[0], share[1])).T.astype(BF)
+                    for j in range(2):
+                        attended[2 * tile + j, g, :, q] = out[j * BLOCK : (j + 1) * BLOCK]
+
+    for g in range(2):
+        work(0, g)
     gather.share()
     for g in range(2):
         trade[g].wait_recv()
         if g == 1:
             gather.share_far()
-
-        @pl.loop(0, 2)
-        def _(tile, g=g):
-            at = pl.ds(pl.multiple_of(tile * TILE, TILE), TILE)
-            bias = key_bias(table, g, tile)
-            for pair in range(2):
-                q = slice(pair * BLOCK, (pair + 1) * BLOCK)
-                k_all = kv[0, g, :, q]
-                v_all = kv[1, g, :, q]
-                out = jnp.zeros((TILE, BLOCK), F32)
-                for h in range(2):
-                    s = dot(k_all, queries[g, at, q] * head_mask(h), NT) + bias
-                    top = jnp.max(s, axis=0, keepdims=True)
-                    p = jnp.exp(s - top)
-                    total = jnp.sum(p, axis=0, keepdims=True)
-                    w = (p * (1.0 / total)).astype(BF)
-                    lse[g, 2 * pair + h : 2 * pair + h + 1, at] = top + jnp.log(total)
-                    out = out + dot(w, v_all * head_mask(h), TN)
-                for j in range(2):
-                    attended[2 * tile + j, g, :, q] = out[j * BLOCK : (j + 1) * BLOCK].astype(BF)
-
+        work(1, g)
     for one in trade:
         one.wait_send()
     gather.finish()
@@ -528,7 +585,7 @@
 SM = pl.BlockSpec(memory_space=pltpu.SMEM)
 
 
-def attend(table, tokens, weight, shift, grad_out, out_rows, cid):
+def attend(table, tokens, weight, shift, cotangent, out_in, cid):
     return pl.pallas_call(
         kernel_attend,
         out_shape=(
@@ -536,14 +593,22 @@
             jax.ShapeDtypeStruct((2, 2, KEYS, HD), BF),
             jax.ShapeDtypeStruct((2, 8, TOKENS), F32),
             jax.ShapeDtypeStruct((4, 2, BLOCK, HD), BF),
+            jax.ShapeDtypeStruct((BLOCK, D), BF),
             FULL,
             jax.ShapeDtypeStruct((4, 4, 16, D), BF),
         ),
-        in_specs=[SM] + [VM] * 5,
-        out_specs=(VM, VM, VM, VM, ANY, ANY),
+        in_specs=[SM, ANY, ANY, VM, VM, VM],
+        out_specs=(VM, VM, VM, VM, VM, ANY, ANY),
         scratch_shapes=[
+            pltpu.VMEM((16, D), BF),
+            pltpu.VMEM((4, 2, BLOCK, D), BF),
+            pltpu.VMEM((D, 3 * HD), BF),
             pltpu.VMEM((2, TOKENS, BLOCK), F32),
             pltpu.VMEM((2, TOKENS, BLOCK), F32),
+            pltpu.VMEM((2, 8, TOKENS), F32),
+            pltpu.VMEM((2, 8, TOKENS), F32),
+            pltpu.VMEM((2, HD, TOKENS), F32),
+            pltpu.SemaphoreType.DMA((5,)),
             pltpu.SemaphoreType.DMA((2,)),
             pltpu.SemaphoreType.DMA((2,)),
         ]
@@ -551,45 +616,77 @@
         + PG_SEMS,
         compiler_params=params(cid),
         name="attend",
-    )(table, tokens, weight, shift, grad_out, out_rows)
+    )(table, tokens, weight, shift, cotangent, out_in)
 
 
 def kernel_attend_back(
     table,
-    branch,
+    branch_own,
     gathered,
     attended,
     queries,
     kv,
     lse,
     mlp_out,
-    middle,
+    middle_hbm,
     joined_grad,
     out_part,
     hidden_out,
+    branch,
+    middle,
+    own_out,
+    probs,
+    local,
     weight,
     grads,
     dq,
+    mean,
     dkv,
     kv_out,
     kv_in,
     send,
     recv,
+    local_sem,
+    gather_send,
+    gather_recv,
     *scratch,
 ):
     partner = {"zh": 1 - lax.axis_index("zh")}
     y0, c, up, opp, dn = ring()
+    order = (opp, up, dn, y0)
+    out_in = load([(mlp_out.at[order[j], c], own_out.at[j]) for j in range(4)], local)
+    (middle_in,) = load([(middle_hbm, middle)], local, 4)
     meet(list(ring_peers(up, dn, c)) + [partner])
+    gather = RingGather(branch_own, branch, local_sem, (gather_send, gather_recv))
+    gather.start()
     sems = (send, recv)
-    order = (opp, up, dn, y0)
     scatter = RingScatter(
-        lambda j, rows: mlp_out[order[j], c, rows, :].astype(F32),
+        lambda j, rows: own_out[j, rows, :].astype(F32),
         lambda j: mlp_out.at[order[j], 1 - c],
         *scratch,
     )
     for one in scatter.sib:
         one.start()
     order_out(gathered, weight)
+
+    def recompute(g):
+        @pl.loop(0, 2)
+        def _(tile):
+            at = pl.ds(pl.multiple_of(tile * TILE, TILE), TILE)
+            bias = key_bias(table, g, tile, range(8))
+            for pair in range(2):
+                q = slice(pair * BLOCK, (pair + 1) * BLOCK)
+                for h in range(2):
+                    row = slice(2 * pair + h, 2 * pair + h + 1)
+                    s = dot(kv[0, g, :, q], queries[g, at, q] * head_mask(h), NT) + bias
+                    probs[g, tile, 2 * pair + h] = jnp.exp(s - lse[g, row, at])
+
+    recompute(0)
+    gather.forward()
+    recompute(1)
+    gather.share()
+    gather.share_far()
+    gather.finish()
 
     @pl.loop(0, 4)
     def _(y):
@@ -598,52 +695,58 @@
         for g in range(2):
             grads[g, at, :] = new[g * BLOCK : (g + 1) * BLOCK].astype(BF)
 
+    for one in out_in:
+        one.wait()
     scatter.send_far()
     scatter.send_early(0)
     scatter.send_early(1)
     trade = [remote(sems, g, kv_out.at[g], kv_in.at[g], partner) for g in range(2)]
-    own, other = pl.ds(0, TOKENS), pl.ds(TOKENS, TOKENS)
-    for g in range(2):
+    dq[...] = jnp.zeros_like(dq)
+    dkv[...] = jnp.zeros_like(dkv)
+    heads = jnp.concatenate([head_mask(0), head_mask(1)] * 4, axis=0).astype(F32)
+
+    def back(part, g):
+        rows = slice(part * TOKENS, (part + 1) * TOKENS)
 
         @pl.loop(0, 2)
-        def _(tile, g=g):
+        def _(tile):
             at = pl.ds(pl.multiple_of(tile * TILE, TILE), TILE)
-            bias = key_bias(table, g, tile)
             for pair in range(2):
                 q = slice(pair * BLOCK, (pair + 1) * BLOCK)
-                k_all = kv[0, g, :, q]
-                v_all = kv[1, g, :, q]
-                new_q = jnp.zeros((TILE, BLOCK), F32)
-                new_k = jnp.zeros((KEYS, BLOCK), F32)
-                new_v = jnp.zeros((KEYS, BLOCK), F32)
+                both = slice(2 * pair, 2 * pair + 2)
+                if part == 1:
+                    mixed = attended[pl.ds(2 * tile, 2), g, :, q].reshape(TILE, BLOCK).astype(F32)
+                    mixed = mixed * grads[g, at, q].astype(F32)
+                    mean[g, both, at] = lax.dot_general(
+                        heads, mixed, NT, precision=lax.Precision.HIGHEST
+                    )[0:2]
+                k_all = kv[0, g, rows, q]
+                v_all = kv[1, g, rows, q]
+                new_q = jnp.zeros((BLOCK, TILE), F32)
+                new_k = jnp.zeros((TOKENS, BLOCK), F32)
+                new_v = jnp.zeros((TOKENS, BLOCK), F32)
                 for h in range(2):
+                    row = slice(2 * pair + h, 2 * pair + h + 1)
                     q_head = queries[g, at, q] * head_mask(h)
                     g_head = grads[g, at, q] * head_mask(h)
-                    s = dot(k_all, q_head, NT) + bias
-                    p = jnp.exp(s - lse[g, 2 * pair + h : 2 * pair + h + 1, at])
+                    p = probs[g, tile, 2 * pair + h, rows, :]
                     p_grad = dot(v_all, g_head, NT)
-                    mean = jnp.sum(p * p_grad, axis=0, keepdims=True)
-                    s_grad = (p * (p_grad - mean)).astype(BF)
+                    s_grad = (p * (p_grad - mean[g, row, at])).astype(BF)
                     new_v = new_v + dot(p.astype(BF), g_head, NN)
                     new_k = new_k + dot(s_grad, q_head, NN)
-                    new_q = new_q + dot(s_grad, k_all * head_mask(h), TN)
-                dq[g, at, q] = new_q * SCALE
-
-                @pl.when(tile == 0)
-                def _():
-                    dkv[0, g, :, q] = new_k
-                    dkv[1, g, :, q] = new_v
-
-                @pl.when(tile != 0)
-                def _():
-                    dkv[0, g, :, q] += new_k
-                    dkv[1, g, :, q] += new_v
-
+                    new_q = new_q + dot(k_all * head_mask(h), s_grad, TN)
+                dq[g, q, at] += new_q
+                dkv[0, g, rows, q] += new_k
+                dkv[1, g, rows, q] += new_v
+
+    for g in range(2):
+        back(1, g)
         for i in range(2):
-            kv_out[g, i] = dkv[i, g, other, :].astype(BF)
+            kv_out[g, i] = dkv[i, g, pl.ds(TOKENS, TOKENS), :].astype(BF)
         trade[g].start()
-        if g == 0:
-            scatter.send_late()
+    scatter.send_late()
+    for g in range(2):
+        back(0, g)
 
     @pl.loop(0, 8)
     def _(i):
@@ -656,11 +759,12 @@
                     out_part[x * 4 + a * 2 + zl, :, q] = new[row : row + 16].astype(BF)
 
     scatter.wait()
+    middle_in.wait()
 
     def add(r):
-        hidden_out[r, :] = (middle[r, :] + scatter.total(r)).astype(BF)
-
-    rows_loop(BLOCK, 32, add)
+        hidden_out[r, :] = restore_rows(middle[r, :] + scatter.total(r)).astype(BF)
+
+    rows_loop(BLOCK, 16, add)
     for g in range(2):
         trade[g].wait_recv()
 
@@ -670,7 +774,8 @@
             cosine, sine = turn_tables(table[g, 0, y])
             for pair in range(2):
                 q = slice(pair * BLOCK, (pair + 1) * BLOCK)
-                joined_grad[y, g, :, q] = turn(dq[g, at, q], cosine, sine, -1.0).astype(BF)
+                new = dq[g, q, at].T * SCALE
+                joined_grad[y, g, :, q] = turn(new, cosine, sine, -1.0).astype(BF)
                 new = dkv[0, g, at, q] + kv_in[g, 0, at, q].astype(F32)
                 joined_grad[y, g, :, HD + pair * BLOCK : HD + (pair + 1) * BLOCK] = turn(
                     new, cosine, sine, -1.0
@@ -692,18 +797,25 @@
             jax.ShapeDtypeStruct((16, 16, D), BF),
             jax.ShapeDtypeStruct((BLOCK, D), BF),
         ),
-        in_specs=[SM] + [VM] * 8,
+        in_specs=[SM] + [VM] * 6 + [ANY, ANY],
         out_specs=(VM, VM, VM),
         scratch_shapes=[
+            pltpu.VMEM((4, 2, BLOCK, D), BF),
+            pltpu.VMEM((BLOCK, D), F32),
+            pltpu.VMEM((4, BLOCK, D), BF),
+            pltpu.VMEM((2, 2, 4, KEYS, TILE), F32),
+            pltpu.SemaphoreType.DMA((5,)),
             OUT_ROWS,
             pltpu.VMEM((2, TOKENS, HD), BF),
-            pltpu.VMEM((2, TOKENS, HD), F32),
+            pltpu.VMEM((2, HD, TOKENS), F32),
+            pltpu.VMEM((2, 8, TOKENS), F32),
             pltpu.VMEM((2, 2, KEYS, HD), F32),
             pltpu.VMEM((2, 2, TOKENS, HD), BF),
             pltpu.VMEM((2, 2, TOKENS, HD), BF),
             pltpu.SemaphoreType.DMA((2,)),
             pltpu.SemaphoreType.DMA((2,)),
         ]
+        + AG_SCRATCH[1:]
         + RS_SCRATCH[2:],
         compiler_params=params(cid),
         name="attend_back",
@@ -711,57 +823,97 @@
 
 
 def kernel_mlp(
-    two,
-    grad_all,
-    w,
+    two_hbm,
+    grad_hbm,
+    w_hbm,
     middle,
     grad_out,
     gains,
     middle_grad,
     sums,
+    own,
+    out_hbm,
+    part_hbm,
+    two,
+    grad_all,
+    w,
     out_part,
     mlp_part,
-    full,
     inner,
-    gate_grad,
-    up_grad,
+    both_grads,
+    local,
+    leave,
     *scratch,
 ):
-    own, local_sem, *sems = scratch[:4]
     y, c, up, opp, dn = ring()
+    order = (opp, up, dn, y)
+    w_in = load([(w_hbm.at[:, k], w.at[k]) for k in range(3)], local)
+    block_in = load(
+        [(src.at[b], dst.at[b]) for b in order for src, dst in ((two_hbm, two), (grad_hbm, grad_all))],
+        local,
+        3,
+    )
     meet(ring_peers(up, dn, c))
-
     held = jnp.logical_or(lane(FP) >= BLOCK, y < 2)
+    gate_lanes, up_lanes = pl.ds(0, FP), pl.ds(FP, FP)
+    waits = [w_in + block_in[0:2], block_in[2:4], block_in[4:6], block_in[6:8]]
+    outs = []
 
     def partial(block, put):
+        for one in waits[len(outs)]:
+            one.wait()
         a = two[block].reshape(TILE, D)
-        gate = dot(a, w[:, 0].reshape(D, FP), NN)
-        up_proj = dot(a, w[:, 1].reshape(D, FP), NN)
-        grad = dot(grad_all[block].reshape(TILE, D), w[:, 2].reshape(D, FP), NN)
+        gate = dot(a, w[0].reshape(D, FP), NN)
+        up_proj = dot(a, w[1].reshape(D, FP), NN)
+        grad = dot(grad_all[block].reshape(TILE, D), w[2].reshape(D, FP), NN)
         sig = 1.0 / (1.0 + jnp.exp(-gate))
         active = gate * sig
         low = (active * up_proj).astype(BF)
         low_gate = (grad * up_proj * sig * (1.0 + gate * (1.0 - sig))).astype(BF)
         low_up = (grad * active).astype(BF)
-        for ref, value in ((inner, low), (gate_grad, low_gate), (up_grad, low_up)):
-            ref[block] = jnp.where(held, value, jnp.zeros((), BF)).reshape(2, BLOCK, FP)
-
-        @pl.loop(0, 4)
+        zero = jnp.zeros((), BF)
+        inner[block] = jnp.where(held, low, zero).reshape(2, BLOCK, FP)
+        both_grads[block, :, :, gate_lanes] = jnp.where(held, low_gate, zero).reshape(2, BLOCK, FP)
+        both_grads[block, :, :, up_lanes] = jnp.where(held, low_up, zero).reshape(2, BLOCK, FP)
+
+        low_gate = both_grads[block, :, :, gate_lanes].reshape(TILE, FP)
+        low_up = both_grads[block, :, :, up_lanes].reshape(TILE, FP)
+        for i in range(4):
+            q, wide = slice(i * 512, (i + 1) * 512), slice(i * 4, (i + 1) * 4)
+            new = dot(low_gate, w[0, wide].reshape(512, FP), NT)
+            new = new + dot(low_up, w[1, wide].reshape(512, FP), NT)
+            put(q, new.reshape(2, BLOCK, 512))
+        low = inner[block].reshape(TILE, FP)
+        for i in range(4):
+            q, wide = slice(i * 512, (i + 1) * 512), slice(i * 4, (i + 1) * 4)
+            new = dot(low, w[2, wide].reshape(512, FP), NT)
+            out_part[block, :, :, q] = new.astype(BF).reshape(2, BLOCK, 512)
+
+        outs.extend(load([(out_part.at[block], out_hbm.at[block])], leave, len(outs)))
+
+    done = []
+
+    def weight_grads(count=1):
+        begin = len(done)
+
+        @pl.loop(begin, begin + count)
         def _(i):
-            q = pl.ds(pl.multiple_of(i * 512, 512), 512)
-            wide = pl.ds(i * 4, 4)
-            new = dot(gate_grad[block].reshape(TILE, FP), w[wide, 0].reshape(512, FP), NT)
-            new = new + dot(up_grad[block].reshape(TILE, FP), w[wide, 1].reshape(512, FP), NT)
-            put(q, new.reshape(2, BLOCK, 512))
-
-        @pl.loop(0, 4)
-        def _(i):
-            q = pl.ds(pl.multiple_of(i * 512, 512), 512)
-            wide = pl.ds(i * 4, 4)
-            new = dot(inner[block].reshape(TILE, FP), w[wide, 2].reshape(512, FP), NT)
-            out_part[block, :, :, q] = new.astype(BF).reshape(2, BLOCK, 512)
-
-    scatter = ring_scatter(partial, scratch[4:])
+            q = pl.ds(pl.multiple_of(i * TILE, TILE), TILE)
+            a = two[:, :, :, q].reshape(TP * BLOCK, TILE)
+            b = grad_all[:, :, :, q].reshape(TP * BLOCK, TILE)
+            new = dot(a, both_grads[...].reshape(TP * BLOCK, 2 * FP), TN).astype(BF)
+            at = pl.ds(2 * i, 2)
+            mlp_part[at, 0] = new[:, :FP].reshape(2, BLOCK, FP)
+            mlp_part[at, 1] = new[:, FP:].reshape(2, BLOCK, FP)
+            new = dot(b, inner[...].reshape(TP * BLOCK, FP), TN).astype(BF)
+            mlp_part[at, 2] = new.reshape(2, BLOCK, FP)
+
+        for i in range(begin, begin + count):
+            done.extend(
+                load([(mlp_part.at[pl.ds(2 * i, 2)], part_hbm.at[pl.ds(2 * i, 2)])], leave, 4 + i)
+            )
+
+    scatter = ring_scatter(partial, scratch, lambda: weight_grads(8))
     sums[...] = jnp.zeros_like(sums)
 
     def back(r):
@@ -774,38 +926,36 @@
         sums[1:2, :] += jnp.sum(row, axis=0, keepdims=True)
 
     rows_loop(BLOCK, 16, back)
-    done = []
-
-    def weight_grads():
-        begin = 2 * len(done)
-        done.append(begin)
-
-        @pl.loop(begin, begin + 2)
-        def _(i):
-            q = pl.ds(pl.multiple_of(i * TILE, TILE), TILE)
-            a = two[:, :, :, q].reshape(TP * BLOCK, TILE)
-            b = grad_all[:, :, :, q].reshape(TP * BLOCK, TILE)
-            for k, (left, right) in enumerate(((a, gate_grad), (a, up_grad), (b, inner))):
-                new = dot(left, right[...].reshape(TP * BLOCK, FP), TN).astype(BF)
-                mlp_part[pl.ds(2 * i, 2), k] = new.reshape(2, BLOCK, FP)
-
-    RingGather(own, full, local_sem, sems).run(weight_grads)
     scatter.finish()
+    for one in outs + done:
+        one.wait()
 
 
 def mlp(two, grad_all, w, middle, grad_out, gains, cid):
+    block = (4, 2, BLOCK, D)
     return pl.pallas_call(
         kernel_mlp,
         out_shape=(
             jax.ShapeDtypeStruct((BLOCK, D), F32),
             jax.ShapeDtypeStruct((8, D), F32),
+            jax.ShapeDtypeStruct((BLOCK, D), BF),
             FULL,
             jax.ShapeDtypeStruct((16, 3, BLOCK, FP), BF),
-            FULL,
         ),
-        in_specs=[VM] * 6,
-        out_specs=(VM, VM, VM, VM, ANY),
-        scratch_shapes=[pltpu.VMEM((4, 2, BLOCK, FP), BF)] * 3 + AG_SCRATCH + RS_SCRATCH,
+        in_specs=[ANY] * 3 + [VM] * 3,
+        out_specs=(VM, VM, VM, ANY, ANY),
+        scratch_shapes=[
+            pltpu.VMEM(block, BF),
+            pltpu.VMEM(block, BF),
+            pltpu.VMEM((3, 16, BLOCK, FP), BF),
+            pltpu.VMEM(block, BF),
+            pltpu.VMEM((16, 3, BLOCK, FP), BF),
+            pltpu.VMEM((4, 2, BLOCK, FP), BF),
+            pltpu.VMEM((4, 2, BLOCK, 2 * FP), BF),
+            pltpu.SemaphoreType.DMA((11,)),
+            pltpu.SemaphoreType.DMA((12,)),
+        ]
+        + RS_SCRATCH,
         compiler_params=params(cid),
         name="mlp",
     )(two, grad_all, w, middle, grad_out, gains)
@@ -896,42 +1046,48 @@
 
 def kernel_qkv_back(
     joined_grad,
-    weight,
+    weight_hbm,
     hidden,
-    middle_grad,
+    middle_hbm,
     gains,
-    tokens,
+    tokens_hbm,
     out_part,
     input_grad,
     sums,
     shift_sum,
     qkv_sum,
     out_sum,
+    tokens,
+    weight,
+    middle_grad,
+    local,
     part,
     *scratch,
 ):
+    token_in = load([(tokens_hbm.at[y], tokens.at[y]) for y in range(4)], local)
+    weight_in, middle_in = load([(weight_hbm, weight), (middle_hbm, middle_grad)], local, 4)
     y, c, up, opp, dn = ring()
     meet(list(ring_peers(up, dn, c)) + plane_peers())
     out_scatter = PlaneScatter(out_part, *scratch[:8])
     qkv_scatter = PlaneScatter(part, *scratch[8:16])
     out_scatter.start()
     flat = joined_grad[...].reshape(TP * BLOCK, 3 * HD)
-
-    @pl.loop(0, 8)
-    def _(i):
-        q = pl.ds(pl.multiple_of(i * TILE, TILE), TILE)
-        new = dot(tokens[:, :, :, q].reshape(TP * BLOCK, TILE), flat, TN).astype(BF)
-        part[i // 2, 2 * lax.rem(i, 2)] = new[:BLOCK]
-        part[i // 2, 2 * lax.rem(i, 2) + 1] = new[BLOCK:]
+    for one in token_in:
+        one.wait()
+
+    for i in range(4):
+        q = slice(i * 512, (i + 1) * 512)
+        new = dot(tokens[:, :, :, q].reshape(TP * BLOCK, 512), flat, TN).astype(BF)
+        part[i] = new.reshape(4, BLOCK, 3 * HD)
 
     qkv_scatter.start()
+    weight_in.wait()
+    middle_in.wait()
 
     def partial(block, put):
         a = joined_grad[block].reshape(2 * BLOCK, 3 * HD)
-
-        @pl.loop(0, 4)
-        def _(i):
-            q = pl.ds(pl.multiple_of(i * 512, 512), 512)
+        for i in range(4):
+            q = slice(i * 512, (i + 1) * 512)
             put(q, dot(a, weight[q, :], NT).reshape(2, BLOCK, 512))
 
     def between():
@@ -947,7 +1103,9 @@
     def back(r):
         row = scatter.total(r)
         normed, inv = layer_norm(hidden[r, :].astype(F32))
-        input_grad[r, :] = middle_grad[r, :] + norm_back(row, normed, inv, gains[0:1, :])
+        input_grad[r, :] = restore_rows(
+            middle_grad[r, :] + norm_back(row, normed, inv, gains[0:1, :])
+        )
         sums[0:1, :] += jnp.sum(row * normed, axis=0, keepdims=True)
         sums[1:2, :] += jnp.sum(row, axis=0, keepdims=True)
 
@@ -967,9 +1125,15 @@
             jax.ShapeDtypeStruct((BLOCK, 3 * HD), BF),
             jax.ShapeDtypeStruct((16, D), BF),
         ),
-        in_specs=[VM] * 7,
+        in_specs=[VM, ANY, VM, ANY, VM, ANY, VM],
         out_specs=(VM,) * 5,
-        scratch_shapes=[pltpu.VMEM((4, 4, BLOCK, 3 * HD), BF)]
+        scratch_shapes=[
+            pltpu.VMEM((4, 2, BLOCK, D), BF),
+            pltpu.VMEM((D, 3 * HD), BF),
+            pltpu.VMEM((BLOCK, D), F32),
+            pltpu.SemaphoreType.DMA((6,)),
+            pltpu.VMEM((4, 4, BLOCK, 3 * HD), BF),
+        ]
         + plane_scratch(16, D)
         + plane_scratch(BLOCK, 3 * HD)
         + RS_SCRATCH,
@@ -1127,7 +1291,7 @@
 
 def kernel_front(
     small,
-    hidden,
+    hidden_in,
     w_qkv,
     w_gate,
     w_up,
@@ -1139,6 +1303,7 @@
     qkv_full,
     mlp_rows,
     out_rows,
+    hidden,
     full,
     own,
     qkv_rows,
@@ -1195,7 +1360,9 @@
     spread_gains(small_all, gains, shift, me)
 
     def norm(r):
-        normed, _ = layer_norm(hidden[r, :].astype(F32))
+        row = permute_rows(hidden_in[r, :].astype(F32))
+        hidden[r, :] = row.astype(BF)
+        normed, _ = layer_norm(row)
         own[r, :] = (normed * gains[0:1, :] + gains[1:2, :]).astype(BF)
 
     rows_loop(BLOCK, 16, norm)
@@ -1223,10 +1390,11 @@
             jax.ShapeDtypeStruct((4, 4, TP, 16, 3 * HD), BF),
             jax.ShapeDtypeStruct((3, TP, 16, FP), BF),
             jax.ShapeDtypeStruct((16, D), BF),
+            jax.ShapeDtypeStruct((BLOCK, D), BF),
             FULL,
         ),
         in_specs=[ANY, VM] + [ANY] * 5,
-        out_specs=(VM, VM, VM, ANY, ANY, ANY, ANY),
+        out_specs=(VM, VM, VM, ANY, ANY, ANY, VM, ANY),
         scratch_shapes=[
             pltpu.VMEM((BLOCK, D), BF),
             pltpu.VMEM((TP, 16, 3 * HD), BF),
@@ -1256,8 +1424,6 @@
     out_grad,
     terms,
     terms_in,
-    shift_own,
-    shift_in,
     own,
     small_all,
     qkv_all,
@@ -1269,43 +1435,37 @@
     me = lax.axis_index("y") * 2 + lax.axis_index("core")
     xz = lax.axis_index("x") * 4 + lax.axis_index("zh") * 2 + lax.axis_index("zl")
     split = lax.axis_index("zh") != lax.axis_index("core")
+    for p in range(16):
+        q = slice(p * BLOCK, (p + 1) * BLOCK)
+        terms[p, 0:2, :] = one_sums[0:2, q]
+        terms[p, 2:4, :] = two_sums[0:2, q]
+        for i in range(6):
+            terms[p, 8 + i : 9 + i, :] = shift[0:1, i * BLOCK : (i + 1) * BLOCK]
+        for i in (4, 5, 6, 7, 14, 15):
+            terms[p, i : i + 1, :] = jnp.zeros((1, BLOCK), F32)
     meet_all(split)
     cp = functools.partial(remote, sems)
-    big, extra = [], []
+    big, extra, wide = [], [], []
     near, tile = pl.ds(BLOCK, FP - BLOCK), pl.ds(0, BLOCK)
-    base = 2 * N_XZ + N_TP
+    base = N_XZ + N_TP
     for k, step in enumerate(TP_STEPS):
         peer, there = tp_peer(step)
         dst = mlp_all.at[:, :, lanes_at(first_lane(me) + BLOCK, FP - BLOCK)]
         big.append(cp(base + k, mlp.at[:, there, :, near], dst, peer))
         dst = mlp_all.at[:, :, lanes_at(first_lane(me), BLOCK)]
         extra.append(cp(base + N_TP + k, mlp.at[:, there, :, tile], dst, peer))
-        for i in range(3):
-            dst = qkv_all.at[:, lanes_at(head_lane(i, me), HD)]
-            big.append(cp(base + (2 + i) * N_TP + k, qkv.at[there, :, pl.ds(i * HD, HD)], dst, peer))
-    keep = []
-    dst = mlp_all.at[:, :, lanes_at(first_lane(me) + BLOCK, FP - BLOCK)]
-    keep.append(pltpu.make_async_copy(mlp.at[:, me, :, near], dst, local.at[0]))
-    for i in range(3):
-        dst = qkv_all.at[:, lanes_at(head_lane(i, me), HD)]
-        keep.append(pltpu.make_async_copy(qkv.at[me, :, pl.ds(i * HD, HD)], dst, local.at[1 + i]))
-    dst = mlp_all.at[:, :, lanes_at(first_lane(me), BLOCK)]
-    keep_tile = pltpu.make_async_copy(mlp.at[:, me, :, tile], dst, local.at[4])
-    first_four = me < 4
-
-    terms[...] = jnp.zeros_like(terms)
-    shift_own[...] = jnp.zeros_like(shift_own)
-    for p in range(16):
-        q = slice(p * BLOCK, (p + 1) * BLOCK)
-        terms[p, 0:2, :] = one_sums[0:2, q]
-        terms[p, 2:4, :] = two_sums[0:2, q]
-    for i in range(6):
-        shift_own[i : i + 1, :] = shift[0:1, i * BLOCK : (i + 1) * BLOCK]
-    wide = []
+        big.append(cp(base + 2 * N_TP + k, qkv.at[there], qkv_all.at[me], peer))
     for k, step in enumerate(XZ_STEPS):
         peer, there = xz_peer(step)
         wide.append(cp(k, terms.at[there], terms_in.at[xz], peer))
-        wide.append(cp(N_XZ + k, shift_own, shift_in.at[xz], peer))
+    dst = mlp_all.at[:, :, lanes_at(first_lane(me) + BLOCK, FP - BLOCK)]
+    keep = [
+        pltpu.make_async_copy(mlp.at[:, me, :, near], dst, local.at[0]),
+        pltpu.make_async_copy(qkv.at[me], qkv_all.at[me], local.at[1]),
+    ]
+    dst = mlp_all.at[:, :, lanes_at(first_lane(me), BLOCK)]
+    keep_tile = pltpu.make_async_copy(mlp.at[:, me, :, tile], dst, local.at[2])
+    first_four = me < 4
     for one in wide + big + keep:
         one.start()
 
@@ -1315,23 +1475,19 @@
         for one in extra:
             one.start()
 
-    last = base + 5 * N_TP
-    swap_start(split, out, out_all, local.at[5], sems, last)
+    last = base + 3 * N_TP
+    swap_start(split, out, out_all, local.at[3], sems, last)
     for one in wide:
         one.wait()
     terms_in[xz] = terms[xz]
-    shift_in[xz] = shift_own[...]
-    own[0:8, :] = jnp.sum(terms_in[...], axis=0)
-    own[8:16, :] = jnp.sum(shift_in[...], axis=0)
+    own[...] = jnp.sum(terms_in[...], axis=0)
     tiny = []
     for k, step in enumerate(TP_STEPS):
         peer, _ = tp_peer(step)
-        tiny.append(cp(2 * N_XZ + k, own, small_all.at[me], peer))
+        tiny.append(cp(N_XZ + k, own, small_all.at[me], peer))
     for one in tiny:
         one.start()
-    for one in big:
-        one.wait()
-    for one in keep:
+    for one in big + keep:
         one.wait()
     for k, step in enumerate(TP_STEPS):
         source = lax.rem(lax.axis_index("y") + 4 - step[0], 4) * 2 + lax.rem(
@@ -1348,12 +1504,15 @@
         for one in extra:
             one.wait_send()
 
-    qkv_grad[...] = qkv_all[...].astype(F32)
+    for t in range(TP):
+        for i in range(3):
+            first = i * D + (t % 2 * 4 + t // 2) * HD
+            qkv_grad[:, first : first + HD] = qkv_all[t, :, i * HD : (i + 1) * HD].astype(F32)
     gate_grad[...] = mlp_all[0].astype(F32)
     up_grad[...] = mlp_all[1].astype(F32)
     down_grad[...] = mlp_all[2].astype(F32)
-    swap_wait(split, out, out_all, local.at[5], sems, last)
-    out_grad[...] = out_all[...].astype(F32)
+    swap_wait(split, out, out_all, local.at[3], sems, last)
+    out_grad[...] = restore_rows(out_all[...].astype(F32))
     for one in tiny:
         one.wait()
     small_all[me] = own[...]
@@ -1361,7 +1520,7 @@
 
 
 def collect(one_sums, two_sums, shift, qkv, mlp, out, cid):
-    n = 2 * N_XZ + 6 * N_TP + 1
+    n = N_XZ + 4 * N_TP + 1
     wide = jax.ShapeDtypeStruct((16, FF), F32)
     return pl.pallas_call(
         kernel_collect,
@@ -1376,16 +1535,14 @@
         in_specs=[VM] * 3 + [ANY] * 3,
         out_specs=(VM,) * 6,
         scratch_shapes=[
-            pltpu.VMEM((16, 8, BLOCK), F32),
-            pltpu.VMEM((16, 8, BLOCK), F32),
-            pltpu.VMEM((8, BLOCK), F32),
-            pltpu.VMEM((16, 8, BLOCK), F32),
+            pltpu.VMEM((16, 16, BLOCK), F32),
+            pltpu.VMEM((16, 16, BLOCK), F32),
             pltpu.VMEM((16, BLOCK), F32),
             pltpu.VMEM((TP, 16, BLOCK), F32),
-            pltpu.VMEM((16, 3 * D), BF),
+            pltpu.VMEM((TP, 16, 3 * HD), BF),
             pltpu.VMEM((3, 16, FF), BF),
             pltpu.VMEM((16, D), BF),
-            pltpu.SemaphoreType.DMA((6,)),
+            pltpu.SemaphoreType.DMA((4,)),
             pltpu.SemaphoreType.DMA((n,)),
             pltpu.SemaphoreType.DMA((n,)),
         ],
@@ -1410,32 +1567,23 @@
     w_up,
     w_down,
 ):
-    bf, f32 = BF, F32
+    f32 = F32
     zh = lax.axis_index("zh")
     y = lax.axis_index("y")
     core = lax.axis_index("core")
     xz = lax.axis_index("x") * 4 + zh * 2 + lax.axis_index("zl")
 
-    lengths = seq_lengths[0]
-    small = jnp.concatenate(
-        [
-            ln1_gain.astype(f32),
-            ln1_bias.astype(f32),
-            ln2_gain.astype(f32),
-            ln2_bias.astype(f32),
-            qkv_bias.astype(f32),
-            lengths.astype(f32),
-            slot_block[0].astype(f32),
-            jnp.zeros(6, f32),
-        ]
-    ).reshape(1, BLOCK)
-    hidden = permute_features(hidden_in[0])
-    small_all, gains, shift, qkv_full, mlp_rows, out_rows, one_all = front(
-        small, hidden, w_qkv, w_gate, w_up, w_down, w_out, 0
+    small, first = jnp.zeros(BLOCK, f32), 0
+    pieces = (ln1_gain, ln1_bias, ln2_gain, ln2_bias, qkv_bias, seq_lengths[0], slot_block[0])
+    for piece in pieces:
+        n = piece.shape[0]
+        small = small + jnp.pad(piece.astype(f32), (first, BLOCK - first - n))
+        first += n
+    small_all, gains, shift, qkv_full, mlp_rows, out_rows, hidden, one_all = front(
+        small.reshape(1, BLOCK), hidden_in[0], w_qkv, w_gate, w_up, w_down, w_out, 0
     )
     qkv_full = qkv_full.reshape(D, 3 * HD)
     mlp_full = lax.all_gather(mlp_rows.reshape(3, BLOCK, FP), XZ, axis=0, tiled=False)
-    out_rows = permute_features(out_rows)
     small_all = small_all.reshape(BLOCK, BLOCK)
 
     plan = lax.dynamic_slice_in_dim(small_all, xz * TP + y * 2, 2, 0)[:, 112:122].astype(jnp.int32)
@@ -1447,24 +1595,18 @@
     second = (start >= first_pad).astype(jnp.int32)
     limit = jnp.where(second == 1, plan[:, 1:2], plan[:, 0:1])
     table = jnp.stack([start - second * first_pad, second, limit], axis=1)
-    place = (zh * 4 + y) * BLOCK
-    _, _, slot_valid = block_places(lengths, slot_block[0])
-    own_valid = lax.dynamic_slice_in_dim(slot_valid, place, BLOCK, 0)
-
-    grad_out = permute_features(cotangent[0]) * own_valid[:, None].astype(bf)
-
-    queries, kv, lse, attended, grad_all, out_full = attend(
-        table, one_all, qkv_full, shift, grad_out, out_rows, 6
+    queries, kv, lse, attended, grad_out, grad_all, out_full = attend(
+        table, one_all, qkv_full, shift, cotangent[0], out_rows, 6
     )
     middle, two_all = out_proj(attended, out_full, hidden, gains, 2)
-    middle_grad, two_sums, mlp_out, mlp_part, branch_all = mlp(
+    middle_grad, two_sums, branch, mlp_out, mlp_part = mlp(
         two_all, grad_all, mlp_full, middle, grad_out, gains, 3
     )
     mlp_sum = lax.psum_scatter(
         mlp_part.reshape(16 * 3 * BLOCK, FP), XZ, scatter_dimension=0, tiled=True
     )
     joined_grad, out_part, hidden_out = attend_back(
-        table, branch_all, out_full, attended, queries, kv, lse, mlp_out, middle, 7
+        table, branch, out_full, attended, queries, kv, lse, mlp_out, middle, 7
     )
     input_grad, one_sums, shift_sum, qkv_sum, out_sum = qkv_back(
         joined_grad, qkv_full, hidden, middle_grad, gains, one_all, out_part, 4
@@ -1485,13 +1627,13 @@
     row = (zh * 4 + y) * 16 + lax.axis_index("x") * 4 + lax.axis_index("zl") * 2 + core
     shift_grad = lax.dynamic_index_in_dim(shift_grad, row, 0, False)
     return (
-        restore_features(hidden_out)[None],
-        restore_features(input_grad)[None],
+        hidden_out[None],
+        input_grad[None],
         vectors[0],
         vectors[1],
         qkv_grad,
         shift_grad,
-        restore_features(out_grad),
+        out_grad,
         vectors[2],
         vectors[3],
         gate_sum,

time: 403 us -> 371 us (0.921)
  Pallas kernels: 352 us -> 337 us
  local copies, waits for them, and re-layouts: 25.7 us -> 10.8 us
    pallas_call x1, Pallas kernels: 74.1 us -> 48.9 us  [mlp(): pl.pallas_call(kernel_mlp, out_shape=(jax.ShapeDtypeStruct((BLOCK, D), F3...]
    pallas_call x1, Pallas kernels: 69.1 us -> 78.7 us  [attend_back(): pl.pallas_call(kernel_attend_back, out_shape=(jax.ShapeDtypeStruct((4, 2,...]
    reshape x7 -> x0, local copies, waits for them, and re-layouts: 5.79 us -> none  [the longest x3 2.14 us: permute_features(): return v.reshape(lead + (D,))]
    unnamed x19 -> x20, local copies, waits for them, and re-layouts: 9.18 us -> 8.02 us
  transfers between devices with their start and end apart: 2 -> 2, of which waited for: 0 -> 0; matrix products, arithmetic and copies ran while one was open for 3% -> 1% of each run, Pallas kernels for 54% -> 61%
where the time goes in v1:
time: 371 us; the launch traced here: 367 us
  Pallas kernels  337 us (91%)
  between operations  14.4 us (4%)
  local copies, waits for them, and re-layouts  10.8 us (3%)
  other arithmetic  4.27 us (1%)
    pallas_call x1, Pallas kernels, attend_back(): pl.pallas_call(kernel_attend_back, out_shape=(jax.ShapeDtypeStruct((4, 2,...  78.7 us
    pallas_call x1, Pallas kernels, out_proj(): pl.pallas_call(kernel_out_proj, out_shape=(jax.ShapeDtypeStruct((BLOCK, D...  51.2 us
    pallas_call x1, Pallas kernels, attend(): pl.pallas_call(kernel_attend, out_shape=(jax.ShapeDtypeStruct((2, TOKENS,...  49.2 us
    pallas_call x1, Pallas kernels, mlp(): pl.pallas_call(kernel_mlp, out_shape=(jax.ShapeDtypeStruct((BLOCK, D), F3...  48.9 us
    pallas_call x1, Pallas kernels, qkv_back(): pl.pallas_call(kernel_qkv_back, out_shape=(jax.ShapeDtypeStruct((BLOCK, D...  45.7 us
    pallas_call x1, Pallas kernels, front(): pl.pallas_call(kernel_front, out_shape=(jax.ShapeDtypeStruct((16, TP, 1,...  45 us
    pallas_call x1, Pallas kernels, collect(): pl.pallas_call(kernel_collect, out_shape=(jax.ShapeDtypeStruct((TP, 16, B...  18.6 us
    unnamed x20, local copies, waits for them, and re-layouts  8.02 us
  transfers between devices with their start and end apart: 2, of which 0 were waited for; matrix products, arithmetic and copies ran while one was open for 1% of the time, Pallas kernels for 61%

profile of v1, /device:TPU:1, one launch (start us, length us, event | category | flops | bytes accessed | tf_op | source)
XLA Modules:
  0.0 367.4 jit_solution(17704258034122136120)
XLA Ops:
  7.2 0.7 convert_bitcast_fusion.1
  7.9 0.7 convert_bitcast_fusion
  8.5 1.3 add_bitcast_fusion.small
  9.8 45.0 %front.1 = (f32[16,8,1,128]{3,2,1,0:T(1,128)}, f32[8,2048]{1,0:T(8,128)}, f32[1,768]{1,0:T(1,128)}, bf16[4,4,8,16,768]{4,3,2,1,0:T(8,128)(2,1)}, bf16[3,8,16,768...) custom-call(f32[1,128]{1,0:T(1,128)} %add_bitcast_fusion.small, ...), custom_call_target="tpu_custom_call" | custom-call | tf_op jit(solution)/shard_map/front/pallas_call | solution.py:1384
  54.9 0.6 reduce-scatter.2.cloned.1.call-start
  55.5 0.7 constant_dynamic-slice_fusion.4
  56.2 0.1 slice.35
  56.3 0.1 copy.37
  56.4 0.1 copy.38
  56.5 0.1 copy.39
  56.6 0.1 fusion
  56.7 0.1 compare_select_fusion
  56.8 0.6 pad_add_fusion.table
  57.4 49.2 %attend.1 = (bf16[2,512,256]{2,1,0:T(8,128)(2,1)}, bf16[2,2,1024,256]{3,2,1,0:T(8,128)(2,1)}, f32[2,8,512]{2,1,0:T(8,128)}, bf16[4,2,128,256]{3,2,1,0:T(8,128)(2...) custom-call(s32[2,3,8]{2,1,0:T(4,128)} %pad_add_fusion.table, ...), custom_call_target="tpu_custom_call" | custom-call | tf_op jit(solution)/shard_map/attend/pallas_call | solution.py:589
  106.6 51.2 %out_proj.1 = (f32[128,2048]{1,0:T(8,128)}, bf16[4,2,128,2048]{3,2,1,0:T(8,128)(2,1)}) custom-call(bf16[4,2,128,256]{3,2,1,0:T(8,128)(2,1)} %get-tuple-element.53.attended, bf16[4,4,16,2048]{3,2,1,0:T(8,128)(2,1)} %get-tuple-element.54.gathered, bf16[128,2048]{1,0:T(8,128)(2,1)} %get-tuple-element.55.hidden, f32[8,2048]{1,0:T(8,128)} %get-tuple-element.56.gains), custom_call_target="tpu_custom_call" | custom-call | tf_op jit(solution)/shard_map/out_proj/pallas_call | solution.py:368
  157.8 48.9 %mlp.1 = (f32[128,2048]{1,0:T(8,128)}, f32[8,2048]{1,0:T(8,128)}, bf16[128,2048]{1,0:T(8,128)(2,1)}, bf16[4,2,128,2048]{3,2,1,0:T(8,128)(2,1)}, bf16[16,3,128,768]{3,2,1,0:T(8,128)(2,1)}) custom-call(bf16[4,2,128,2048]{3,2,1,0:T(8,128)(2,1)} %get-tuple-element.57.two_hbm, bf16[4,2,128,2048]{3,2,1,0:T(8,128)(2,1)} %get-tuple-element.58.grad_hbm, ...), custom_call_target="tpu_custom_call" | custom-call | tf_op jit(solution)/shard_map/mlp/pallas_call | solution.py:936
  206.8 78.7 %attend_back.1 = (bf16[4,2,128,768]{3,2,1,0:T(8,128)(2,1)}, bf16[16,16,2048]{2,1,0:T(8,128)(2,1)}, bf16[128,2048]{1,0:T(8,128)(2,1)}) custom-call(s32[2,3,8]{2,1,0:T(4,128)} %pad_add_fusion.table, bf16[128,2048]{1,0:T(8,128)(2,1)} %get-tuple-element.62.branch_own, bf16[4,4,16,2048]{3,2,1,0:T(8,128)(2,1)} %get-tuple-element.54.gathered, ...), custom_call_target="tpu_custom_call" | custom-call | tf_op jit(solution)/shard_map/attend_back/pallas_call | solution.py:793
  285.5 45.7 %qkv_back.1 = (f32[128,2048]{1,0:T(8,128)}, f32[8,2048]{1,0:T(8,128)}, f32[8,768]{1,0:T(8,128)}, bf16[128,768]{1,0:T(8,128)(2,1)}, bf16[16,2048]{1,0:T(8,128)(2,1)}) custom-call(bf16[4,2,128,768]{3,2,1,0:T(8,128)(2,1)} %get-tuple-element.68.joined_grad, bf16[2048,768]{1,0:T(8,128)(2,1)} %bitcast.36, bf16[128,2048]{1,0:T(8,128)(2,1)} %get-tuple-element.55.hidden, ...), custom_call_target="tpu_custom_call" | custom-call | tf_op jit(solution)/shard_map/qkv_back/pallas_call | solution.py:1119
  331.1 18.6 %collect.1 = (f32[8,16,128]{2,1,0:T(8,128)}, f32[16,6144]{1,0:T(8,128)}, f32[16,5632]{1,0:T(8,128)}, f32[16,5632]{1,0:T(8,128)}, f32[16,5632]{1,0:T(8,128)}, /*index=5*/f32[16,2048]{1,0:T(8,128)}) custom-call(f32[8,2048]{1,0:T(8,128)} %get-tuple-element.72.one_sums, f32[8,2048]{1,0:T(8,128)} %get-tuple-element.73.two_sums, ...), custom_call_target="tpu_custom_call" | custom-call | tf_op jit(solution)/shard_map/collect/pallas_call | solution.py:1525
  349.7 0.9 slice_reduce_fusion
  350.6 0.8 slice.44
  351.4 0.1 constant_dynamic-slice_fusion.1
  351.5 0.5 slice_bitcast_fusion.1
  352.0 0.1 reshape.284
  352.1 0.5 fusion.1
  352.6 0.8 copy.47
  353.4 2.3 copy.48
  355.7 1.8 copy.49
  357.5 0.7 copy.50
  358.2 0.7 copy.51
  358.9 0.7 copy.52
  359.6 0.7 copy.53
  (21 shorter events, 0.2 us)
Async XLA Ops:
  7.2 150.6 %all-gather.2.cloned.1.call-start = ((), (), s32[]{:S(2)}) async-start(), calls=%async_computation.1 | async-start | bytes 10027008 | tf_op jit(solution)/shard_map/all_gather | solution.py:1586
  54.9 276.2 %reduce-scatter.2.cloned.1.call-start = ((), (), s32[]{:S(2)}) async-start(), calls=%async_computation.2 | async-start | bytes 10027008 | tf_op jit(solution)/shard_map/reduce_scatter | solution.py:1605
  285.4 67.2 %copy-start = (bf16[128,2048]{1,0:T(8,128)(2,1)S(1)}, bf16[128,2048]{1,0:T(8,128)(2,1)}, u32[]{:S(2)}) copy-start(bf16[128,2048]{1,0:T(8,128)(2,1)} %get-tuple-element.67) | copy-start | bytes 1572868
  349.7 7.8 %copy-start.4 = (f32[16,2048]{1,0:T(8,128)S(1)}, f32[16,2048]{1,0:T(8,128)}, u32[]{:S(2)}) copy-start(f32[16,2048]{1,0:T(8,128)} %get-tuple-element.115) | copy-start | bytes 393220
  349.7 8.4 %copy-start.3 = (f32[16,5632]{1,0:T(8,128)S(1)}, f32[16,5632]{1,0:T(8,128)}, u32[]{:S(2)}) copy-start(f32[16,5632]{1,0:T(8,128)} %get-tuple-element.118) | copy-start | bytes 1081348
  349.7 9.2 %copy-start.2 = (f32[16,5632]{1,0:T(8,128)S(1)}, f32[16,5632]{1,0:T(8,128)}, u32[]{:S(2)}) copy-start(f32[16,5632]{1,0:T(8,128)} %get-tuple-element.119) | copy-start | bytes 1081348
  349.7 9.9 %copy-start.1 = (f32[16,5632]{1,0:T(8,128)S(1)}, f32[16,5632]{1,0:T(8,128)}, u32[]{:S(2)}) copy-start(f32[16,5632]{1,0:T(8,128)} %get-tuple-element.120) | copy-start | bytes 1081348
Sparse Core Ops, SparseCore 0:
  55.0 97.7 all-gather.1
  206.9 119.0 reduce-scatter.1

commit v2 on v1

--- a/solution.py
+++ b/solution.py
@@ -178,11 +178,14 @@
         self.far2.wait_recv()
         self.sib[4].start()
 
+    def sends(self):
+        return [self.up1, self.dn1, self.up2, self.dn2, self.far1, self.far2] + self.sib
+
     def finish(self):
         for one in self.sib:
             one.wait_recv()
         self.here.wait()
-        for one in [self.up1, self.dn1, self.up2, self.dn2, self.far1, self.far2] + self.sib:
+        for one in self.sends():
             one.wait_send()
 
     def run(self, work=None):
@@ -339,43 +342,6 @@
 OUT_ROWS = pltpu.VMEM((HD, D), BF)
 
 
-def kernel_out_proj(attended, gathered, hidden, gains, middle, full, weight, *scratch):
-    own, local_sem, *sems = scratch[:4]
-    y, c, up, opp, dn = ring()
-    meet(ring_peers(up, dn, c))
-    order_out(gathered, weight)
-
-    def partial(block, put):
-        a = attended[block].reshape(2 * BLOCK, HD)
-        for i in range(4):
-            q = slice(i * 512, (i + 1) * 512)
-            put(q, dot(a, weight[:, q], NN).reshape(2, BLOCK, 512))
-
-    scatter = ring_scatter(partial, scratch[4:])
-
-    def norm(r):
-        row = hidden[r, :].astype(F32) + scatter.total(r)
-        middle[r, :] = row
-        normed, _ = layer_norm(row)
-        own[r, :] = (normed * gains[2:3, :] + gains[3:4, :]).astype(BF)
-
-    rows_loop(BLOCK, 16, norm)
-    RingGather(own, full, local_sem, sems).run()
-    scatter.finish()
-
-
-def out_proj(attended, weight, hidden, gains, cid):
-    return pl.pallas_call(
-        kernel_out_proj,
-        out_shape=(jax.ShapeDtypeStruct((BLOCK, D), F32), FULL),
-        in_specs=[VM] * 4,
-        out_specs=(VM, ANY),
-        scratch_shapes=[OUT_ROWS] + AG_SCRATCH + RS_SCRATCH,
-        compiler_params=params(cid),
-        name="out_proj",
-    )(attended, weight, hidden, gains)
-
-
 NN = (((1,), (0,)), ((), ()))
 NT = (((1,), (1,)), ((), ()))
 TN = (((0,), (0,)), ((), ()))
@@ -411,12 +377,13 @@
     return v * cosine + jnp.where(entry < ROT // 2, -ahead, behind) * s
 
 
-def key_bias(table, g, tile, blocks):
+def key_bias(table, g, tile, blocks, q_part=0):
     token = lane(BLOCK)
     q_code, q_low = [], []
     for j in range(2):
-        low = table[g, 1, 2 * tile + j] * 4096
-        q_code.append(low + table[g, 0, 2 * tile + j] + token)
+        block = 4 * q_part + 2 * tile + j
+        low = table[g, 1, block] * 4096
+        q_code.append(low + table[g, 0, block] + token)
         q_low.append(low + jnp.zeros_like(token))
     q_code = jnp.concatenate(q_code, axis=1)
     q_low = jnp.concatenate(q_low, axis=1)
@@ -450,14 +417,20 @@
     shift,
     cotangent,
     out_in,
+    hidden,
+    gains,
     queries,
     kv,
     lse,
     attended,
     grad_out,
+    out_full,
+    middle,
     grad_all,
-    out_full,
+    two_all,
     out_rows,
+    out_weight,
+    own_two,
     tokens,
     weight,
     cosines,
@@ -475,31 +448,25 @@
         [(weight_hbm, weight)] + [(tokens_hbm.at[y], tokens.at[y]) for y in range(4)], local
     )
     y0, c, up, opp, dn = ring()
-    base, limit = table[c, 0, y0], table[c, 2, y0]
-
-    def mask(r):
-        place = base + r.start + lax.broadcasted_iota(jnp.int32, (16, 1), 0)
-        row = jnp.where(place < limit, cotangent[r, :].astype(F32), 0.0)
-        grad_out[r, :] = permute_rows(row).astype(BF)
-
-    rows_loop(BLOCK, 16, mask)
     out_rows[...] = permute_rows(out_in[...].astype(F32)).astype(BF)
     meet(list(ring_peers(up, dn, c)) + plane_peers())
     gather = RingGather(grad_out, grad_all, sems[0], sems[1:3])
-    gather.start()
-    plane = PlaneGather(out_rows, out_full, *sems[3:])
+    plane = PlaneGather(out_rows, out_full, *sems[3:6], 0)
+    two_gather = RingGather(own_two, two_all, sems[6], sems[7:9])
+    part, sib_out = sems[9:11]
+    scatter = RingScatter(
+        lambda j, rows: part[j, rows, :], lambda j: sib_out.at[j], *sems[11:]
+    )
     plane.start()
-
+    lse[...] = jnp.zeros_like(lse)
+    weight_in.wait()
     for y in range(4):
+        at = slice(y * BLOCK, (y + 1) * BLOCK)
         for g in range(2):
-            at = slice(y * BLOCK, (y + 1) * BLOCK)
             cosine, sine = turn_tables(table[g, 0, y])
             cosines[g, at, :] = cosine
             sines[g, at, :] = sine
-    weight_in.wait()
-    for y in range(4):
         token_in[y].wait()
-        at = slice(y * BLOCK, (y + 1) * BLOCK)
         new = dot(tokens[y].reshape(TILE, D), weight[:, HD:], NN) + shift[:, HD:]
         for g in range(2):
             rows = slice(g * BLOCK, (g + 1) * BLOCK)
@@ -516,7 +483,16 @@
     ]
     for one in trade:
         one.start()
-    gather.forward()
+    plane.middle()
+    base, limit = table[c, 0, y0], table[c, 2, y0]
+
+    def mask(r):
+        place = base + r.start + lax.broadcasted_iota(jnp.int32, (16, 1), 0)
+        row = jnp.where(place < limit, cotangent[r, :].astype(F32), 0.0)
+        grad_out[r, :] = permute_rows(row).astype(BF)
+
+    rows_loop(BLOCK, 16, mask)
+    gather.start()
     for y in range(4):
         at = slice(y * BLOCK, (y + 1) * BLOCK)
         new = dot(tokens[y].reshape(TILE, D), weight[:, :HD], NN) + shift[:, :HD]
@@ -527,7 +503,6 @@
                 turned = turn(new[rows, q], cosines[g, at, :], sines[g, at, :], 1.0)
                 queries[g, at, q] = turned.astype(BF) * jnp.asarray(SCALE, BF)
 
-    plane.middle()
     first_head = lax.broadcasted_iota(jnp.int32, (BLOCK, 1), 0) < HEAD_DIM
 
     def work(part, g):
@@ -568,24 +543,84 @@
                     for j in range(2):
                         attended[2 * tile + j, g, :, q] = out[j * BLOCK : (j + 1) * BLOCK]
 
-    for g in range(2):
-        work(0, g)
+    def project(g):
+        for j in range(4):
+            a = attended[scatter.order[j], g]
+            for i in range(4):
+                q = slice(i * 512, (i + 1) * 512)
+                value = dot(a, out_weight[:, q], NN)
+
+                @pl.when(c == g)
+                def _(j=j, q=q, value=value):
+                    part[j, :, q] = value
+
+                @pl.when(c != g)
+                def _(j=j, q=q, value=value):
+                    sib_out[j, :, q] = value.astype(BF)
+
+            @pl.when(c != g)
+            def _(j=j):
+                scatter.sib[j].start()
+
+    def norm(r):
+        row = hidden[r, :].astype(F32) + scatter.total(r)
+        middle[r, :] = row
+        normed, _ = layer_norm(row)
+        own_two[r, :] = (normed * gains[2:3, :] + gains[3:4, :]).astype(BF)
+
+    def exchange():
+        scatter.send_far()
+        scatter.send_early(0)
+        scatter.send_early(1)
+
+    def settle():
+        scatter.send_late()
+        scatter.wait()
+        rows_loop(BLOCK, 16, norm)
+        two_gather.start()
+
+    def pass_on():
+        two_gather.forward()
+        two_gather.share()
+        two_gather.share_far()
+
+    work(0, 0)
+    gather.forward()
+    work(0, 1)
     gather.share()
-    for g in range(2):
-        trade[g].wait_recv()
-        if g == 1:
-            gather.share_far()
-        work(1, g)
+    plane.finish()
+    order_out(out_full, out_weight)
+    trade[0].wait_recv()
+    work(1, 0)
+    project(0)
+    gather.share_far()
+
+    @pl.when(c == 0)
+    def _():
+        exchange()
+
+    trade[1].wait_recv()
+    work(1, 1)
+    project(1)
+
+    @pl.when(c == 1)
+    def _():
+        exchange()
+
+    settle()
+    pass_on()
+
     for one in trade:
         one.wait_send()
     gather.finish()
-    plane.finish()
+    two_gather.finish()
+    scatter.finish()
 
 
 SM = pl.BlockSpec(memory_space=pltpu.SMEM)
 
 
-def attend(table, tokens, weight, shift, cotangent, out_in, cid):
+def attend(table, tokens, weight, shift, cotangent, out_in, hidden, gains, cid):
     return pl.pallas_call(
         kernel_attend,
         out_shape=(
@@ -594,13 +629,17 @@
             jax.ShapeDtypeStruct((2, 8, TOKENS), F32),
             jax.ShapeDtypeStruct((4, 2, BLOCK, HD), BF),
             jax.ShapeDtypeStruct((BLOCK, D), BF),
+            jax.ShapeDtypeStruct((4, 4, 16, D), BF),
+            jax.ShapeDtypeStruct((BLOCK, D), F32),
             FULL,
-            jax.ShapeDtypeStruct((4, 4, 16, D), BF),
+            FULL,
         ),
-        in_specs=[SM, ANY, ANY, VM, VM, VM],
-        out_specs=(VM, VM, VM, VM, VM, ANY, ANY),
+        in_specs=[SM, ANY, ANY] + [VM] * 5,
+        out_specs=(VM,) * 7 + (ANY, ANY),
         scratch_shapes=[
             pltpu.VMEM((16, D), BF),
+            OUT_ROWS,
+            pltpu.VMEM((BLOCK, D), BF),
             pltpu.VMEM((4, 2, BLOCK, D), BF),
             pltpu.VMEM((D, 3 * HD), BF),
             pltpu.VMEM((2, TOKENS, BLOCK), F32),
@@ -613,10 +652,12 @@
             pltpu.SemaphoreType.DMA((2,)),
         ]
         + AG_SCRATCH[1:]
-        + PG_SEMS,
+        + PG_SEMS
+        + AG_SCRATCH[1:]
+        + RS_SCRATCH,
         compiler_params=params(cid),
         name="attend",
-    )(table, tokens, weight, shift, cotangent, out_in)
+    )(table, tokens, weight, shift, cotangent, out_in, hidden, gains)
 
 
 def kernel_attend_back(
@@ -627,6 +668,8 @@
     queries,
     kv,
     lse,
+    other_queries,
+    other_lse,
     mlp_out,
     middle_hbm,
     joined_grad,
@@ -636,14 +679,15 @@
     middle,
     own_out,
     probs,
+    other_probs,
     local,
     weight,
     grads,
+    other_grads,
     dq,
     mean,
+    other_mean,
     dkv,
-    kv_out,
-    kv_in,
     send,
     recv,
     local_sem,
@@ -659,7 +703,6 @@
     meet(list(ring_peers(up, dn, c)) + [partner])
     gather = RingGather(branch_own, branch, local_sem, (gather_send, gather_recv))
     gather.start()
-    sems = (send, recv)
     scatter = RingScatter(
         lambda j, rows: own_out[j, rows, :].astype(F32),
         lambda j: mlp_out.at[order[j], 1 - c],
@@ -668,58 +711,72 @@
     for one in scatter.sib:
         one.start()
     order_out(gathered, weight)
-
-    def recompute(g):
+    trade = [
+        remote((send, recv), 0, grads, other_grads, partner),
+        remote((send, recv), 1, mean, other_mean, partner),
+    ]
+
+    def recompute(part, g):
+        q_src, lse_src = (queries, lse) if part == 0 else (other_queries, other_lse)
+        dst = probs if part == 0 else other_probs
+        blocks = range(8) if part == 0 else range(4)
+        rows = slice(0, len(blocks) * BLOCK)
+
         @pl.loop(0, 2)
         def _(tile):
             at = pl.ds(pl.multiple_of(tile * TILE, TILE), TILE)
-            bias = key_bias(table, g, tile, range(8))
+            bias = key_bias(table, g, tile, blocks, part)
             for pair in range(2):
                 q = slice(pair * BLOCK, (pair + 1) * BLOCK)
                 for h in range(2):
                     row = slice(2 * pair + h, 2 * pair + h + 1)
-                    s = dot(kv[0, g, :, q], queries[g, at, q] * head_mask(h), NT) + bias
-                    probs[g, tile, 2 * pair + h] = jnp.exp(s - lse[g, row, at])
-
-    recompute(0)
+                    s = dot(kv[0, g, rows, q], q_src[g, at, q] * head_mask(h), NT) + bias
+                    dst[g, tile, 2 * pair + h] = jnp.exp(s - lse_src[g, row, at])
+
+    recompute(0, 0)
     gather.forward()
-    recompute(1)
+    recompute(0, 1)
     gather.share()
     gather.share_far()
+    recompute(1, 0)
+    recompute(1, 1)
     gather.finish()
 
-    @pl.loop(0, 4)
-    def _(y):
-        at = pl.ds(pl.multiple_of(y * BLOCK, BLOCK), BLOCK)
+    dq[...] = jnp.zeros_like(dq)
+    dkv[...] = jnp.zeros_like(dkv)
+    mean[...] = jnp.zeros_like(mean)
+    heads = jnp.concatenate([head_mask(0), head_mask(1)] * 4, axis=0).astype(F32)
+    for y in range(4):
+        at = slice(y * BLOCK, (y + 1) * BLOCK)
         new = dot(branch[y].reshape(TILE, D), weight[...], NT)
         for g in range(2):
-            grads[g, at, :] = new[g * BLOCK : (g + 1) * BLOCK].astype(BF)
-
+            rows = slice(g * BLOCK, (g + 1) * BLOCK)
+            grads[g, at, :] = new[rows].astype(BF)
+            for pair in range(2):
+                q = slice(pair * BLOCK, (pair + 1) * BLOCK)
+                both = slice(2 * pair, 2 * pair + 2)
+                mixed = attended[y, g, :, q].astype(F32) * new[rows, q].astype(BF).astype(F32)
+                mean[g, both, at] = lax.dot_general(
+                    heads, mixed, NT, precision=lax.Precision.HIGHEST
+                )[0:2]
+    for one in trade:
+        one.start()
     for one in out_in:
         one.wait()
     scatter.send_far()
     scatter.send_early(0)
     scatter.send_early(1)
-    trade = [remote(sems, g, kv_out.at[g], kv_in.at[g], partner) for g in range(2)]
-    dq[...] = jnp.zeros_like(dq)
-    dkv[...] = jnp.zeros_like(dkv)
-    heads = jnp.concatenate([head_mask(0), head_mask(1)] * 4, axis=0).astype(F32)
 
     def back(part, g):
-        rows = slice(part * TOKENS, (part + 1) * TOKENS)
+        q_src, g_src = (queries, grads) if part == 0 else (other_queries, other_grads)
+        mean_src, p_src = (mean, probs) if part == 0 else (other_mean, other_probs)
+        rows = slice(0, KEYS if part == 0 else TOKENS)
 
         @pl.loop(0, 2)
         def _(tile):
             at = pl.ds(pl.multiple_of(tile * TILE, TILE), TILE)
             for pair in range(2):
                 q = slice(pair * BLOCK, (pair + 1) * BLOCK)
-                both = slice(2 * pair, 2 * pair + 2)
-                if part == 1:
-                    mixed = attended[pl.ds(2 * tile, 2), g, :, q].reshape(TILE, BLOCK).astype(F32)
-                    mixed = mixed * grads[g, at, q].astype(F32)
-                    mean[g, both, at] = lax.dot_general(
-                        heads, mixed, NT, precision=lax.Precision.HIGHEST
-                    )[0:2]
                 k_all = kv[0, g, rows, q]
                 v_all = kv[1, g, rows, q]
                 new_q = jnp.zeros((BLOCK, TILE), F32)
@@ -727,26 +784,23 @@
                 new_v = jnp.zeros((TOKENS, BLOCK), F32)
                 for h in range(2):
                     row = slice(2 * pair + h, 2 * pair + h + 1)
-                    q_head = queries[g, at, q] * head_mask(h)
-                    g_head = grads[g, at, q] * head_mask(h)
-                    p = probs[g, tile, 2 * pair + h, rows, :]
+                    q_head = q_src[g, at, q] * head_mask(h)
+                    g_head = g_src[g, at, q] * head_mask(h)
+                    p = p_src[g, tile, 2 * pair + h]
                     p_grad = dot(v_all, g_head, NT)
-                    s_grad = (p * (p_grad - mean[g, row, at])).astype(BF)
-                    new_v = new_v + dot(p.astype(BF), g_head, NN)
-                    new_k = new_k + dot(s_grad, q_head, NN)
-                    new_q = new_q + dot(k_all * head_mask(h), s_grad, TN)
-                dq[g, q, at] += new_q
-                dkv[0, g, rows, q] += new_k
-                dkv[1, g, rows, q] += new_v
-
-    for g in range(2):
-        back(1, g)
-        for i in range(2):
-            kv_out[g, i] = dkv[i, g, pl.ds(TOKENS, TOKENS), :].astype(BF)
-        trade[g].start()
+                    s_grad = (p * (p_grad - mean_src[g, row, at])).astype(BF)
+                    new_v = new_v + dot(p[:TOKENS].astype(BF), g_head, NN)
+                    new_k = new_k + dot(s_grad[:TOKENS], q_head, NN)
+                    if part == 0:
+                        new_q = new_q + dot(k_all * head_mask(h), s_grad, TN)
+                if part == 0:
+                    dq[g, q, at] += new_q
+                dkv[0, g, :, q] += new_k
+                dkv[1, g, :, q] += new_v
+
+    back(0, 0)
     scatter.send_late()
-    for g in range(2):
-        back(0, g)
+    back(0, 1)
 
     @pl.loop(0, 8)
     def _(i):
@@ -758,6 +812,10 @@
                     row = x * 64 + zl * 32 + a * 16
                     out_part[x * 4 + a * 2 + zl, :, q] = new[row : row + 16].astype(BF)
 
+    for one in trade:
+        one.wait_recv()
+    back(1, 0)
+    back(1, 1)
     scatter.wait()
     middle_in.wait()
 
@@ -766,7 +824,6 @@
 
     rows_loop(BLOCK, 16, add)
     for g in range(2):
-        trade[g].wait_recv()
 
         @pl.loop(0, 4)
         def _(y, g=g):
@@ -776,20 +833,30 @@
                 q = slice(pair * BLOCK, (pair + 1) * BLOCK)
                 new = dq[g, q, at].T * SCALE
                 joined_grad[y, g, :, q] = turn(new, cosine, sine, -1.0).astype(BF)
-                new = dkv[0, g, at, q] + kv_in[g, 0, at, q].astype(F32)
                 joined_grad[y, g, :, HD + pair * BLOCK : HD + (pair + 1) * BLOCK] = turn(
-                    new, cosine, sine, -1.0
+                    dkv[0, g, at, q], cosine, sine, -1.0
                 ).astype(BF)
-            joined_grad[y, g, :, 2 * HD :] = (
-                dkv[1, g, at, :] + kv_in[g, 1, at, :].astype(F32)
-            ).astype(BF)
+            joined_grad[y, g, :, 2 * HD :] = dkv[1, g, at, :].astype(BF)
 
     for one in trade:
         one.wait_send()
     scatter.finish()
 
 
-def attend_back(table, branch, weight, attended, queries, kv, lse, mlp_out, middle, cid):
+def attend_back(
+    table,
+    branch,
+    gathered,
+    attended,
+    queries,
+    kv,
+    lse,
+    other_queries,
+    other_lse,
+    mlp_out,
+    middle,
+    cid,
+):
     return pl.pallas_call(
         kernel_attend_back,
         out_shape=(
@@ -797,21 +864,22 @@
             jax.ShapeDtypeStruct((16, 16, D), BF),
             jax.ShapeDtypeStruct((BLOCK, D), BF),
         ),
-        in_specs=[SM] + [VM] * 6 + [ANY, ANY],
+        in_specs=[SM] + [VM] * 8 + [ANY, ANY],
         out_specs=(VM, VM, VM),
         scratch_shapes=[
             pltpu.VMEM((4, 2, BLOCK, D), BF),
             pltpu.VMEM((BLOCK, D), F32),
             pltpu.VMEM((4, BLOCK, D), BF),
             pltpu.VMEM((2, 2, 4, KEYS, TILE), F32),
+            pltpu.VMEM((2, 2, 4, TOKENS, TILE), F32),
             pltpu.SemaphoreType.DMA((5,)),
             OUT_ROWS,
             pltpu.VMEM((2, TOKENS, HD), BF),
+            pltpu.VMEM((2, TOKENS, HD), BF),
             pltpu.VMEM((2, HD, TOKENS), F32),
             pltpu.VMEM((2, 8, TOKENS), F32),
-            pltpu.VMEM((2, 2, KEYS, HD), F32),
-            pltpu.VMEM((2, 2, TOKENS, HD), BF),
-            pltpu.VMEM((2, 2, TOKENS, HD), BF),
+            pltpu.VMEM((2, 8, TOKENS), F32),
+            pltpu.VMEM((2, 2, TOKENS, HD), F32),
             pltpu.SemaphoreType.DMA((2,)),
             pltpu.SemaphoreType.DMA((2,)),
         ]
@@ -819,7 +887,19 @@
         + RS_SCRATCH[2:],
         compiler_params=params(cid),
         name="attend_back",
-    )(table, branch, weight, attended, queries, kv, lse, mlp_out, middle)
+    )(
+        table,
+        branch,
+        gathered,
+        attended,
+        queries,
+        kv,
+        lse,
+        other_queries,
+        other_lse,
+        mlp_out,
+        middle,
+    )
 
 
 def kernel_mlp(
@@ -829,9 +909,13 @@
     middle,
     grad_out,
     gains,
+    queries,
+    lse,
     middle_grad,
     sums,
     own,
+    other_queries,
+    other_lse,
     out_hbm,
     part_hbm,
     two,
@@ -843,9 +927,12 @@
     both_grads,
     local,
     leave,
+    send,
+    recv,
     *scratch,
 ):
     y, c, up, opp, dn = ring()
+    partner = {"zh": 1 - lax.axis_index("zh")}
     order = (opp, up, dn, y)
     w_in = load([(w_hbm.at[:, k], w.at[k]) for k in range(3)], local)
     block_in = load(
@@ -853,7 +940,13 @@
         local,
         3,
     )
-    meet(ring_peers(up, dn, c))
+    meet(list(ring_peers(up, dn, c)) + [partner])
+    trade = [
+        remote((send, recv), 0, queries, other_queries, partner),
+        remote((send, recv), 1, lse, other_lse, partner),
+    ]
+    for one in trade:
+        one.start()
     held = jnp.logical_or(lane(FP) >= BLOCK, y < 2)
     gate_lanes, up_lanes = pl.ds(0, FP), pl.ds(FP, FP)
     waits = [w_in + block_in[0:2], block_in[2:4], block_in[4:6], block_in[6:8]]
@@ -927,11 +1020,11 @@
 
     rows_loop(BLOCK, 16, back)
     scatter.finish()
-    for one in outs + done:
+    for one in outs + done + trade:
         one.wait()
 
 
-def mlp(two, grad_all, w, middle, grad_out, gains, cid):
+def mlp(two, grad_all, w, middle, grad_out, gains, queries, lse, cid):
     block = (4, 2, BLOCK, D)
     return pl.pallas_call(
         kernel_mlp,
@@ -939,11 +1032,13 @@
             jax.ShapeDtypeStruct((BLOCK, D), F32),
             jax.ShapeDtypeStruct((8, D), F32),
             jax.ShapeDtypeStruct((BLOCK, D), BF),
+            jax.ShapeDtypeStruct((2, TOKENS, HD), BF),
+            jax.ShapeDtypeStruct((2, 8, TOKENS), F32),
             FULL,
             jax.ShapeDtypeStruct((16, 3, BLOCK, FP), BF),
         ),
-        in_specs=[ANY] * 3 + [VM] * 3,
-        out_specs=(VM, VM, VM, ANY, ANY),
+        in_specs=[ANY] * 3 + [VM] * 5,
+        out_specs=(VM,) * 5 + (ANY, ANY),
         scratch_shapes=[
             pltpu.VMEM(block, BF),
             pltpu.VMEM(block, BF),
@@ -954,11 +1049,13 @@
             pltpu.VMEM((4, 2, BLOCK, 2 * FP), BF),
             pltpu.SemaphoreType.DMA((11,)),
             pltpu.SemaphoreType.DMA((12,)),
+            pltpu.SemaphoreType.DMA((2,)),
+            pltpu.SemaphoreType.DMA((2,)),
         ]
         + RS_SCRATCH,
         compiler_params=params(cid),
         name="mlp",
-    )(two, grad_all, w, middle, grad_out, gains)
+    )(two, grad_all, w, middle, grad_out, gains, queries, lse)
 
 
 class PlaneScatter:
@@ -1206,10 +1303,9 @@
 class PlaneGather:
     COPIES = 12
 
-    def __init__(self, src, full, local_sem, send, recv):
+    def __init__(self, src, full, local_sem, send, recv, x_first):
         sems = send, recv
-        half = src.shape[-1] // 2
-        a, b = pl.ds(0, half), pl.ds(half, half)
+        a, b = pl.ds(0, x_first), pl.ds(x_first, src.shape[-1] - x_first)
         rest = (slice(None),) * (len(src.shape) - 1)
         x = lax.axis_index("x")
         z = lax.axis_index("zh") * 2 + lax.axis_index("zl")
@@ -1220,11 +1316,14 @@
             z_to = lax.rem(z + d, 4)
             to_x = {"x": lax.rem(x + d, 4)}
             to_z = {"zh": z_to // 2, "zl": lax.rem(z_to, 2)}
-            self.one.append(remote(sems, k, src.at[rest + (a,)], full.at[(x, z) + rest + (a,)], to_x))
-            self.one.append(remote(sems, 3 + k, src.at[rest + (b,)], full.at[(x, z) + rest + (b,)], to_z))
-            row = full.at[(every, z) + rest + (a,)]
-            self.two.append(remote(sems, 6 + k, row, row, to_z))
-            row = full.at[(x, every) + rest + (b,)]
+            if x_first:
+                at = rest + (a,)
+                self.one.append(remote(sems, k, src.at[at], full.at[(x, z) + at], to_x))
+                row = full.at[(every, z) + at]
+                self.two.append(remote(sems, 6 + k, row, row, to_z))
+            at = rest + (b,)
+            self.one.append(remote(sems, 3 + k, src.at[at], full.at[(x, z) + at], to_z))
+            row = full.at[(x, every) + at]
             self.two.append(remote(sems, 9 + k, row, row, to_x))
         self.here = pltpu.make_async_copy(src, full.at[x, z], local_sem)
 
@@ -1349,7 +1448,7 @@
         one.start()
     for one in qkv + keep[1:]:
         one.wait()
-    plane = PlaneGather(qkv_rows, qkv_full, *sems[:3])
+    plane = PlaneGather(qkv_rows, qkv_full, *sems[:3], 3 * HD // 2)
     plane.start()
     for one in mlp:
         one.start()
@@ -1595,18 +1694,28 @@
     second = (start >= first_pad).astype(jnp.int32)
     limit = jnp.where(second == 1, plan[:, 1:2], plan[:, 0:1])
     table = jnp.stack([start - second * first_pad, second, limit], axis=1)
-    queries, kv, lse, attended, grad_out, grad_all, out_full = attend(
-        table, one_all, qkv_full, shift, cotangent[0], out_rows, 6
-    )
-    middle, two_all = out_proj(attended, out_full, hidden, gains, 2)
-    middle_grad, two_sums, branch, mlp_out, mlp_part = mlp(
-        two_all, grad_all, mlp_full, middle, grad_out, gains, 3
+    queries, kv, lse, attended, grad_out, out_full, middle, grad_all, two_all = attend(
+        table, one_all, qkv_full, shift, cotangent[0], out_rows, hidden, gains, 6
+    )
+    middle_grad, two_sums, branch, other_queries, other_lse, mlp_out, mlp_part = mlp(
+        two_all, grad_all, mlp_full, middle, grad_out, gains, queries, lse, 3
     )
     mlp_sum = lax.psum_scatter(
         mlp_part.reshape(16 * 3 * BLOCK, FP), XZ, scatter_dimension=0, tiled=True
     )
     joined_grad, out_part, hidden_out = attend_back(
-        table, branch, out_full, attended, queries, kv, lse, mlp_out, middle, 7
+        table,
+        branch,
+        out_full,
+        attended,
+        queries,
+        kv,
+        lse,
+        other_queries,
+        other_lse,
+        mlp_out,
+        middle,
+        7,
     )
     input_grad, one_sums, shift_sum, qkv_sum, out_sum = qkv_back(
         joined_grad, qkv_full, hidden, middle_grad, gains, one_all, out_part, 4

time: 371 us -> 351 us (0.946)
  Pallas kernels: 337 us -> 312 us
  waiting for transfers between devices: 0.08 us -> 5.79 us
    pallas_call x1 -> x0, Pallas kernels: 51.2 us -> none  [out_proj(): pl.pallas_call(kernel_out_proj, out_shape=(jax.ShapeDtypeStruct((BLOCK, D...]
    pallas_call x1, Pallas kernels: 49.2 us -> 84.4 us  [attend(): pl.pallas_call(kernel_attend, out_shape=(jax.ShapeDtypeStruct((2, TOKENS,...]
    pallas_call x1, Pallas kernels: 78.7 us -> 69 us  [attend_back(): pl.pallas_call(kernel_attend_back, out_shape=(jax.ShapeDtypeStruct((4, 2,...]
    all_gather x1, waiting for transfers between devices: 0.02 us -> 5.74 us  [body(): lax.all_gather(mlp_rows.reshape(3, BLOCK, FP), XZ, axis=0, tiled=False)]
  transfers between devices with their start and end apart: 2 -> 2, of which waited for: 0 -> 1; matrix products, arithmetic and copies ran while one was open for 1% -> 1% of each run, Pallas kernels for 61% -> 58%
where the time goes in v2:
time: 351 us; the launch traced here: 347 us
  Pallas kernels  312 us (89%)
  between operations  14.4 us (4%)
  local copies, waits for them, and re-layouts  10.8 us (3%)
  waiting for transfers between devices  5.79 us (2%)
  other arithmetic  4.27 us (1%)
    pallas_call x1, Pallas kernels, attend(): pl.pallas_call(kernel_attend, out_shape=(jax.ShapeDtypeStruct((2, TOKENS,...  84.4 us
    pallas_call x1, Pallas kernels, attend_back(): pl.pallas_call(kernel_attend_back, out_shape=(jax.ShapeDtypeStruct((4, 2,...  69 us
    pallas_call x1, Pallas kernels, mlp(): pl.pallas_call(kernel_mlp, out_shape=(jax.ShapeDtypeStruct((BLOCK, D), F3...  49.2 us
    pallas_call x1, Pallas kernels, qkv_back(): pl.pallas_call(kernel_qkv_back, out_shape=(jax.ShapeDtypeStruct((BLOCK, D...  46.7 us
    pallas_call x1, Pallas kernels, front(): pl.pallas_call(kernel_front, out_shape=(jax.ShapeDtypeStruct((16, TP, 1,...  45 us
    pallas_call x1, Pallas kernels, collect(): pl.pallas_call(kernel_collect, out_shape=(jax.ShapeDtypeStruct((TP, 16, B...  17.2 us
    unnamed x20, local copies, waits for them, and re-layouts  8.02 us
  transfers between devices with their start and end apart: 2, of which 1 were waited for; matrix products, arithmetic and copies ran while one was open for 1% of the time, Pallas kernels for 58%

profile of v2, /device:TPU:1, one launch (start us, length us, event | category | flops | bytes accessed | tf_op | source)
XLA Modules:
  0.0 347.5 jit_solution(13716209423531029424)
XLA Ops:
  7.2 0.7 convert_bitcast_fusion.1
  7.9 0.7 convert_bitcast_fusion
  8.5 1.3 add_bitcast_fusion.small
  9.8 45.0 %front.1 = (f32[16,8,1,128]{3,2,1,0:T(1,128)}, f32[8,2048]{1,0:T(8,128)}, f32[1,768]{1,0:T(1,128)}, bf16[4,4,8,16,768]{4,3,2,1,0:T(8,128)(2,1)}, bf16[3,8,16,768...) custom-call(f32[1,128]{1,0:T(1,128)} %add_bitcast_fusion.small, ...), custom_call_target="tpu_custom_call" | custom-call | tf_op jit(solution)/shard_map/front/pallas_call | solution.py:1483
  54.9 0.6 reduce-scatter.2.cloned.1.call-start
  55.5 0.7 constant_dynamic-slice_fusion.4
  56.2 0.1 slice.35
  56.3 0.1 copy.37
  56.4 0.1 copy.38
  56.5 0.1 copy.39
  56.6 0.1 fusion
  56.7 0.1 compare_select_fusion
  56.7 0.6 pad_add_fusion.table
  57.4 84.4 %attend.1 = (bf16[2,512,256]{2,1,0:T(8,128)(2,1)}, bf16[2,2,1024,256]{3,2,1,0:T(8,128)(2,1)}, f32[2,8,512]{2,1,0:T(8,128)}, bf16[4,2,128,256]{3,2,1,0:T(8,128)(2...) custom-call(s32[2,3,8]{2,1,0:T(4,128)} %pad_add_fusion.table, ...), custom_call_target="tpu_custom_call" | custom-call | tf_op jit(solution)/shard_map/attend/pallas_call | solution.py:624
  141.8 5.7 %all-gather.2.cloned.1.call-done.w_hbm = bf16[16,3,128,768]{3,2,1,0:T(8,128)(2,1)} async-done(((bf16[1,3,128,768]{3,2,1,0:T(8,128)(2,1)}), bf16[16,3,128,768]{3,2,1,0:T(8,128)(2,1)}) %all-gather.2.cloned.1.call-update) | async-done | bytes 9437200 | tf_op jit(solution)/shard_map/all_gather | solution.py:1685
  147.5 49.2 %mlp.1 = (f32[128,2048]{1,0:T(8,128)}, f32[8,2048]{1,0:T(8,128)}, bf16[128,2048]{1,0:T(8,128)(2,1)}, bf16[2,512,256]{2,1,0:T(8,128)(2,1)}, f32[2,8,512]{2,1,0:T(...) custom-call(bf16[4,2,128,2048]{3,2,1,0:T(8,128)(2,1)} %get-tuple-element.57.two_hbm, ...), custom_call_target="tpu_custom_call" | custom-call | tf_op jit(solution)/shard_map/mlp/pallas_call | solution.py:1029
  196.8 69.0 %attend_back.1 = (bf16[4,2,128,768]{3,2,1,0:T(8,128)(2,1)}, bf16[16,16,2048]{2,1,0:T(8,128)(2,1)}, bf16[128,2048]{1,0:T(8,128)(2,1)}) custom-call(s32[2,3,8]{2,1,0:T(4,128)} %pad_add_fusion.table, bf16[128,2048]{1,0:T(8,128)(2,1)} %get-tuple-element.64.branch_own, bf16[4,4,16,2048]{3,2,1,0:T(8,128)(2,1)} %get-tuple-element.65.gathered, ...), custom_call_target="tpu_custom_call" | custom-call | tf_op jit(solution)/shard_map/attend_back/pallas_call | solution.py:860
  265.8 46.7 %qkv_back.1 = (f32[128,2048]{1,0:T(8,128)}, f32[8,2048]{1,0:T(8,128)}, f32[8,768]{1,0:T(8,128)}, bf16[128,768]{1,0:T(8,128)(2,1)}, bf16[16,2048]{1,0:T(8,128)(2,1)}) custom-call(bf16[4,2,128,768]{3,2,1,0:T(8,128)(2,1)} %get-tuple-element.72.joined_grad, bf16[2048,768]{1,0:T(8,128)(2,1)} %bitcast.36, bf16[128,2048]{1,0:T(8,128)(2,1)} %get-tuple-element.55.hidden, ...), custom_call_target="tpu_custom_call" | custom-call | tf_op jit(solution)/shard_map/qkv_back/pallas_call | solution.py:1216
  312.6 17.2 %collect.1 = (f32[8,16,128]{2,1,0:T(8,128)}, f32[16,6144]{1,0:T(8,128)}, f32[16,5632]{1,0:T(8,128)}, f32[16,5632]{1,0:T(8,128)}, f32[16,5632]{1,0:T(8,128)}, /*index=5*/f32[16,2048]{1,0:T(8,128)}) custom-call(f32[8,2048]{1,0:T(8,128)} %get-tuple-element.76.one_sums, f32[8,2048]{1,0:T(8,128)} %get-tuple-element.77.two_sums, ...), custom_call_target="tpu_custom_call" | custom-call | tf_op jit(solution)/shard_map/collect/pallas_call | solution.py:1624
  329.8 0.9 slice_reduce_fusion
  330.7 0.8 slice.44
  331.5 0.1 constant_dynamic-slice_fusion.1
  331.6 0.5 slice_bitcast_fusion.1
  332.1 0.1 reshape.284
  332.2 0.5 fusion.1
  332.7 0.8 copy.47
  333.5 2.3 copy.48
  335.8 1.8 copy.49
  337.6 0.7 copy.50
  338.2 0.7 copy.51
  339.0 0.7 copy.52
  339.7 0.7 copy.53
  (20 shorter events, 0.2 us)
Async XLA Ops:
  7.2 140.3 %all-gather.2.cloned.1.call-start = ((), (), s32[]{:S(2)}) async-start(), calls=%async_computation.1 | async-start | bytes 10027008 | tf_op jit(solution)/shard_map/all_gather | solution.py:1685
  54.9 257.6 %reduce-scatter.2.cloned.1.call-start = ((), (), s32[]{:S(2)}) async-start(), calls=%async_computation.2 | async-start | bytes 10027008 | tf_op jit(solution)/shard_map/reduce_scatter | solution.py:1703
  265.8 66.9 %copy-start = (bf16[128,2048]{1,0:T(8,128)(2,1)S(1)}, bf16[128,2048]{1,0:T(8,128)(2,1)}, u32[]{:S(2)}) copy-start(bf16[128,2048]{1,0:T(8,128)(2,1)} %get-tuple-element.71) | copy-start | bytes 1572868
  329.8 7.8 %copy-start.4 = (f32[16,2048]{1,0:T(8,128)S(1)}, f32[16,2048]{1,0:T(8,128)}, u32[]{:S(2)}) copy-start(f32[16,2048]{1,0:T(8,128)} %get-tuple-element.119) | copy-start | bytes 393220
  329.8 8.4 %copy-start.3 = (f32[16,5632]{1,0:T(8,128)S(1)}, f32[16,5632]{1,0:T(8,128)}, u32[]{:S(2)}) copy-start(f32[16,5632]{1,0:T(8,128)} %get-tuple-element.122) | copy-start | bytes 1081348
  329.8 9.2 %copy-start.2 = (f32[16,5632]{1,0:T(8,128)S(1)}, f32[16,5632]{1,0:T(8,128)}, u32[]{:S(2)}) copy-start(f32[16,5632]{1,0:T(8,128)} %get-tuple-element.123) | copy-start | bytes 1081348
  329.8 9.9 %copy-start.1 = (f32[16,5632]{1,0:T(8,128)S(1)}, f32[16,5632]{1,0:T(8,128)}, u32[]{:S(2)}) copy-start(f32[16,5632]{1,0:T(8,128)} %get-tuple-element.124) | copy-start | bytes 1081348
Sparse Core Ops, SparseCore 0:
  55.0 92.4 all-gather.1
  196.9 109.6 reduce-scatter.1

commit v3 on v2

--- a/solution.py
+++ b/solution.py
@@ -22,7 +22,7 @@
 NEG = -1e30
 SCALE = HEAD_DIM ** (-0.5)
 TPA = ("y", "core")
-XZ = ("x", "zh", "zl")
+ZX = ("zh", "zl", "x")
 ROWS = ("zh", "y", "x", "zl", "core")
 GRP = ("x", "zl", "core")
 SLOT = ("zh", "y")
@@ -585,6 +585,7 @@
         two_gather.share_far()
 
     work(0, 0)
+    plane.forward()
     gather.forward()
     work(0, 1)
     gather.share()
@@ -745,20 +746,22 @@
     dq[...] = jnp.zeros_like(dq)
     dkv[...] = jnp.zeros_like(dkv)
     mean[...] = jnp.zeros_like(mean)
-    heads = jnp.concatenate([head_mask(0), head_mask(1)] * 4, axis=0).astype(F32)
+    heads = jnp.concatenate([head_mask(0), head_mask(1)] * 8, axis=0)
     for y in range(4):
         at = slice(y * BLOCK, (y + 1) * BLOCK)
         new = dot(branch[y].reshape(TILE, D), weight[...], NT)
         for g in range(2):
             rows = slice(g * BLOCK, (g + 1) * BLOCK)
             grads[g, at, :] = new[rows].astype(BF)
-            for pair in range(2):
-                q = slice(pair * BLOCK, (pair + 1) * BLOCK)
-                both = slice(2 * pair, 2 * pair + 2)
-                mixed = attended[y, g, :, q].astype(F32) * new[rows, q].astype(BF).astype(F32)
-                mean[g, both, at] = lax.dot_general(
-                    heads, mixed, NT, precision=lax.Precision.HIGHEST
-                )[0:2]
+    for g in range(2):
+        for pair in range(2):
+            q = slice(pair * BLOCK, (pair + 1) * BLOCK)
+            mixed = attended[:, g, :, q].reshape(TOKENS, BLOCK).astype(F32)
+            mixed = mixed * grads[g, :, q].astype(F32)
+            high = mixed.astype(BF)
+            low = (mixed - high.astype(F32)).astype(BF)
+            both = dot(heads, high, NT) + dot(heads, low, NT)
+            mean[g, 2 * pair : 2 * pair + 2, :] = both[0:2]
     for one in trade:
         one.start()
     for one in out_in:
@@ -802,10 +805,9 @@
     scatter.send_late()
     back(0, 1)
 
-    @pl.loop(0, 8)
-    def _(i):
-        q = pl.ds(pl.multiple_of(i * TILE, TILE), TILE)
-        new = dot(attended[...].reshape(8 * BLOCK, HD), branch[:, :, :, q].reshape(8 * BLOCK, TILE), TN)
+    for i in range(2):
+        q = slice(i * 1024, (i + 1) * 1024)
+        new = dot(attended[...].reshape(8 * BLOCK, HD), branch[:, :, :, q].reshape(8 * BLOCK, 1024), TN)
         for x in range(4):
             for zl in range(2):
                 for a in range(2):
@@ -934,12 +936,16 @@
     y, c, up, opp, dn = ring()
     partner = {"zh": 1 - lax.axis_index("zh")}
     order = (opp, up, dn, y)
-    w_in = load([(w_hbm.at[:, k], w.at[k]) for k in range(3)], local)
-    block_in = load(
-        [(src.at[b], dst.at[b]) for b in order for src, dst in ((two_hbm, two), (grad_hbm, grad_all))],
-        local,
-        3,
-    )
+    first = order[0]
+    loads = load([(two_hbm.at[first], two.at[first])], local)
+    weights_in = [
+        load([(w_hbm.at[z, :, k], w.at[k, :, z]) for z in range(4)], local, 8 + 4 * k)
+        for k in range(3)
+    ]
+    loads += load([(grad_hbm.at[first], grad_all.at[first])], local, 1)
+    for i, b in enumerate(order[1:]):
+        pairs = [(two_hbm.at[b], two.at[b]), (grad_hbm.at[b], grad_all.at[b])]
+        loads += load(pairs, local, 2 + 2 * i)
     meet(list(ring_peers(up, dn, c)) + [partner])
     trade = [
         remote((send, recv), 0, queries, other_queries, partner),
@@ -949,15 +955,23 @@
         one.start()
     held = jnp.logical_or(lane(FP) >= BLOCK, y < 2)
     gate_lanes, up_lanes = pl.ds(0, FP), pl.ds(FP, FP)
-    waits = [w_in + block_in[0:2], block_in[2:4], block_in[4:6], block_in[6:8]]
     outs = []
 
+    def arrive(k):
+        loads.pop(0).wait()
+        if not outs:
+            for one in weights_in[k]:
+                one.wait()
+
     def partial(block, put):
-        for one in waits[len(outs)]:
-            one.wait()
+        arrive(0)
         a = two[block].reshape(TILE, D)
         gate = dot(a, w[0].reshape(D, FP), NN)
+        if not outs:
+            for one in weights_in[1]:
+                one.wait()
         up_proj = dot(a, w[1].reshape(D, FP), NN)
+        arrive(2)
         grad = dot(grad_all[block].reshape(TILE, D), w[2].reshape(D, FP), NN)
         sig = 1.0 / (1.0 + jnp.exp(-gate))
         active = gate * sig
@@ -972,14 +986,14 @@
         low_gate = both_grads[block, :, :, gate_lanes].reshape(TILE, FP)
         low_up = both_grads[block, :, :, up_lanes].reshape(TILE, FP)
         for i in range(4):
-            q, wide = slice(i * 512, (i + 1) * 512), slice(i * 4, (i + 1) * 4)
-            new = dot(low_gate, w[0, wide].reshape(512, FP), NT)
-            new = new + dot(low_up, w[1, wide].reshape(512, FP), NT)
+            q = slice(i * 512, (i + 1) * 512)
+            new = dot(low_gate, w[0, i].reshape(512, FP), NT)
+            new = new + dot(low_up, w[1, i].reshape(512, FP), NT)
             put(q, new.reshape(2, BLOCK, 512))
         low = inner[block].reshape(TILE, FP)
         for i in range(4):
-            q, wide = slice(i * 512, (i + 1) * 512), slice(i * 4, (i + 1) * 4)
-            new = dot(low, w[2, wide].reshape(512, FP), NT)
+            q = slice(i * 512, (i + 1) * 512)
+            new = dot(low, w[2, i].reshape(512, FP), NT)
             out_part[block, :, :, q] = new.astype(BF).reshape(2, BLOCK, 512)
 
         outs.extend(load([(out_part.at[block], out_hbm.at[block])], leave, len(outs)))
@@ -1003,7 +1017,11 @@
 
         for i in range(begin, begin + count):
             done.extend(
-                load([(mlp_part.at[pl.ds(2 * i, 2)], part_hbm.at[pl.ds(2 * i, 2)])], leave, 4 + i)
+                load(
+                    [(mlp_part.at[pl.ds(2 * i, 2)], part_hbm.at[pl.ds(i % 2 * 2, 2), i // 2])],
+                    leave,
+                    4 + i,
+                )
             )
 
     scatter = ring_scatter(partial, scratch, lambda: weight_grads(8))
@@ -1035,19 +1053,19 @@
             jax.ShapeDtypeStruct((2, TOKENS, HD), BF),
             jax.ShapeDtypeStruct((2, 8, TOKENS), F32),
             FULL,
-            jax.ShapeDtypeStruct((16, 3, BLOCK, FP), BF),
+            jax.ShapeDtypeStruct((4, 4, 3, BLOCK, FP), BF),
         ),
         in_specs=[ANY] * 3 + [VM] * 5,
         out_specs=(VM,) * 5 + (ANY, ANY),
         scratch_shapes=[
             pltpu.VMEM(block, BF),
             pltpu.VMEM(block, BF),
-            pltpu.VMEM((3, 16, BLOCK, FP), BF),
+            pltpu.VMEM((3, 4, 4, BLOCK, FP), BF),
             pltpu.VMEM(block, BF),
             pltpu.VMEM((16, 3, BLOCK, FP), BF),
             pltpu.VMEM((4, 2, BLOCK, FP), BF),
             pltpu.VMEM((4, 2, BLOCK, 2 * FP), BF),
-            pltpu.SemaphoreType.DMA((11,)),
+            pltpu.SemaphoreType.DMA((20,)),
             pltpu.SemaphoreType.DMA((12,)),
             pltpu.SemaphoreType.DMA((2,)),
             pltpu.SemaphoreType.DMA((2,)),
@@ -1169,17 +1187,16 @@
     qkv_scatter = PlaneScatter(part, *scratch[8:16])
     out_scatter.start()
     flat = joined_grad[...].reshape(TP * BLOCK, 3 * HD)
-    for one in token_in:
-        one.wait()
-
-    for i in range(4):
-        q = slice(i * 512, (i + 1) * 512)
-        new = dot(tokens[:, :, :, q].reshape(TP * BLOCK, 512), flat, TN).astype(BF)
-        part[i] = new.reshape(4, BLOCK, 3 * HD)
-
-    qkv_scatter.start()
-    weight_in.wait()
-    middle_in.wait()
+    def weight_grads():
+        for one in token_in:
+            one.wait()
+        for i in range(4):
+            q = slice(i * 512, (i + 1) * 512)
+            new = dot(tokens[:, :, :, q].reshape(TP * BLOCK, 512), flat, TN).astype(BF)
+            part[i] = new.reshape(4, BLOCK, 3 * HD)
+        qkv_scatter.start()
+        weight_in.wait()
+        middle_in.wait()
 
     def partial(block, put):
         a = joined_grad[block].reshape(2 * BLOCK, 3 * HD)
@@ -1194,6 +1211,7 @@
         )
         qkv_scatter.middle()
 
+    weight_grads()
     scatter = ring_scatter(partial, scratch[16:], between)
     sums[...] = jnp.zeros_like(sums)
 
@@ -1301,7 +1319,7 @@
 
 
 class PlaneGather:
-    COPIES = 12
+    COPIES = 14
 
     def __init__(self, src, full, local_sem, send, recv, x_first):
         sems = send, recv
@@ -1309,22 +1327,39 @@
         rest = (slice(None),) * (len(src.shape) - 1)
         x = lax.axis_index("x")
         z = lax.axis_index("zh") * 2 + lax.axis_index("zl")
-        self.one, self.two = [], []
-        every = slice(None)
+        self.one, self.two, self.three = [], [], []
+        every, low, high = slice(None), pl.ds(0, 2), pl.ds(2, 2)
+
+        def x_at(d):
+            return lax.rem(x + d, 4)
+
+        def z_at(d):
+            return lax.rem(z + d, 4)
+
+        def to_x(d):
+            return {"x": x_at(d)}
+
+        def to_z(d):
+            return {"zh": z_at(d) // 2, "zl": lax.rem(z_at(d), 2)}
+
+        def pass_on(i, at, peer):
+            return remote(sems, i, full.at[at], full.at[at], peer)
+
+        if x_first:
+            at = rest + (a,)
+            for d in range(1, 4):
+                self.one.append(remote(sems, d - 1, src.at[at], full.at[(x, z) + at], to_x(d)))
+            self.two.append(pass_on(6, (every, z) + at, to_z(1)))
+            self.two.append(pass_on(7, (every, z) + at, to_z(3)))
+            self.three.append(pass_on(8, (low, z_at(3)) + at, to_z(1)))
+            self.three.append(pass_on(9, (high, z_at(1)) + at, to_z(3)))
+        at = rest + (b,)
         for d in range(1, 4):
-            k = d - 1
-            z_to = lax.rem(z + d, 4)
-            to_x = {"x": lax.rem(x + d, 4)}
-            to_z = {"zh": z_to // 2, "zl": lax.rem(z_to, 2)}
-            if x_first:
-                at = rest + (a,)
-                self.one.append(remote(sems, k, src.at[at], full.at[(x, z) + at], to_x))
-                row = full.at[(every, z) + at]
-                self.two.append(remote(sems, 6 + k, row, row, to_z))
-            at = rest + (b,)
-            self.one.append(remote(sems, 3 + k, src.at[at], full.at[(x, z) + at], to_z))
-            row = full.at[(x, every) + at]
-            self.two.append(remote(sems, 9 + k, row, row, to_x))
+            self.one.append(remote(sems, 2 + d, src.at[at], full.at[(x, z) + at], to_z(d)))
+        self.two.append(pass_on(10, (x, every) + at, to_x(1)))
+        self.two.append(pass_on(11, (x, every) + at, to_x(3)))
+        self.three.append(pass_on(12, (x_at(3), low) + at, to_x(1)))
+        self.three.append(pass_on(13, (x_at(1), high) + at, to_x(3)))
         self.here = pltpu.make_async_copy(src, full.at[x, z], local_sem)
 
     def start(self):
@@ -1339,10 +1374,15 @@
         for copy in self.two:
             copy.start()
 
+    def forward(self):
+        for copy, later in zip(self.two, self.three):
+            copy.wait_recv()
+            later.start()
+
     def finish(self):
-        for copy in self.two:
+        for copy in self.three:
             copy.wait_recv()
-        for copy in self.one + self.two:
+        for copy in self.one + self.two + self.three:
             copy.wait_send()
 
 
@@ -1365,15 +1405,20 @@
     return pl.ds(pl.multiple_of(start, BLOCK), n)
 
 
-def spread_gains(small_all, gains, shift, rank):
+def spread_gains(small_all, gains, entries):
     rows = small_all[...].reshape(BLOCK, BLOCK)
     source = lax.broadcasted_iota(jnp.int32, (BLOCK, 1), 0)
     f = lane(D)
     mine = (f // 16) == source
-    for i in range(4):
+    for i in entries:
         pick = (source == 16 * i + lax.rem(f, 16)).astype(F32)
         value = jnp.dot(rows, pick, preferred_element_type=F32)
         gains[i : i + 1, :] = jnp.sum(jnp.where(mine, value, 0.0), axis=0, keepdims=True)
+
+
+def spread_shift(small_all, shift, rank):
+    rows = small_all[...].reshape(BLOCK, BLOCK)
+    source = lax.broadcasted_iota(jnp.int32, (BLOCK, 1), 0)
     core = lax.rem(source, 2)
     y = lax.rem(source // 2, 4)
     zl = lax.rem(source // 8, 2)
@@ -1405,6 +1450,7 @@
     hidden,
     full,
     own,
+    normed,
     qkv_rows,
     local,
     send,
@@ -1434,7 +1480,7 @@
         keep.append(pltpu.make_async_copy(src, dst, local.at[1 + i]))
         src = w.at[:, lanes_at(first_lane(me), FP)]
         keep.append(pltpu.make_async_copy(src, mlp_rows.at[i, me], local.at[4 + i]))
-    for one in tiny + qkv + keep:
+    for one in tiny + qkv + mlp + keep:
         one.start()
     last = 7 * N_TP + N_XZ
     for one in tiny:
@@ -1450,26 +1496,31 @@
         one.wait()
     plane = PlaneGather(qkv_rows, qkv_full, *sems[:3], 3 * HD // 2)
     plane.start()
-    for one in mlp:
-        one.start()
     swap_start(split, w_out, out_rows, local.at[7], (send, recv), last)
-    for one in wide:
-        one.wait()
-    gains[...] = jnp.zeros_like(gains)
-    spread_gains(small_all, gains, shift, me)
 
     def norm(r):
         row = permute_rows(hidden_in[r, :].astype(F32))
         hidden[r, :] = row.astype(BF)
-        normed, _ = layer_norm(row)
-        own[r, :] = (normed * gains[0:1, :] + gains[1:2, :]).astype(BF)
+        normed[r, :], _ = layer_norm(row)
 
     rows_loop(BLOCK, 16, norm)
+    gains[...] = jnp.zeros_like(gains)
+    for one in wide:
+        one.wait()
+    spread_gains(small_all, gains, (0, 1))
+
+    def scale(r):
+        own[r, :] = (normed[r, :] * gains[0:1, :] + gains[1:2, :]).astype(BF)
+
+    rows_loop(BLOCK, 16, scale)
     gather = RingGather(own, full, sems[3], sems[4:])
     gather.start()
     plane.middle()
     gather.forward()
+    spread_gains(small_all, gains, (2, 3))
+    spread_shift(small_all, shift, me)
     gather.share()
+    plane.forward()
     gather.share_far()
     for one in mlp:
         one.wait()
@@ -1496,6 +1547,7 @@
         out_specs=(VM, VM, VM, ANY, ANY, ANY, VM, ANY),
         scratch_shapes=[
             pltpu.VMEM((BLOCK, D), BF),
+            pltpu.VMEM((BLOCK, D), F32),
             pltpu.VMEM((TP, 16, 3 * HD), BF),
             pltpu.SemaphoreType.DMA((8,)),
             pltpu.SemaphoreType.DMA((n,)),
@@ -1515,19 +1567,13 @@
     qkv,
     mlp,
     out,
-    small,
-    qkv_grad,
-    gate_grad,
-    up_grad,
-    down_grad,
-    out_grad,
-    terms,
-    terms_in,
-    own,
     small_all,
     qkv_all,
     mlp_all,
     out_all,
+    terms,
+    terms_in,
+    own,
     local,
     *sems,
 ):
@@ -1565,7 +1611,7 @@
     dst = mlp_all.at[:, :, lanes_at(first_lane(me), BLOCK)]
     keep_tile = pltpu.make_async_copy(mlp.at[:, me, :, tile], dst, local.at[2])
     first_four = me < 4
-    for one in wide + big + keep:
+    for one in big[0::2]:
         one.start()
 
     @pl.when(first_four)
@@ -1573,6 +1619,9 @@
         keep_tile.start()
         for one in extra:
             one.start()
+
+    for one in wide + big[1::2] + keep:
+        one.start()
 
     last = base + 3 * N_TP
     swap_start(split, out, out_all, local.at[3], sems, last)
@@ -1603,44 +1652,28 @@
         for one in extra:
             one.wait_send()
 
-    for t in range(TP):
-        for i in range(3):
-            first = i * D + (t % 2 * 4 + t // 2) * HD
-            qkv_grad[:, first : first + HD] = qkv_all[t, :, i * HD : (i + 1) * HD].astype(F32)
-    gate_grad[...] = mlp_all[0].astype(F32)
-    up_grad[...] = mlp_all[1].astype(F32)
-    down_grad[...] = mlp_all[2].astype(F32)
     swap_wait(split, out, out_all, local.at[3], sems, last)
-    out_grad[...] = restore_rows(out_all[...].astype(F32))
     for one in tiny:
         one.wait()
     small_all[me] = own[...]
-    small[...] = small_all[...]
 
 
 def collect(one_sums, two_sums, shift, qkv, mlp, out, cid):
     n = N_XZ + 4 * N_TP + 1
-    wide = jax.ShapeDtypeStruct((16, FF), F32)
     return pl.pallas_call(
         kernel_collect,
         out_shape=(
             jax.ShapeDtypeStruct((TP, 16, BLOCK), F32),
-            jax.ShapeDtypeStruct((16, 3 * D), F32),
-            wide,
-            wide,
-            wide,
-            jax.ShapeDtypeStruct((16, D), F32),
+            jax.ShapeDtypeStruct((TP, 16, 3 * HD), BF),
+            jax.ShapeDtypeStruct((3, 16, FF), BF),
+            jax.ShapeDtypeStruct((16, D), BF),
         ),
         in_specs=[VM] * 3 + [ANY] * 3,
-        out_specs=(VM,) * 6,
+        out_specs=(VM, ANY, ANY, ANY),
         scratch_shapes=[
             pltpu.VMEM((16, 16, BLOCK), F32),
             pltpu.VMEM((16, 16, BLOCK), F32),
             pltpu.VMEM((16, BLOCK), F32),
-            pltpu.VMEM((TP, 16, BLOCK), F32),
-            pltpu.VMEM((TP, 16, 3 * HD), BF),
-            pltpu.VMEM((3, 16, FF), BF),
-            pltpu.VMEM((16, D), BF),
             pltpu.SemaphoreType.DMA((4,)),
             pltpu.SemaphoreType.DMA((n,)),
             pltpu.SemaphoreType.DMA((n,)),
@@ -1648,6 +1681,64 @@
         compiler_params=params(cid),
         name="collect",
     )(one_sums, two_sums, shift, qkv, mlp, out)
+
+
+def kernel_finish(
+    qkv_hbm,
+    mlp_hbm,
+    out_hbm,
+    hidden_hbm,
+    grad_hbm,
+    qkv_grad,
+    gate,
+    up,
+    down,
+    out,
+    hidden_out,
+    input_grad,
+    qkv_all,
+    mlp_all,
+    out_all,
+    local,
+):
+    pairs = [(qkv_hbm, qkv_all), (mlp_hbm, mlp_all), (out_hbm, out_all)]
+    pairs += [(hidden_hbm, hidden_out), (grad_hbm, input_grad)]
+    for one in load(pairs, local):
+        one.wait()
+    for t in range(TP):
+        for i in range(3):
+            first = i * D + (t % 2 * 4 + t // 2) * HD
+            qkv_grad[:, first : first + HD] = qkv_all[t, :, i * HD : (i + 1) * HD].astype(F32)
+    gate[...] = mlp_all[0].astype(F32)
+    up[...] = mlp_all[1].astype(F32)
+    down[...] = mlp_all[2].astype(F32)
+    out[...] = restore_rows(out_all[...].astype(F32))
+
+
+def finish(qkv_all, mlp_all, out_all, hidden, grad):
+    wide = jax.ShapeDtypeStruct((16, FF), F32)
+    return pl.pallas_call(
+        kernel_finish,
+        out_shape=(
+            jax.ShapeDtypeStruct((16, 3 * D), F32),
+            wide,
+            wide,
+            wide,
+            jax.ShapeDtypeStruct((16, D), F32),
+            jax.ShapeDtypeStruct((BLOCK, D), BF),
+            jax.ShapeDtypeStruct((BLOCK, D), F32),
+        ),
+        in_specs=[ANY] * 5,
+        out_specs=(VM,) * 7,
+        scratch_shapes=[
+            pltpu.VMEM((TP, 16, 3 * HD), BF),
+            pltpu.VMEM((3, 16, FF), BF),
+            pltpu.VMEM((16, D), BF),
+            pltpu.SemaphoreType.DMA((5,)),
+        ],
+        compiler_params=pltpu.CompilerParams(vmem_limit_bytes=60 * 1024 * 1024),
+        name="finish",
+    )(qkv_all, mlp_all, out_all, hidden, grad)
 
 
 def body(
@@ -1682,7 +1773,7 @@
         small.reshape(1, BLOCK), hidden_in[0], w_qkv, w_gate, w_up, w_down, w_out, 0
     )
     qkv_full = qkv_full.reshape(D, 3 * HD)
-    mlp_full = lax.all_gather(mlp_rows.reshape(3, BLOCK, FP), XZ, axis=0, tiled=False)
+    mlp_full = lax.all_gather(mlp_rows.reshape(3, BLOCK, FP), ZX, axis=0, tiled=False)
     small_all = small_all.reshape(BLOCK, BLOCK)
 
     plan = lax.dynamic_slice_in_dim(small_all, xz * TP + y * 2, 2, 0)[:, 112:122].astype(jnp.int32)
@@ -1698,10 +1789,10 @@
         table, one_all, qkv_full, shift, cotangent[0], out_rows, hidden, gains, 6
     )
     middle_grad, two_sums, branch, other_queries, other_lse, mlp_out, mlp_part = mlp(
-        two_all, grad_all, mlp_full, middle, grad_out, gains, queries, lse, 3
+        two_all, grad_all, mlp_full.reshape(4, 4, 3, BLOCK, FP), middle, grad_out, gains, queries, lse, 3
     )
     mlp_sum = lax.psum_scatter(
-        mlp_part.reshape(16 * 3 * BLOCK, FP), XZ, scatter_dimension=0, tiled=True
+        mlp_part.reshape(16 * 3 * BLOCK, FP), ZX, scatter_dimension=0, tiled=True
     )
     joined_grad, out_part, hidden_out = attend_back(
         table,
@@ -1721,7 +1812,7 @@
         joined_grad, qkv_full, hidden, middle_grad, gains, one_all, out_part, 4
     )
 
-    small_sum, qkv_grad, gate_sum, up_sum, down_sum, out_grad = collect(
+    small_sum, qkv_all, mlp_all, out_all = collect(
         one_sums,
         two_sums,
         shift_sum,
@@ -1729,6 +1820,9 @@
         mlp_sum.reshape(3, TP, 16, FP),
         out_sum,
         5,
+    )
+    qkv_grad, gate_sum, up_sum, down_sum, out_grad, hidden_out, input_grad = finish(
+        qkv_all, mlp_all, out_all, hidden_out, input_grad
     )
     vectors = jnp.sum(small_sum[:, :4], axis=0)
     vectors = lax.dynamic_slice_in_dim(vectors, (y * 2 + core) * 16, 16, 1)

time: 351 us -> 340 us (0.969)
  local copies, waits for them, and re-layouts: 10.8 us -> 3.06 us
    unnamed x20 -> x3, local copies, waits for them, and re-layouts: 8.02 us -> 0.29 us
    pallas_call x1, Pallas kernels: 69 us -> 64.8 us  [attend_back(): pl.pallas_call(kernel_attend_back, out_shape=(jax.ShapeDtypeStruct((4, 2,...]
where the time goes in v3:
time: 340 us; the launch traced here: 337 us
  Pallas kernels  309 us (91%)
  between operations  14.4 us (4%)
  waiting for transfers between devices  6.36 us (2%)
  other arithmetic  4.18 us (1%)
    pallas_call x1, Pallas kernels, attend(): pl.pallas_call(kernel_attend, out_shape=(jax.ShapeDtypeStruct((2, TOKENS,...  84.7 us
    pallas_call x1, Pallas kernels, attend_back(): pl.pallas_call(kernel_attend_back, out_shape=(jax.ShapeDtypeStruct((4, 2,...  64.8 us
    pallas_call x1, Pallas kernels, mlp(): pl.pallas_call(kernel_mlp, out_shape=(jax.ShapeDtypeStruct((BLOCK, D), F3...  49.2 us
    pallas_call x1, Pallas kernels, qkv_back(): pl.pallas_call(kernel_qkv_back, out_shape=(jax.ShapeDtypeStruct((BLOCK, D...  44.5 us
    pallas_call x1, Pallas kernels, front(): pl.pallas_call(kernel_front, out_shape=(jax.ShapeDtypeStruct((16, TP, 1,...  42.6 us
    pallas_call x1, Pallas kernels, collect(): pl.pallas_call(kernel_collect, out_shape=(jax.ShapeDtypeStruct((TP, 16, B...  19.1 us
  transfers between devices with their start and end apart: 2, of which 1 were waited for; matrix products, arithmetic and copies ran while one was open for 1% of the time, Pallas kernels for 58%

profile of v3, /device:TPU:1, one launch (start us, length us, event | category | flops | bytes accessed | tf_op | source)
XLA Modules:
  0.0 337.1 jit_solution(12770448912300743279)
XLA Ops:
  7.2 0.0 all-gather.2.cloned.1.call-start
  7.2 0.7 convert_bitcast_fusion.1
  7.9 0.7 convert_bitcast_fusion
  8.5 1.3 add_bitcast_fusion.small
  9.9 42.6 %front.1 = (f32[16,8,1,128]{3,2,1,0:T(1,128)}, f32[8,2048]{1,0:T(8,128)}, f32[1,768]{1,0:T(1,128)}, bf16[4,4,8,16,768]{4,3,2,1,0:T(8,128)(2,1)}, bf16[3,8,16,768...) custom-call(f32[1,128]{1,0:T(1,128)} %add_bitcast_fusion.small, ...), custom_call_target="tpu_custom_call" | custom-call | tf_op jit(solution)/shard_map/front/pallas_call | solution.py:1534
  52.5 0.0 all-gather.2.cloned.1.call-update
  52.5 0.6 reduce-scatter.2.cloned.1.call-start
  53.1 0.7 constant_dynamic-slice_fusion.4
  53.8 0.1 slice.35
  53.9 0.1 copy.37
  54.0 0.1 copy.38
  54.1 0.1 copy.39
  54.2 0.1 fusion
  54.3 0.1 compare_select_fusion
  54.4 0.6 pad_add_fusion.table
  55.0 84.7 %attend.1 = (bf16[2,512,256]{2,1,0:T(8,128)(2,1)}, bf16[2,2,1024,256]{3,2,1,0:T(8,128)(2,1)}, f32[2,8,512]{2,1,0:T(8,128)}, bf16[4,2,128,256]{3,2,1,0:T(8,128)(2...) custom-call(s32[2,3,8]{2,1,0:T(4,128)} %pad_add_fusion.table, ...), custom_call_target="tpu_custom_call" | custom-call | tf_op jit(solution)/shard_map/attend/pallas_call | solution.py:625
  139.7 6.3 %all-gather.2.cloned.1.call-done = bf16[16,3,128,768]{3,2,1,0:T(8,128)(2,1)} async-done(((bf16[1,3,128,768]{3,2,1,0:T(8,128)(2,1)}), bf16[16,3,128,768]{3,2,1,0:T(8,128)(2,1)}) %all-gather.2.cloned.1.call-update) | async-done | bytes 9437200 | tf_op jit(solution)/shard_map/all_gather | solution.py:1776
  146.0 49.2 %mlp.1 = (f32[128,2048]{1,0:T(8,128)}, f32[8,2048]{1,0:T(8,128)}, bf16[128,2048]{1,0:T(8,128)(2,1)}, bf16[2,512,256]{2,1,0:T(8,128)(2,1)}, f32[2,8,512]{2,1,0:T(...) custom-call(bf16[4,2,128,2048]{3,2,1,0:T(8,128)(2,1)} %get-tuple-element.62.two_hbm, ...), custom_call_target="tpu_custom_call" | custom-call | tf_op jit(solution)/shard_map/mlp/pallas_call | solution.py:1047
  195.2 0.0 reduce-scatter.2.cloned.1.call-update
  195.3 64.8 %attend_back.1 = (bf16[4,2,128,768]{3,2,1,0:T(8,128)(2,1)}, bf16[16,16,2048]{2,1,0:T(8,128)(2,1)}, bf16[128,2048]{1,0:T(8,128)(2,1)}) custom-call(s32[2,3,8]{2,1,0:T(4,128)} %pad_add_fusion.table, bf16[128,2048]{1,0:T(8,128)(2,1)} %get-tuple-element.69.branch_own, bf16[4,4,16,2048]{3,2,1,0:T(8,128)(2,1)} %get-tuple-element.70.gathered, ...), custom_call_target="tpu_custom_call" | custom-call | tf_op jit(solution)/shard_map/attend_back/pallas_call | solution.py:862
  260.1 44.5 %qkv_back.1 = (f32[128,2048]{1,0:T(8,128)}, f32[8,2048]{1,0:T(8,128)}, f32[8,768]{1,0:T(8,128)}, bf16[128,768]{1,0:T(8,128)(2,1)}, bf16[16,2048]{1,0:T(8,128)(2,1)}) custom-call(bf16[4,2,128,768]{3,2,1,0:T(8,128)(2,1)} %get-tuple-element.76.joined_grad, bf16[2048,768]{1,0:T(8,128)(2,1)} %bitcast.37, bf16[128,2048]{1,0:T(8,128)(2,1)} %get-tuple-element.60.hidden, ...), custom_call_target="tpu_custom_call" | custom-call | tf_op jit(solution)/shard_map/qkv_back/pallas_call | solution.py:1234
  304.7 0.0 reduce-scatter.2.cloned.1.call-done
  304.7 19.1 %collect.1 = (f32[8,16,128]{2,1,0:T(8,128)}, bf16[8,16,768]{2,1,0:T(8,128)(2,1)}, bf16[3,16,5632]{2,1,0:T(8,128)(2,1)}, bf16[16,2048]{1,0:T(8,128)(2,1)}) custom-call(f32[8,2048]{1,0:T(8,128)} %get-tuple-element.79.one_sums, f32[8,2048]{1,0:T(8,128)} %get-tuple-element.80.two_sums, f32[8,768]{1,0:T(8,128)} %get-tuple-element.81.shift, ...), custom_call_target="tpu_custom_call" | custom-call | tf_op jit(solution)/shard_map/collect/pallas_call | solution.py:1663
  323.9 0.8 slice_reduce_fusion
  324.6 0.8 slice.44
  325.4 0.1 constant_dynamic-slice_fusion.1
  325.5 0.5 slice_bitcast_fusion.1
  326.0 0.1 reshape.288
  326.1 0.5 fusion.1
  326.7 3.4 %finish.1 = (f32[16,6144]{1,0:T(8,128)}, f32[16,5632]{1,0:T(8,128)}, f32[16,5632]{1,0:T(8,128)}, f32[16,5632]{1,0:T(8,128)}, f32[16,2048]{1,0:T(8,128)}, /*index=5*/bf16[128,2048]{1,0:T(8,128)(2,1)}, f32[128,2048]{1,0:T(8,128)}) custom-call(bf16[8,16,768]{2,1,0:T(8,128)(2,1)} %get-tuple-element.85.qkv_hbm, bf16[3,16,5632]{2,1,0:T(8,128)(2,1)} %get-tuple-element.86.mlp_hbm, ...), custom_call_target="tpu_custom_call" | custom-call | tf_op jit(solution)/shard_map/finish/pallas_call | solution.py:1720
  (6 shorter events, 0.1 us)
Async XLA Ops:
  7.2 138.8 %all-gather.2.cloned.1.call-start = ((), (), s32[]{:S(2)}) async-start(), calls=%async_computation.1 | async-start | bytes 10027008 | tf_op jit(solution)/shard_map/all_gather | solution.py:1776
  52.5 252.2 %reduce-scatter.2.cloned.1.call-start = ((), (), s32[]{:S(2)}) async-start(), calls=%async_computation.2 | async-start | bytes 10027008 | tf_op jit(solution)/shard_map/reduce_scatter | solution.py:1794
Sparse Core Ops, SparseCore 0:
  52.7 93.3 all-gather.1
  195.4 105.7 reduce-scatter.1

commit v4 on v3

--- a/solution.py
+++ b/solution.py
@@ -713,8 +713,9 @@
         one.start()
     order_out(gathered, weight)
     trade = [
-        remote((send, recv), 0, grads, other_grads, partner),
-        remote((send, recv), 1, mean, other_mean, partner),
+        remote((send, recv), 0, mean, other_mean, partner),
+        remote((send, recv), 1, grads.at[0], other_grads.at[0], partner),
+        remote((send, recv), 2, grads.at[1], other_grads.at[1], partner),
     ]
 
     def recompute(part, g):
@@ -814,10 +815,6 @@
                     row = x * 64 + zl * 32 + a * 16
                     out_part[x * 4 + a * 2 + zl, :, q] = new[row : row + 16].astype(BF)
 
-    for one in trade:
-        one.wait_recv()
-    back(1, 0)
-    back(1, 1)
     scatter.wait()
     middle_in.wait()
 
@@ -825,20 +822,31 @@
         hidden_out[r, :] = restore_rows(middle[r, :] + scatter.total(r)).astype(BF)
 
     rows_loop(BLOCK, 16, add)
-    for g in range(2):
-
+
+    def turn_back(g, queries_part):
         @pl.loop(0, 4)
-        def _(y, g=g):
+        def _(y):
             at = pl.ds(pl.multiple_of(y * BLOCK, BLOCK), BLOCK)
             cosine, sine = turn_tables(table[g, 0, y])
             for pair in range(2):
                 q = slice(pair * BLOCK, (pair + 1) * BLOCK)
-                new = dq[g, q, at].T * SCALE
-                joined_grad[y, g, :, q] = turn(new, cosine, sine, -1.0).astype(BF)
-                joined_grad[y, g, :, HD + pair * BLOCK : HD + (pair + 1) * BLOCK] = turn(
-                    dkv[0, g, at, q], cosine, sine, -1.0
-                ).astype(BF)
-            joined_grad[y, g, :, 2 * HD :] = dkv[1, g, at, :].astype(BF)
+                if queries_part:
+                    new = dq[g, q, at].T * SCALE
+                    joined_grad[y, g, :, q] = turn(new, cosine, sine, -1.0).astype(BF)
+                else:
+                    joined_grad[y, g, :, HD + pair * BLOCK : HD + (pair + 1) * BLOCK] = turn(
+                        dkv[0, g, at, q], cosine, sine, -1.0
+                    ).astype(BF)
+            if not queries_part:
+                joined_grad[y, g, :, 2 * HD :] = dkv[1, g, at, :].astype(BF)
+
+    for g in range(2):
+        turn_back(g, True)
+    trade[0].wait_recv()
+    for g in range(2):
+        trade[1 + g].wait_recv()
+        back(1, g)
+        turn_back(g, False)
 
     for one in trade:
         one.wait_send()
@@ -882,8 +890,8 @@
             pltpu.VMEM((2, 8, TOKENS), F32),
             pltpu.VMEM((2, 8, TOKENS), F32),
             pltpu.VMEM((2, 2, TOKENS, HD), F32),
-            pltpu.SemaphoreType.DMA((2,)),
-            pltpu.SemaphoreType.DMA((2,)),
+            pltpu.SemaphoreType.DMA((3,)),
+            pltpu.SemaphoreType.DMA((3,)),
         ]
         + AG_SCRATCH[1:]
         + RS_SCRATCH[2:],
@@ -1077,74 +1085,104 @@
 
 
 class PlaneScatter:
-    COPIES = 12
-
-    def __init__(self, part, a_in, b_in, a_mid, b_mid, a_last, b_last, send, recv):
-        self.refs = part, a_in, b_in, a_mid, b_mid, a_last, b_last
-        sems = send, recv
+    COPIES = 18
+
+    def __init__(self, part, *scratch):
+        near, far, relay, mid, last = (scratch[2 * i : 2 * i + 2] for i in range(5))
+        sems = scratch[10:12]
+        self.part, self.near, self.far, self.passed, self.mid, self.last = (
+            part,
+            near,
+            far,
+            relay,
+            mid,
+            last,
+        )
         half = part.shape[-1] // 2
         self.lanes = pl.ds(0, half), pl.ds(half, half)
-        self.x = lax.axis_index("x")
-        self.z = lax.axis_index("zh") * 2 + lax.axis_index("zl")
-        self.one, self.two = [], []
-        for d in range(1, 4):
-            x = lax.rem(self.x + d, 4)
-            z = lax.rem(self.z + d, 4)
-            to_x = {"x": x}
-            to_z = {"zh": z // 2, "zl": lax.rem(z, 2)}
-            a, b = self.lanes
-            k = d - 1
-            self.one.append(remote(sems, k, part.at[:, z, :, a], a_in.at[k], to_z))
-            self.one.append(remote(sems, 3 + k, part.at[x, :, :, b], b_in.at[k], to_x))
-            self.two.append(remote(sems, 6 + k, a_mid.at[x], a_last.at[k], to_x))
-            self.two.append(remote(sems, 9 + k, b_mid.at[z], b_last.at[k], to_z))
+        x = lax.axis_index("x")
+        z = lax.axis_index("zh") * 2 + lax.axis_index("zl")
+        self.place = z, x
+        low, high = pl.ds(0, 2), pl.ds(2, 2)
+        self.low, self.high = low, high
+
+        def to_x(d):
+            return {"x": lax.rem(x + d, 4)}
+
+        def to_z(d):
+            there = lax.rem(z + d, 4)
+            return {"zh": there // 2, "zl": lax.rem(there, 2)}
+
+        self.first, self.late, self.two = [], [], []
+        for k in range(2):
+            first_to, second_to = (to_z, to_x) if k == 0 else (to_x, to_z)
+            base = 9 * k
+            up, dn = first_to(1), first_to(3)
+            pieces = (
+                (self.piece(k, low, 2), far[k].at[0], up),
+                (self.piece(k, high, 2), far[k].at[1], dn),
+                (self.piece(k, high, 1), near[k].at[0, high], up),
+                (self.piece(k, low, 3), near[k].at[1, low], dn),
+            )
+            for i, (src, dst, peer) in enumerate(pieces):
+                self.first.append(remote(sems, base + i, src, dst, peer))
+            self.late.append(remote(sems, base + 4, relay[k].at[0], near[k].at[0, low], up))
+            self.late.append(remote(sems, base + 5, relay[k].at[1], near[k].at[1, high], dn))
+            for d in range(1, 4):
+                there = lax.rem(self.place[1 - k] + d, 4)
+                copy = remote(sems, base + 5 + d, mid[k].at[there], last[k].at[d - 1], second_to(d))
+                self.two.append(copy)
+
+    def piece(self, k, rest, d):
+        there = lax.rem(self.place[k] + d, 4)
+        at = (rest, there) if k == 0 else (there, rest)
+        return self.part.at[at + (slice(None), self.lanes[k])]
 
     def start(self):
-        for copy in self.one:
+        for copy in self.first:
             copy.start()
 
+    def relay(self):
+        for k in range(2):
+            for i, (rest, d) in enumerate(((self.low, 1), (self.high, 3))):
+                self.first[4 * k + i].wait_recv()
+                self.passed[k][i] = (
+                    self.piece(k, rest, d)[...].astype(F32) + self.far[k][i].astype(F32)
+                ).astype(BF)
+                self.late[2 * k + i].start()
+
     def middle(self):
-        part, a_in, b_in, a_mid, b_mid, _, _ = self.refs
-        for copy in self.one:
-            copy.wait_recv()
-        a, b = self.lanes
-
-        @pl.loop(0, 4)
-        def _(i):
-            a_mid[i] = (
-                part[i, self.z, :, a].astype(F32) + jnp.sum(a_in[:, i].astype(F32), axis=0)
-            ).astype(BF)
-            b_mid[i] = (
-                part[self.x, i, :, b].astype(F32) + jnp.sum(b_in[:, i].astype(F32), axis=0)
-            ).astype(BF)
-
-        for copy in self.two:
-            copy.start()
+        for k in range(2):
+            for copy in self.first[4 * k + 2 : 4 * k + 4] + self.late[2 * k : 2 * k + 2]:
+                copy.wait_recv()
+
+            @pl.loop(0, 4)
+            def _(i, k=k):
+                at = (i, self.place[0]) if k == 0 else (self.place[1], i)
+                own = self.part[at + (slice(None), self.lanes[k])].astype(F32)
+                near = self.near[k][0, i].astype(F32) + self.near[k][1, i].astype(F32)
+                self.mid[k][i] = (own + near).astype(BF)
+
+            for copy in self.two[3 * k : 3 * k + 3]:
+                copy.start()
 
     def finish(self, out):
-        _, _, _, a_mid, b_mid, a_last, b_last = self.refs
         for copy in self.two:
             copy.wait_recv()
-        a, b = self.lanes
-        out[:, a] = (
-            a_mid[self.x].astype(F32) + jnp.sum(a_last[...].astype(F32), axis=0)
-        ).astype(BF)
-        out[:, b] = (
-            b_mid[self.z].astype(F32) + jnp.sum(b_last[...].astype(F32), axis=0)
-        ).astype(BF)
-        for copy in self.one + self.two:
+        for k in range(2):
+            out[:, self.lanes[k]] = (
+                self.mid[k][self.place[1 - k]].astype(F32)
+                + jnp.sum(self.last[k][...].astype(F32), axis=0)
+            ).astype(BF)
+        for copy in self.first + self.late + self.two:
             copy.wait_send()
 
 
 def plane_scratch(rows, lanes):
     half = lanes // 2
-    return [
-        pltpu.VMEM((3, 4, rows, half), BF),
-        pltpu.VMEM((3, 4, rows, half), BF),
-        pltpu.VMEM((4, rows, half), BF),
-        pltpu.VMEM((4, rows, half), BF),
-        pltpu.VMEM((3, rows, half), BF),
-        pltpu.VMEM((3, rows, half), BF),
+    shapes = [(2, 4, rows, half), (2, 2, rows, half), (2, 2, rows, half), (4, rows, half)]
+    shapes += [(3, rows, half)]
+    return [pltpu.VMEM(shape, BF) for shape in shapes for _ in range(2)] + [
         pltpu.SemaphoreType.DMA((PlaneScatter.COPIES,)),
         pltpu.SemaphoreType.DMA((PlaneScatter.COPIES,)),
     ]
@@ -1183,8 +1221,8 @@
     weight_in, middle_in = load([(weight_hbm, weight), (middle_hbm, middle_grad)], local, 4)
     y, c, up, opp, dn = ring()
     meet(list(ring_peers(up, dn, c)) + plane_peers())
-    out_scatter = PlaneScatter(out_part, *scratch[:8])
-    qkv_scatter = PlaneScatter(part, *scratch[8:16])
+    out_scatter = PlaneScatter(out_part, *scratch[:12])
+    qkv_scatter = PlaneScatter(part, *scratch[12:24])
     out_scatter.start()
     flat = joined_grad[...].reshape(TP * BLOCK, 3 * HD)
     def weight_grads():
@@ -1204,15 +1242,9 @@
             q = slice(i * 512, (i + 1) * 512)
             put(q, dot(a, weight[q, :], NT).reshape(2, BLOCK, 512))
 
-    def between():
-        out_scatter.middle()
-        shift_sum[...] = jnp.broadcast_to(
-            jnp.sum(flat.astype(F32), axis=0, keepdims=True), shift_sum.shape
-        )
-        qkv_scatter.middle()
-
     weight_grads()
-    scatter = ring_scatter(partial, scratch[16:], between)
+    out_scatter.relay()
+    scatter = ring_scatter(partial, scratch[24:], qkv_scatter.relay)
     sums[...] = jnp.zeros_like(sums)
 
     def back(r):
@@ -1225,6 +1257,11 @@
         sums[1:2, :] += jnp.sum(row, axis=0, keepdims=True)
 
     rows_loop(BLOCK, 16, back)
+    out_scatter.middle()
+    qkv_scatter.middle()
+    shift_sum[...] = jnp.broadcast_to(
+        jnp.sum(flat.astype(F32), axis=0, keepdims=True), shift_sum.shape
+    )
     scatter.finish()
     out_scatter.finish(out_sum)
     qkv_scatter.finish(qkv_sum)

time: 340 us -> 335 us (0.985)
  Pallas kernels: 309 us -> 303 us
    pallas_call x1, Pallas kernels: 64.8 us -> 59.6 us  [attend_back(): pl.pallas_call(kernel_attend_back, out_shape=(jax.ShapeDtypeStruct((4, 2,...]
where the time goes in v4:
time: 335 us; the launch traced here: 332 us
  Pallas kernels  303 us (90%)
  between operations  14.4 us (4%)
  waiting for transfers between devices  6.36 us (2%)
  other arithmetic  4.18 us (1%)
    pallas_call x1, Pallas kernels, attend(): pl.pallas_call(kernel_attend, out_shape=(jax.ShapeDtypeStruct((2, TOKENS,...  84.7 us
    pallas_call x1, Pallas kernels, attend_back(): pl.pallas_call(kernel_attend_back, out_shape=(jax.ShapeDtypeStruct((4, 2,...  59.6 us
    pallas_call x1, Pallas kernels, mlp(): pl.pallas_call(kernel_mlp, out_shape=(jax.ShapeDtypeStruct((BLOCK, D), F3...  49.2 us
    pallas_call x1, Pallas kernels, qkv_back(): pl.pallas_call(kernel_qkv_back, out_shape=(jax.ShapeDtypeStruct((BLOCK, D...  47.5 us
    pallas_call x1, Pallas kernels, front(): pl.pallas_call(kernel_front, out_shape=(jax.ShapeDtypeStruct((16, TP, 1,...  42.6 us
    pallas_call x1, Pallas kernels, collect(): pl.pallas_call(kernel_collect, out_shape=(jax.ShapeDtypeStruct((TP, 16, B...  16 us
  transfers between devices with their start and end apart: 2, of which 1 were waited for; matrix products, arithmetic and copies ran while one was open for 1% of the time, Pallas kernels for 58%

profile of v4, /device:TPU:1, one launch (start us, length us, event | category | flops | bytes accessed | tf_op | source)
XLA Modules:
  0.0 331.7 jit_solution(12031856105497693204)
XLA Ops:
  7.2 0.0 all-gather.2.cloned.1.call-start
  7.2 0.7 convert_bitcast_fusion.1
  7.9 0.7 convert_bitcast_fusion
  8.5 1.3 add_bitcast_fusion.small
  9.9 42.6 %front.1 = (f32[16,8,1,128]{3,2,1,0:T(1,128)}, f32[8,2048]{1,0:T(8,128)}, f32[1,768]{1,0:T(1,128)}, bf16[4,4,8,16,768]{4,3,2,1,0:T(8,128)(2,1)}, bf16[3,8,16,768...) custom-call(f32[1,128]{1,0:T(1,128)} %add_bitcast_fusion.small, ...), custom_call_target="tpu_custom_call" | custom-call | tf_op jit(solution)/shard_map/front/pallas_call | solution.py:1571
  52.5 0.0 all-gather.2.cloned.1.call-update
  52.5 0.6 reduce-scatter.2.cloned.1.call-start
  53.1 0.7 constant_dynamic-slice_fusion.4
  53.8 0.1 slice.35
  53.9 0.1 copy.37
  54.0 0.1 copy.38
  54.1 0.1 copy.39
  54.2 0.1 fusion
  54.3 0.1 compare_select_fusion
  54.4 0.6 pad_add_fusion.table
  55.0 84.7 %attend.1 = (bf16[2,512,256]{2,1,0:T(8,128)(2,1)}, bf16[2,2,1024,256]{3,2,1,0:T(8,128)(2,1)}, f32[2,8,512]{2,1,0:T(8,128)}, bf16[4,2,128,256]{3,2,1,0:T(8,128)(2...) custom-call(s32[2,3,8]{2,1,0:T(4,128)} %pad_add_fusion.table, ...), custom_call_target="tpu_custom_call" | custom-call | tf_op jit(solution)/shard_map/attend/pallas_call | solution.py:625
  139.7 6.3 %all-gather.2.cloned.1.call-done = bf16[16,3,128,768]{3,2,1,0:T(8,128)(2,1)} async-done(((bf16[1,3,128,768]{3,2,1,0:T(8,128)(2,1)}), bf16[16,3,128,768]{3,2,1,0:T(8,128)(2,1)}) %all-gather.2.cloned.1.call-update) | async-done | bytes 9437200 | tf_op jit(solution)/shard_map/all_gather | solution.py:1813
  146.0 49.2 %mlp.1 = (f32[128,2048]{1,0:T(8,128)}, f32[8,2048]{1,0:T(8,128)}, bf16[128,2048]{1,0:T(8,128)(2,1)}, bf16[2,512,256]{2,1,0:T(8,128)(2,1)}, f32[2,8,512]{2,1,0:T(...) custom-call(bf16[4,2,128,2048]{3,2,1,0:T(8,128)(2,1)} %get-tuple-element.62.two_hbm, ...), custom_call_target="tpu_custom_call" | custom-call | tf_op jit(solution)/shard_map/mlp/pallas_call | solution.py:1055
  195.2 0.0 reduce-scatter.2.cloned.1.call-update
  195.3 59.6 %attend_back.1 = (bf16[4,2,128,768]{3,2,1,0:T(8,128)(2,1)}, bf16[16,16,2048]{2,1,0:T(8,128)(2,1)}, bf16[128,2048]{1,0:T(8,128)(2,1)}) custom-call(s32[2,3,8]{2,1,0:T(4,128)} %pad_add_fusion.table, bf16[128,2048]{1,0:T(8,128)(2,1)} %get-tuple-element.69.branch_own, bf16[4,4,16,2048]{3,2,1,0:T(8,128)(2,1)} %get-tuple-element.70.gathered, ...), custom_call_target="tpu_custom_call" | custom-call | tf_op jit(solution)/shard_map/attend_back/pallas_call | solution.py:870
  254.9 47.5 %qkv_back.1 = (f32[128,2048]{1,0:T(8,128)}, f32[8,2048]{1,0:T(8,128)}, f32[8,768]{1,0:T(8,128)}, bf16[128,768]{1,0:T(8,128)(2,1)}, bf16[16,2048]{1,0:T(8,128)(2,1)}) custom-call(bf16[4,2,128,768]{3,2,1,0:T(8,128)(2,1)} %get-tuple-element.76.joined_grad, bf16[2048,768]{1,0:T(8,128)(2,1)} %bitcast.37, bf16[128,2048]{1,0:T(8,128)(2,1)} %get-tuple-element.60.hidden, ...), custom_call_target="tpu_custom_call" | custom-call | tf_op jit(solution)/shard_map/qkv_back/pallas_call | solution.py:1271
  302.4 0.0 reduce-scatter.2.cloned.1.call-done
  302.4 16.0 %collect.1 = (f32[8,16,128]{2,1,0:T(8,128)}, bf16[8,16,768]{2,1,0:T(8,128)(2,1)}, bf16[3,16,5632]{2,1,0:T(8,128)(2,1)}, bf16[16,2048]{1,0:T(8,128)(2,1)}) custom-call(f32[8,2048]{1,0:T(8,128)} %get-tuple-element.79.one_sums, f32[8,2048]{1,0:T(8,128)} %get-tuple-element.80.two_sums, f32[8,768]{1,0:T(8,128)} %get-tuple-element.81.shift, ...), custom_call_target="tpu_custom_call" | custom-call | tf_op jit(solution)/shard_map/collect/pallas_call | solution.py:1700
  318.5 0.8 slice_reduce_fusion
  319.2 0.8 slice.44
  320.0 0.1 constant_dynamic-slice_fusion.1
  320.1 0.5 slice_bitcast_fusion.1
  320.7 0.1 reshape.288
  320.8 0.5 fusion.1
  321.3 3.4 %finish.1 = (f32[16,6144]{1,0:T(8,128)}, f32[16,5632]{1,0:T(8,128)}, f32[16,5632]{1,0:T(8,128)}, f32[16,5632]{1,0:T(8,128)}, f32[16,2048]{1,0:T(8,128)}, /*index=5*/bf16[128,2048]{1,0:T(8,128)(2,1)}, f32[128,2048]{1,0:T(8,128)}) custom-call(bf16[8,16,768]{2,1,0:T(8,128)(2,1)} %get-tuple-element.85.qkv_hbm, bf16[3,16,5632]{2,1,0:T(8,128)(2,1)} %get-tuple-element.86.mlp_hbm, ...), custom_call_target="tpu_custom_call" | custom-call | tf_op jit(solution)/shard_map/finish/pallas_call | solution.py:1757
  (6 shorter events, 0.1 us)
Async XLA Ops:
  7.2 138.8 %all-gather.2.cloned.1.call-start = ((), (), s32[]{:S(2)}) async-start(), calls=%async_computation.1 | async-start | bytes 10027008 | tf_op jit(solution)/shard_map/all_gather | solution.py:1813
  52.5 249.9 %reduce-scatter.2.cloned.1.call-start = ((), (), s32[]{:S(2)}) async-start(), calls=%async_computation.2 | async-start | bytes 10027008 | tf_op jit(solution)/shard_map/reduce_scatter | solution.py:1831
Sparse Core Ops, SparseCore 0:
  52.7 93.3 all-gather.1
  195.4 100.2 reduce-scatter.1

commit v5 on v4

--- a/solution.py
+++ b/solution.py
@@ -293,7 +293,7 @@
             one.wait_send()
 
 
-def ring_scatter(partial, scratch, between=None):
+def ring_scatter(partial, scratch, between=None, before_late=None):
     part, sib_out = scratch[:2]
     c = lax.axis_index("core")
     scatter = RingScatter(
@@ -314,6 +314,8 @@
     scatter.send_early(0)
     produce(2)
     scatter.send_early(1)
+    if before_late is not None:
+        before_late()
     scatter.send_late()
     produce(3)
     if between is not None:
@@ -1244,7 +1246,7 @@
 
     weight_grads()
     out_scatter.relay()
-    scatter = ring_scatter(partial, scratch[24:], qkv_scatter.relay)
+    scatter = ring_scatter(partial, scratch[24:], out_scatter.middle, qkv_scatter.relay)
     sums[...] = jnp.zeros_like(sums)
 
     def back(r):
@@ -1257,7 +1259,6 @@
         sums[1:2, :] += jnp.sum(row, axis=0, keepdims=True)
 
     rows_loop(BLOCK, 16, back)
-    out_scatter.middle()
     qkv_scatter.middle()
     shift_sum[...] = jnp.broadcast_to(
         jnp.sum(flat.astype(F32), axis=0, keepdims=True), shift_sum.shape

time: 335 us -> 333 us (level)
  transfers between devices with their start and end apart: 2 -> 2, of which waited for: 1 -> 1; matrix products, arithmetic and copies ran while one was open for 1% -> 1% of each run, Pallas kernels for 58% -> 57%
where the time goes in v5:
time: 333 us; the launch traced here: 330 us
  Pallas kernels  301 us (90%)
  between operations  14.4 us (4%)
  waiting for transfers between devices  6.36 us (2%)
  other arithmetic  4.18 us (1%)
    pallas_call x1, Pallas kernels, attend(): pl.pallas_call(kernel_attend, out_shape=(jax.ShapeDtypeStruct((2, TOKENS,...  84.7 us
    pallas_call x1, Pallas kernels, attend_back(): pl.pallas_call(kernel_attend_back, out_shape=(jax.ShapeDtypeStruct((4, 2,...  59.6 us
    pallas_call x1, Pallas kernels, mlp(): pl.pallas_call(kernel_mlp, out_shape=(jax.ShapeDtypeStruct((BLOCK, D), F3...  49.2 us
    pallas_call x1, Pallas kernels, qkv_back(): pl.pallas_call(kernel_qkv_back, out_shape=(jax.ShapeDtypeStruct((BLOCK, D...  45.2 us
    pallas_call x1, Pallas kernels, front(): pl.pallas_call(kernel_front, out_shape=(jax.ShapeDtypeStruct((16, TP, 1,...  42.6 us
    pallas_call x1, Pallas kernels, collect(): pl.pallas_call(kernel_collect, out_shape=(jax.ShapeDtypeStruct((TP, 16, B...  16.6 us
  transfers between devices with their start and end apart: 2, of which 1 were waited for; matrix products, arithmetic and copies ran while one was open for 1% of the time, Pallas kernels for 57%

profile of v5, /device:TPU:1, one launch (start us, length us, event | category | flops | bytes accessed | tf_op | source)
XLA Modules:
  0.0 329.9 jit_solution(2657653535697155336)
XLA Ops:
  7.2 0.0 all-gather.2.cloned.1.call-start
  7.2 0.7 convert_bitcast_fusion.1
  7.9 0.7 convert_bitcast_fusion
  8.5 1.3 add_bitcast_fusion.small
  9.9 42.6 %front.1 = (f32[16,8,1,128]{3,2,1,0:T(1,128)}, f32[8,2048]{1,0:T(8,128)}, f32[1,768]{1,0:T(1,128)}, bf16[4,4,8,16,768]{4,3,2,1,0:T(8,128)(2,1)}, bf16[3,8,16,768...) custom-call(f32[1,128]{1,0:T(1,128)} %add_bitcast_fusion.small, ...), custom_call_target="tpu_custom_call" | custom-call | tf_op jit(solution)/shard_map/front/pallas_call | solution.py:1572
  52.5 0.0 all-gather.2.cloned.1.call-update
  52.5 0.6 reduce-scatter.2.cloned.1.call-start
  53.1 0.7 constant_dynamic-slice_fusion.4
  53.8 0.1 slice.35
  53.9 0.1 copy.37
  54.0 0.1 copy.38
  54.1 0.1 copy.39
  54.2 0.1 fusion
  54.3 0.1 compare_select_fusion
  54.4 0.6 pad_add_fusion.table
  55.0 84.7 %attend.1 = (bf16[2,512,256]{2,1,0:T(8,128)(2,1)}, bf16[2,2,1024,256]{3,2,1,0:T(8,128)(2,1)}, f32[2,8,512]{2,1,0:T(8,128)}, bf16[4,2,128,256]{3,2,1,0:T(8,128)(2...) custom-call(s32[2,3,8]{2,1,0:T(4,128)} %pad_add_fusion.table, ...), custom_call_target="tpu_custom_call" | custom-call | tf_op jit(solution)/shard_map/attend/pallas_call | solution.py:627
  139.7 6.3 %all-gather.2.cloned.1.call-done = bf16[16,3,128,768]{3,2,1,0:T(8,128)(2,1)} async-done(((bf16[1,3,128,768]{3,2,1,0:T(8,128)(2,1)}), bf16[16,3,128,768]{3,2,1,0:T(8,128)(2,1)}) %all-gather.2.cloned.1.call-update) | async-done | bytes 9437200 | tf_op jit(solution)/shard_map/all_gather | solution.py:1814
  146.0 49.2 %mlp.1 = (f32[128,2048]{1,0:T(8,128)}, f32[8,2048]{1,0:T(8,128)}, bf16[128,2048]{1,0:T(8,128)(2,1)}, bf16[2,512,256]{2,1,0:T(8,128)(2,1)}, f32[2,8,512]{2,1,0:T(...) custom-call(bf16[4,2,128,2048]{3,2,1,0:T(8,128)(2,1)} %get-tuple-element.62.two_hbm, ...), custom_call_target="tpu_custom_call" | custom-call | tf_op jit(solution)/shard_map/mlp/pallas_call | solution.py:1057
  195.2 0.0 reduce-scatter.2.cloned.1.call-update
  195.3 59.6 %attend_back.1 = (bf16[4,2,128,768]{3,2,1,0:T(8,128)(2,1)}, bf16[16,16,2048]{2,1,0:T(8,128)(2,1)}, bf16[128,2048]{1,0:T(8,128)(2,1)}) custom-call(s32[2,3,8]{2,1,0:T(4,128)} %pad_add_fusion.table, bf16[128,2048]{1,0:T(8,128)(2,1)} %get-tuple-element.69.branch_own, bf16[4,4,16,2048]{3,2,1,0:T(8,128)(2,1)} %get-tuple-element.70.gathered, ...), custom_call_target="tpu_custom_call" | custom-call | tf_op jit(solution)/shard_map/attend_back/pallas_call | solution.py:872
  254.9 45.2 %qkv_back.1 = (f32[128,2048]{1,0:T(8,128)}, f32[8,2048]{1,0:T(8,128)}, f32[8,768]{1,0:T(8,128)}, bf16[128,768]{1,0:T(8,128)(2,1)}, bf16[16,2048]{1,0:T(8,128)(2,1)}) custom-call(bf16[4,2,128,768]{3,2,1,0:T(8,128)(2,1)} %get-tuple-element.76.joined_grad, bf16[2048,768]{1,0:T(8,128)(2,1)} %bitcast.37, bf16[128,2048]{1,0:T(8,128)(2,1)} %get-tuple-element.60.hidden, ...), custom_call_target="tpu_custom_call" | custom-call | tf_op jit(solution)/shard_map/qkv_back/pallas_call | solution.py:1272
  300.1 0.0 reduce-scatter.2.cloned.1.call-done
  300.1 16.6 %collect.1 = (f32[8,16,128]{2,1,0:T(8,128)}, bf16[8,16,768]{2,1,0:T(8,128)(2,1)}, bf16[3,16,5632]{2,1,0:T(8,128)(2,1)}, bf16[16,2048]{1,0:T(8,128)(2,1)}) custom-call(f32[8,2048]{1,0:T(8,128)} %get-tuple-element.79.one_sums, f32[8,2048]{1,0:T(8,128)} %get-tuple-element.80.two_sums, f32[8,768]{1,0:T(8,128)} %get-tuple-element.81.shift, ...), custom_call_target="tpu_custom_call" | custom-call | tf_op jit(solution)/shard_map/collect/pallas_call | solution.py:1701
  316.7 0.8 slice_reduce_fusion
  317.4 0.8 slice.44
  318.2 0.1 constant_dynamic-slice_fusion.1
  318.3 0.5 slice_bitcast_fusion.1
  318.9 0.1 reshape.288
  319.0 0.5 fusion.1
  319.5 3.4 %finish.1 = (f32[16,6144]{1,0:T(8,128)}, f32[16,5632]{1,0:T(8,128)}, f32[16,5632]{1,0:T(8,128)}, f32[16,5632]{1,0:T(8,128)}, f32[16,2048]{1,0:T(8,128)}, /*index=5*/bf16[128,2048]{1,0:T(8,128)(2,1)}, f32[128,2048]{1,0:T(8,128)}) custom-call(bf16[8,16,768]{2,1,0:T(8,128)(2,1)} %get-tuple-element.85.qkv_hbm, bf16[3,16,5632]{2,1,0:T(8,128)(2,1)} %get-tuple-element.86.mlp_hbm, ...), custom_call_target="tpu_custom_call" | custom-call | tf_op jit(solution)/shard_map/finish/pallas_call | solution.py:1758
  (6 shorter events, 0.1 us)
Async XLA Ops:
  7.2 138.8 %all-gather.2.cloned.1.call-start = ((), (), s32[]{:S(2)}) async-start(), calls=%async_computation.1 | async-start | bytes 10027008 | tf_op jit(solution)/shard_map/all_gather | solution.py:1814
  52.5 247.6 %reduce-scatter.2.cloned.1.call-start = ((), (), s32[]{:S(2)}) async-start(), calls=%async_computation.2 | async-start | bytes 10027008 | tf_op jit(solution)/shard_map/reduce_scatter | solution.py:1832
Sparse Core Ops, SparseCore 0:
  52.7 93.3 all-gather.1
  195.4 97.6 reduce-scatter.1
